TPU v7x, 32 devices: a whole 2x2x4 slice. The times are simulated.
32 devices in a mesh: ctx: 8 (over z, x), tp: 4 (over y, core).
Axes of the slice: x: 2, y: 2, z: 4, core: 2. Of those that a mesh axis runs over, the one named last changes fastest.
Arguments:
- tokens: bfloat16 [2048, 8192], P('ctx', 'tp'), may hold values from -6 to 6
- in_weight: bfloat16 [8192, 8192], P('ctx', 'tp'), may hold values from -0.09375 to 0.09375
- filters: float32 [2048, 8192], P('ctx', 'tp'), may hold values from -1 to 1
- gate: bfloat16 [2048, 8192], P('ctx', 'tp'), may hold values from -6 to 6
- cotangent: bfloat16 [2048, 8192], P('ctx', 'tp'), may hold values from -6 to 6
Outputs:
- gated_output: bfloat16 [2048, 8192], P('ctx', 'tp')
- grad_gate: bfloat16 [2048, 8192], P('ctx', 'tp')
- grad_tokens: bfloat16 [2048, 8192], P('ctx', 'tp')
All inputs are finite; a program needn't handle non-finite values.
Results may differ from a plain program's by a relative error of at most 0.028.
Values may be sent and summed in bfloat16 or wider, within the bound.
No kernel may reach another device: no remote copies, remote signals or barrier semaphores. Data moves between devices by JAX's collectives and lax.ppermute only.
A program may use at most 192 MiB of HBM per device.

v0:
```python
import math

import jax
import jax.numpy as jnp
from jax import lax
from jax.sharding import PartitionSpec as P

PRECISE = lax.Precision.HIGHEST
TWO_PI = 2.0 * math.pi


def shortened(shard):
    return jax.tree.map(lambda a: a.astype(jnp.bfloat16) if a.dtype == jnp.float32 else a, shard)


def counting(length):
    return jnp.arange(length, dtype=jnp.int32)


def phase_table(left_index, right_index, modulus):
    product = left_index * right_index % modulus
    return product.astype(jnp.float32) * (TWO_PI / modulus)


def first_forward(pieces, offsets, blocks, total_length):
    freq_count = 2 * blocks
    angles = phase_table(counting(freq_count)[:, None], counting(blocks)[None, :], freq_count)
    real_part = jnp.einsum("kp,bpsc->bksc", jnp.cos(angles), pieces, precision=PRECISE)
    imag_part = -jnp.einsum("kp,bpsc->bksc", jnp.sin(angles), pieces, precision=PRECISE)
    twiddle = phase_table(counting(freq_count)[:, None], offsets[None, :], total_length)
    cos_twiddle = jnp.cos(twiddle)[None, :, :, None]
    sin_twiddle = jnp.sin(twiddle)[None, :, :, None]
    return jnp.stack(
        [
            real_part * cos_twiddle + imag_part * sin_twiddle,
            imag_part * cos_twiddle - real_part * sin_twiddle,
        ]
    )


def second_forward(mixture):
    length = mixture.shape[3]
    angles = phase_table(counting(length)[:, None], counting(length)[None, :], length)
    cos_table = jnp.cos(angles)
    sin_table = jnp.sin(angles)
    real_part = jnp.einsum("qr,bjrc->bjqc", cos_table, mixture[0], precision=PRECISE) + jnp.einsum(
        "qr,bjrc->bjqc", sin_table, mixture[1], precision=PRECISE
    )
    imag_part = jnp.einsum("qr,bjrc->bjqc", cos_table, mixture[1], precision=PRECISE) - jnp.einsum(
        "qr,bjrc->bjqc", sin_table, mixture[0], precision=PRECISE
    )
    return jnp.stack([real_part, imag_part])


def first_inverse(spectrum):
    length = spectrum.shape[3]
    angles = phase_table(counting(length)[:, None], counting(length)[None, :], length)
    cos_table = jnp.cos(angles)
    sin_table = jnp.sin(angles)
    real_part = jnp.einsum("rq,bjqc->bjrc", cos_table, spectrum[0], precision=PRECISE) - jnp.einsum(
        "rq,bjqc->bjrc", sin_table, spectrum[1], precision=PRECISE
    )
    imag_part = jnp.einsum("rq,bjqc->bjrc", cos_table, spectrum[1], precision=PRECISE) + jnp.einsum(
        "rq,bjqc->bjrc", sin_table, spectrum[0], precision=PRECISE
    )
    return jnp.stack([real_part, imag_part])


def turn_inverse(signal, freq_index, total_length):
    length = signal.shape[3]
    twiddle = phase_table(freq_index[:, None], counting(length)[None, :], total_length)
    cos_twiddle = jnp.cos(twiddle)[None, :, :, None]
    sin_twiddle = jnp.sin(twiddle)[None, :, :, None]
    return jnp.stack(
        [
            signal[0] * cos_twiddle - signal[1] * sin_twiddle,
            signal[1] * cos_twiddle + signal[0] * sin_twiddle,
        ]
    )


def second_inverse(mixture, blocks, total_length):
    freq_count = 2 * blocks
    angles = phase_table(counting(blocks)[:, None], counting(freq_count)[None, :], freq_count)
    real_sum = jnp.einsum(
        "pk,bksc->bpsc", jnp.cos(angles), mixture[0], precision=PRECISE
    ) - jnp.einsum("pk,bksc->bpsc", jnp.sin(angles), mixture[1], precision=PRECISE)
    return real_sum / total_length


def local_forward(signal, blocks):
    batch_count, length, channel_count = signal.shape
    share_rows = length // blocks
    pieces = signal.reshape(batch_count, blocks, share_rows, channel_count)
    mixture = first_forward(pieces, counting(share_rows), blocks, 2 * length)
    return second_forward(mixture)


def local_inverse(spectrum, blocks):
    share_rows = spectrum.shape[3]
    total_length = 2 * blocks * share_rows
    turned = turn_inverse(first_inverse(spectrum), counting(2 * blocks), total_length)
    signal = second_inverse(turned, blocks, total_length)
    return signal.reshape(signal.shape[0], blocks * share_rows, signal.shape[3])


def complex_product(spectrum, filter_real, filter_imag):
    return jnp.stack(
        [
            spectrum[0] * filter_real - spectrum[1] * filter_imag,
            spectrum[0] * filter_imag + spectrum[1] * filter_real,
        ]
    )


def per_device(tokens, in_weight, filters, gate, cotangent):
    full_rows = lax.all_gather(tokens, "tp", axis=1, tiled=True)
    weight_all = lax.all_gather(in_weight, "ctx", axis=0, tiled=True)
    values = jnp.dot(full_rows, weight_all, preferred_element_type=jnp.float32).astype(jnp.bfloat16)
    gate_wide = gate.astype(jnp.float32)
    cotangent_wide = cotangent.astype(jnp.float32)
    grad_conv = cotangent_wide * gate_wide
    signals = values.astype(jnp.float32)
    blocks = lax.axis_size("ctx")
    channel_rows = lax.all_to_all(
        jnp.stack([filters, signals, grad_conv]).astype(jnp.bfloat16),
        "ctx",
        split_axis=2,
        concat_axis=1,
        tiled=True,
    ).astype(jnp.float32)
    spectrum = local_forward(channel_rows, blocks)
    filter_real = spectrum[0, 0:1]
    filter_imag = spectrum[1, 0:1]
    pair_real = jnp.concatenate([filter_real, filter_real], axis=0)
    pair_imag = jnp.concatenate([filter_imag, -filter_imag], axis=0)
    result = local_inverse(complex_product(spectrum[:, 1:], pair_real, pair_imag), blocks)
    result = lax.all_to_all(
        shortened(result), "ctx", split_axis=1, concat_axis=2, tiled=True
    ).astype(result.dtype)
    convolved = result[0]
    grad_signal = result[1]
    gated_output = (gate_wide * convolved).astype(jnp.bfloat16)
    grad_gate = (cotangent_wide * convolved).astype(jnp.bfloat16)
    grad_values = grad_signal.astype(jnp.bfloat16)
    partial_value = lax.dot_general(
        grad_values, weight_all, (((1,), (1,)), ((), ())), preferred_element_type=jnp.float32
    )
    grad_tokens = lax.psum_scatter(
        partial_value.astype(jnp.bfloat16), "tp", scatter_dimension=1, tiled=True
    )
    return (gated_output, grad_gate, grad_tokens)


def solution(mesh):
    placed = (P("ctx", "tp"), P("ctx", "tp"), P("ctx", "tp"), P("ctx", "tp"), P("ctx", "tp"))
    return jax.shard_map(
        per_device,
        mesh=mesh,
        in_specs=placed,
        out_specs=(P("ctx", "tp"), P("ctx", "tp"), P("ctx", "tp")),
        check_vma=False,
    )
```

profile of v0, /device:TPU:4, one launch (start us, length us, event | category | flops | bytes accessed | tf_op | source)
XLA Modules:
  0.0 1181.6 jit_solution(10986527905346825172)
XLA Ops:
  12.8 31.3 %all-gather.3.cloned.1.call-done = bf16[256,8192]{1,0:T(8,128)(2,1)} async-done(((bf16[256,2048]{1,0:T(8,128)(2,1)}), bf16[256,8192]{1,0:T(8,128)(2,1)}) %all-gather.3.cloned.1.call-update) | async-done | bytes 4194320 | tf_op jit(solution)/shard_map/all_gather | solution.py:117
  44.1 640.5 %all-gather.5.cloned.1.call-done = bf16[8192,2048]{1,0:T(8,128)(2,1)} async-done(((bf16[1024,2048]{1,0:T(8,128)(2,1)}), bf16[8192,2048]{1,0:T(8,128)(2,1)}) %all-gather.5.cloned.1.call-update) | async-done | bytes 33554448 | tf_op jit(solution)/shard_map/all_gather | solution.py:118
  684.6 16.4 %fusion.10 = bf16[1,256,2048]{2,1,0:T(8,128)(2,1)S(1)} fusion(bf16[256,8192]{1,0:T(8,128)(2,1)} %all-gather.3.cloned.1.call-done, bf16[8192,2048]{1,0:T(8,128)(2,1)} %all-gather.5.cloned.1.call-done), kind=kOutput, calls=%fused_computation.31 | convolution fusion | flops 8590458880 | bytes 38797312 | tf_op jit(solution)/shard_map/dot_general | solution.py:119
  711.4 92.9 %all-to-all-done = bf16[3,256,2048]{1,0,2:T(4,128)(2,1)} async-done(((bf16[3,256,2048]{1,0,2:T(4,128)(2,1)}), bf16[3,256,2048]{1,0,2:T(4,128)(2,1)}, u32[]{:S(2)}, u32[]{:S(2)}) %all-to-all-start) | async-done | bytes 3145760 | tf_op jit(solution)/shard_map/all_to_all | solution.py:125
  808.9 8.1 fusion.6
  817.0 16.4 %fusion.1 = (f32[3,16,256,256]{3,1,2,0:T(8,128)}, f32[3,16,256,256]{3,1,2,0:T(8,128)}) fusion(f32[3,256,256,16]{2,3,1,0:T(8,128)} %fusion.6, f32[16,256]{0,1:T(8,128)S(1)} %copy.55, f32[16,256]{0,1:T(8,128)S(1)} %copy.54, bf16[3,256,8,256]{3,2,1,0:T(8,128)(2,1)S(1)} %copy.73), kind=kOutput, calls=%fused_computation.3 | convolution fusion | flops 324011776 | bytes 40927232 | tf_op jit(solution)/shard_map/kp,bpsc->bksc/dot_general | solution.py:28
  833.4 12.8 %copy.57 = f32[3,16,256,256]{2,3,1,0:T(8,128)} copy(f32[3,16,256,256]{3,1,2,0:T(8,128)} %get-tuple-element.7) | data formatting | bytes 25165824 | tf_op jit(solution)/shard_map/sub | solution.py:36
  846.2 12.8 %copy.56 = f32[3,16,256,256]{2,3,1,0:T(8,128)} copy(f32[3,16,256,256]{3,1,2,0:T(8,128)} %get-tuple-element.8) | data formatting | bytes 25165824 | tf_op jit(solution)/shard_map/add | solution.py:35
  859.0 17.5 %fusion.31 = f32[3,16,256,256]{3,2,1,0:T(8,128)} fusion(f32[3,16,256,256]{2,3,1,0:T(8,128)} %copy.56), kind=kOutput, calls=%fused_computation.57 | convolution fusion | flops 9664593920 | bytes 25165824 | tf_op jit(solution)/shard_map/qr,bjrc->bjqc/dot_general | solution.py:46
  876.6 15.7 %fusion.29 = f32[3,16,256,256]{3,2,1,0:T(8,128)} fusion(f32[3,16,256,256]{2,3,1,0:T(8,128)S(1)} %copy-done), kind=kOutput, calls=%fused_computation.55 | convolution fusion | flops 9664593920 | bytes 25165824 | tf_op jit(solution)/shard_map/qr,bjrc->bjqc/dot_general | solution.py:49
  892.3 19.2 %subtract_bitcast_fusion = f32[1,3,16,256,256]{3,4,2,1,0:T(8,128)} fusion(f32[3,16,256,256]{3,2,1,0:T(8,128)} %fusion.29, f32[3,16,256,256]{2,3,1,0:T(8,128)} %copy.56), kind=kOutput, calls=%fused_computation.6 | convolution fusion | flops 9667739648 | bytes 37748736 | tf_op jit(solution)/shard_map/qr,bjrc->bjqc/dot_general | solution.py:49
  920.6 18.1 %add_bitcast_fusion = f32[1,3,16,256,256]{3,4,2,1,0:T(8,128)} fusion(f32[3,16,256,256]{3,2,1,0:T(8,128)} %fusion.31, f32[3,16,256,256]{2,3,1,0:T(8,128)S(1)} %copy-done), kind=kOutput, calls=%fused_computation.7 | convolution fusion | flops 9667739648 | bytes 37748736 | tf_op jit(solution)/shard_map/qr,bjrc->bjqc/dot_general | solution.py:46
  943.4 17.3 %fusion.4 = (f32[2,16,256,256]{2,3,1,0:T(8,128)}, f32[2,16,256,256]{2,3,1,0:T(8,128)}) fusion(f32[1,16,256,256]{2,3,1,0:T(8,128)} %slice_bitcast_fusion.3, f32[1,3,16,256,256]{3,4,2,1,0:T(8,128)} %add_bitcast_fusion, f32[1,3,16,256,256]{3,4,2,1,0:T(8,128)} %subtract_bitcast_fusion, f32[1,16,256,256]{2,3,1,0:T(8,128)S(1)} %copy-done.3, ...), kind=kLoop, calls=%fused_computation.14 | loop fusion | flops 16777216 | bytes 46137344 | tf_op jit(solution)/shard_map/sub | solution.py:110
  960.7 13.1 %fusion.25 = f32[2,16,256,256]{3,2,1,0:T(8,128)} fusion(f32[2,16,256,256]{2,3,1,0:T(8,128)} %get-tuple-element.4), kind=kOutput, calls=%fused_computation.51 | convolution fusion | flops 6443368448 | bytes 16777216 | tf_op jit(solution)/shard_map/rq,bjqc->bjrc/dot_general | solution.py:63
  973.9 11.1 fusion.21
  985.0 11.0 fusion.19
  995.9 19.7 %add_bitcast_fusion.1 = (f32[2,16,256,256]{2,3,1,0:T(8,128)}, f32[2,16,256,256]{2,3,1,0:T(8,128)}) fusion(f32[16,256]{1,0:T(8,128)S(1)} %get-tuple-element.15, f32[16,256]{1,0:T(8,128)S(1)} %get-tuple-element.16, f32[2,16,256,256]{3,2,1,0:T(8,128)} %fusion.25, f32[2,16,256,256]{3,2,1,0:T(8,128)} %fusion.19, f32[2,16,256,256]{3,2,1,0:T(8,128)} %fusion.21, ...), kind=kOutput, calls=%fused_computation.17 | convolution fusion | flops 6460145664 | bytes 50364416 | tf_op jit(solution)/shard_map/rq,bjqc->bjrc/dot_general | solution.py:60
  1015.6 10.3 copy.61
  1025.9 10.3 copy.60
  1036.2 7.2 fusion.61
  1048.8 12.8 %copy.63 = bf16[2,2048,256]{2,0,1:T(2,128)(2,1)S(1)} copy(bf16[2,2048,256]{2,1,0:T(8,128)(2,1)S(1)} %bitcast.134) | data formatting | bytes 4194304 | tf_op jit(solution)/shard_map/convert_element_type | solution.py:13
  1061.6 51.8 %all_to_all.24 = bf16[2,2048,256]{2,0,1:T(2,128)(2,1)S(1)} all-to-all(bf16[2,2048,256]{2,0,1:T(2,128)(2,1)S(1)} %copy.63), channel_id=1, replica_groups=mesh['ctx'=8,'tp'=4] {'ctx'}, dimensions={1} | all-to-all | bytes 4194304 | tf_op jit(solution)/shard_map/all_to_all | solution.py:138
  1115.3 17.0 %convolution_convert_fusion = bf16[256,8192]{1,0:T(8,128)(2,1)} fusion(bf16[256,2048]{0,1:T(8,128)(2,1)} %bitcast.135, bf16[8192,2048]{1,0:T(8,128)(2,1)} %all-gather.5.cloned.1.call-done), kind=kOutput, calls=%fused_computation.8 | convolution fusion | flops 8592031744 | bytes 38797312 | tf_op jit(solution)/shard_map/dot_general | solution.py:146
  1136.7 38.1 %reduce-scatter.2.cloned.1.call-done = bf16[256,2048]{1,0:T(8,128)(2,1)} async-done(((bf16[256,8192]{1,0:T(8,128)(2,1)}), bf16[256,2048]{1,0:T(8,128)(2,1)}) %reduce-scatter.2.cloned.1.call-update) | async-done | bytes 1048592 | tf_op jit(solution)/shard_map/reduce_scatter | solution.py:149
  (43 shorter events, 46.0 us)
Async XLA Ops:
  7.2 37.0 %all-gather.3.cloned.1.call-start = ((), (), s32[]{:S(2)}) async-start(), calls=%async_computation.3 | async-start | bytes 5242880 | tf_op jit(solution)/shard_map/all_gather | solution.py:117
  7.9 676.7 %all-gather.5.cloned.1.call-start = ((), (), s32[]{:S(2)}) async-start(), calls=%async_computation.4 | async-start | bytes 37748736 | tf_op jit(solution)/shard_map/all_gather | solution.py:118
  684.6 16.4 %copy-start.5 = (bf16[1,256,2048]{2,1,0:T(8,128)(2,1)S(1)}, bf16[1,256,2048]{2,1,0:T(8,128)(2,1)}, u32[]{:S(2)}) copy-start(bf16[1,256,2048]{2,1,0:T(8,128)(2,1)} %get-tuple-element.13) | copy-start | bytes 3145732
  684.6 16.4 %copy-start.6 = (bf16[1,256,2048]{2,1,0:T(8,128)(2,1)S(1)}, bf16[1,256,2048]{2,1,0:T(8,128)(2,1)}, u32[]{:S(2)}) copy-start(bf16[1,256,2048]{2,1,0:T(8,128)(2,1)} %get-tuple-element.14) | copy-start | bytes 3145732
  706.2 98.1 %all-to-all-start = ((bf16[3,256,2048]{1,0,2:T(4,128)(2,1)}), bf16[3,256,2048]{1,0,2:T(4,128)(2,1)}, u32[]{:S(2)}, u32[]{:S(2)}) async-start(bf16[3,256,2048]{1,0,2:T(4,128)(2,1)} %copy.52), calls=%async_computation | async-start | bytes 8388608 | tf_op jit(solution)/shard_map/all_to_all | solution.py:125
  710.7 464.1 %reduce-scatter.2.cloned.1.call-start = ((), (), s32[]{:S(2)}) async-start(), calls=%async_computation.5 | async-start | bytes 5242880 | tf_op jit(solution)/shard_map/reduce_scatter | solution.py:149
  859.0 17.5 %copy-start = (f32[3,16,256,256]{2,3,1,0:T(8,128)S(1)}, f32[3,16,256,256]{2,3,1,0:T(8,128)}, u32[]{:S(2)}) copy-start(f32[3,16,256,256]{2,3,1,0:T(8,128)} %copy.57) | copy-start | bytes 37748740
  938.7 4.7 copy-start.3
  960.7 13.2 %copy-start.1 = (f32[2,16,256,256]{2,3,1,0:T(8,128)S(1)}, f32[2,16,256,256]{2,3,1,0:T(8,128)}, u32[]{:S(2)}) copy-start(f32[2,16,256,256]{2,3,1,0:T(8,128)} %get-tuple-element.4) | copy-start | bytes 25165828
  960.7 24.2 %slice-start = ((s8[8388608]{0:T(1024)(128)(4,1)}), s8[4194304]{0:T(1024)(128)(4,1)S(1)}, s32[]{:S(2)}) async-start(s8[8388608]{0:T(1024)(128)(4,1)} %bitcast.129), calls=%async_computation.6 | async-start | bytes 8388608
  973.9 11.1 slice-start.1
  1036.2 7.2 copy-start.2
  1132.3 1.2 copy-start.4
Sparse Core Ops, SparseCore 0:
  9.6 34.5 all-gather.2
  45.7 638.8 all-gather.4
  1132.5 42.3 reduce-scatter.1
where the time goes:
time: 1190 us; the launch traced here: 1180 us
  waiting for transfers between devices  804 us (68%)
  matrix products  196 us (16%)
  local copies, waits for them, and re-layouts  81.3 us (7%)
  blocking collectives  51.8 us (4%)
  other arithmetic  29.7 us (2%)
  between operations  14.1 us (1%)
    all_gather x1, waiting for transfers between devices, per_device(): weight_all = lax.all_gather(in_weight, 'ctx', axis=0, tiled=True)  640 us
    all_to_all x1, waiting for transfers between devices, per_device(): lax.all_to_all(jnp.stack([filters, signals, grad_conv]).astype(jnp.bfloat...  92.9 us
    all_to_all x1, blocking collectives, per_device(): lax.all_to_all(shortened(result), 'ctx', split_axis=1, concat_axis=2, til...  51.8 us
    reduce_scatter x1, waiting for transfers between devices, per_device(): lax.psum_scatter(partial_value.astype(jnp.bfloat16), 'tp', scatter_dimens...  38.1 us
    all_gather x1, waiting for transfers between devices, per_device(): full_rows = lax.all_gather(tokens, 'tp', axis=1, tiled=True)  31.3 us
  transfers between devices with their start and end apart: 4, of which 4 were waited for; matrix products, arithmetic and copies ran while one was open for 1% of the time, Pallas kernels for 0%

commit v1 on v0

v1 whole, which is shorter than its diff:
```python
import functools
import math

import jax
import jax.numpy as jnp
import numpy as np
from jax import lax
from jax.experimental import pallas as pl
from jax.experimental.pallas import tpu as pltpu
from jax.sharding import Mesh, PartitionSpec as P

TWO_PI = 2.0 * math.pi
WIDE = jnp.float32
SHORT = jnp.bfloat16
LAST_TWO = (((1,), (1,)), ((), ()))


def transform_table(length):
    period = 16 * length
    fine_count = 32
    fine = jnp.arange(fine_count, dtype=jnp.int32)[:, None]
    coarse = jnp.arange(length // fine_count, dtype=jnp.int32)[:, None]
    time = 4 * jnp.arange(length, dtype=jnp.int32)[None, :] + 1
    scale = TWO_PI / period
    fine_angle = ((4 * fine + 1) * time % period).astype(WIDE) * scale
    coarse_angle = (4 * fine_count * coarse * time % period).astype(WIDE) * scale
    fine_cos, fine_sin, coarse_cos, coarse_sin = lax.optimization_barrier(
        (jnp.cos(fine_angle), jnp.sin(fine_angle), jnp.cos(coarse_angle), jnp.sin(coarse_angle))
    )
    fine_cos, fine_sin = fine_cos[None], fine_sin[None]
    coarse_cos, coarse_sin = coarse_cos[:, None], coarse_sin[:, None]
    cos_part = (coarse_cos * fine_cos - coarse_sin * fine_sin).astype(SHORT)
    sin_part = (coarse_sin * fine_cos + coarse_cos * fine_sin).astype(SHORT)
    return cos_part.reshape(length, length), sin_part.reshape(length, length)


def table_block(length):
    return min(512, length // 2)


def rotation(length):
    angle = (4 * jnp.arange(length, dtype=jnp.int32) + 1).astype(WIDE) * (TWO_PI / (16 * length))
    return jnp.stack([jnp.cos(angle), jnp.sin(angle)], axis=1)


def wide_dot(left, right):
    return jnp.dot(left, right, preferred_element_type=WIDE)


def wide_dot_turned(left, right):
    return lax.dot_general(left, right, LAST_TWO, preferred_element_type=WIDE)


def kernel_params(axes):
    return pltpu.CompilerParams(
        dimension_semantics=("arbitrary",) * axes, vmem_limit_bytes=48 * 1024 * 1024
    )


def cost(flops, bytes_accessed):
    return pl.CostEstimate(flops=flops, bytes_accessed=bytes_accessed, transcendentals=0)


ANYWHERE = pl.BlockSpec(memory_space=pl.ANY)


def waiting(kernel, count):
    return lambda index_ref, *refs: kernel(index_ref, *refs[count:])


def aligned(index, size):
    return pl.ds(pl.multiple_of(index * size, size), size)


def correlate_kernel(cos_ref, sin_ref, turn_ref, both_ref, out_ref, spectrum_ref, signal_ref, mix_ref):
    phase, step = pl.program_id(0), pl.program_id(1)
    block = cos_ref.shape[0]
    length, channels = mix_ref.shape[1:]
    rows = aligned(step, block)

    @pl.when((phase == 0) & (step == 0))
    def _():
        for which in range(2):
            signal_ref[:, which * channels : (which + 1) * channels] = both_ref[:, which].reshape(length, channels)

    @pl.when(phase == 0)
    def _():
        turn_cos, turn_sin = turn_ref[:, 0:1], turn_ref[:, 1:2]
        cos_sums = wide_dot(cos_ref[...], signal_ref[...])
        sin_sums = wide_dot(sin_ref[...], signal_ref[...])
        raw_cos, signal_cos = cos_sums[:, :channels], cos_sums[:, channels:]
        raw_sin, signal_sin = sin_sums[:, :channels], sin_sums[:, channels:]
        filter_cos = raw_cos * turn_cos + raw_sin * turn_sin
        filter_sin = raw_sin * turn_cos - raw_cos * turn_sin
        spectrum_ref[0] = filter_cos.astype(SHORT)
        spectrum_ref[1] = filter_sin.astype(SHORT)
        mix_ref[0, rows] = (signal_cos * filter_cos + signal_sin * filter_sin).astype(SHORT)
        mix_ref[1, rows] = (signal_sin * filter_cos - signal_cos * filter_sin).astype(SHORT)

    @pl.when(phase == 1)
    def _():
        total = wide_dot(cos_ref[...], mix_ref[0]) + wide_dot(sin_ref[...], mix_ref[1])
        out_ref[...] = (total * (1.0 / length)).astype(out_ref.dtype)


def correlate(table, turn, both):
    parts, _, rows, channels = both.shape
    length = parts * rows
    block = table_block(length)
    steps = length // block
    table_spec = pl.BlockSpec((block, length), lambda p, s: (s, 0))
    return pl.pallas_call(
        correlate_kernel,
        grid=(2, steps),
        in_specs=[
            table_spec,
            table_spec,
            pl.BlockSpec((block, 2), lambda p, s: (s, 0)),
            pl.BlockSpec((parts, 2, rows, channels), lambda p, s: (0, 0, 0, 0)),
        ],
        out_specs=[
            pl.BlockSpec((block, channels), lambda p, s: (p * s, 0)),
            pl.BlockSpec((2, block, channels), lambda p, s: (0, s + p * (steps - 1 - s), 0)),
        ],
        out_shape=[
            jax.ShapeDtypeStruct((length, channels), SHORT),
            jax.ShapeDtypeStruct((2, length, channels), SHORT),
        ],
        scratch_shapes=[pltpu.VMEM((length, 2 * channels), SHORT), pltpu.VMEM((2, length, channels), SHORT)],
        compiler_params=kernel_params(2),
        cost_estimate=cost(12 * length * length * channels, 8 * length * length),
    )(table[0], table[1], turn, both)


def convolve_kernel(inner, places_ref, cos_ref, sin_ref, spectrum_ref, *refs):
    part_refs, (out_ref, signal_ref, mix_ref) = refs[:inner], refs[inner:]
    phase, step = pl.program_id(0), pl.program_id(1)
    block = cos_ref.shape[0]
    length = signal_ref.shape[0]
    rows = aligned(step, block)
    pieces = places_ref.shape[1]
    size = part_refs[0].shape[0] // pieces

    @pl.when((phase == 0) & (step == 0))
    def _():
        for s in range(inner):
            for p in range(pieces):
                signal_ref[aligned(places_ref[s, p], size)] = part_refs[s][p * size : (p + 1) * size]

    @pl.when(phase == 0)
    def _():
        filter_cos, filter_sin = spectrum_ref[0].astype(WIDE), spectrum_ref[1].astype(WIDE)
        signal_cos = wide_dot(cos_ref[...], signal_ref[...])
        signal_sin = wide_dot(sin_ref[...], signal_ref[...])
        mix_ref[0, rows] = (signal_cos * filter_cos - signal_sin * filter_sin).astype(SHORT)
        mix_ref[1, rows] = (signal_cos * filter_sin + signal_sin * filter_cos).astype(SHORT)

    @pl.when(phase == 1)
    def _():
        total = wide_dot(cos_ref[...], mix_ref[0]) + wide_dot(sin_ref[...], mix_ref[1])
        out_ref[...] = (total * (1.0 / length)).astype(out_ref.dtype)


def convolve(table, spectrum, parts, places):
    length, channels = spectrum.shape[1:]
    block = table_block(length)
    steps = length // block
    table_spec = pl.BlockSpec((block, length), lambda p, s, _: (s, 0))
    return pl.pallas_call(
        functools.partial(convolve_kernel, len(parts)),
        grid_spec=pltpu.PrefetchScalarGridSpec(
            num_scalar_prefetch=1,
            grid=(2, steps),
            in_specs=[
                table_spec,
                table_spec,
                pl.BlockSpec((2, block, channels), lambda p, s, _: (0, s + p * (steps - 1 - s), 0)),
            ]
            + [pl.BlockSpec(part.shape, lambda p, s, _: (0, 0)) for part in parts],
            out_specs=pl.BlockSpec((block, channels), lambda p, s, _: (p * s, 0)),
            scratch_shapes=[pltpu.VMEM((length, channels), SHORT), pltpu.VMEM((2, length, channels), SHORT)],
        ),
        out_shape=jax.ShapeDtypeStruct((length, channels), SHORT),
        compiler_params=kernel_params(2),
        cost_estimate=cost(8 * length * length * channels, 8 * length * length),
    )(places, table[0], table[1], spectrum, *parts)


def prepare_kernel(index_ref, filters_ref, gate_ref, cotangent_ref, out_ref):
    out_ref[0, 0] = filters_ref[...].astype(SHORT)
    out_ref[0, 1] = (cotangent_ref[...].astype(WIDE) * gate_ref[...].astype(WIDE)).astype(SHORT)


def prepare(filters, gate, cotangent, groups, waits):
    rows, width = filters.shape
    channels = width // groups
    if channels % 128:
        both = jnp.stack([filters, cotangent.astype(WIDE) * gate.astype(WIDE)]).astype(SHORT)
        return both.reshape(2, rows, groups, channels).transpose(2, 0, 1, 3)
    spec = pl.BlockSpec((rows, channels), lambda g: (0, g))
    return pl.pallas_call(
        waiting(prepare_kernel, len(waits)),
        grid=(groups,),
        in_specs=[pl.BlockSpec(memory_space=pltpu.SMEM)] + [ANYWHERE] * len(waits) + [spec] * 3,
        out_specs=pl.BlockSpec((1, 2, rows, channels), lambda g: (g, 0, 0, 0)),
        out_shape=jax.ShapeDtypeStruct((groups, 2, rows, channels), SHORT),
        compiler_params=kernel_params(1),
        cost_estimate=cost(2 * rows * width, 12 * rows * width),
    )(jnp.zeros((1,), jnp.int32), *waits, filters, gate, cotangent)


def finish_kernel(convolved_ref, gate_ref, cotangent_ref, output_ref, grad_ref):
    convolved = convolved_ref[0].astype(WIDE)
    output_ref[...] = (gate_ref[...].astype(WIDE) * convolved).astype(SHORT)
    grad_ref[...] = (cotangent_ref[...].astype(WIDE) * convolved).astype(SHORT)


def finish(convolved, gate, cotangent):
    groups, rows, channels = convolved.shape
    width = groups * channels
    if channels % 128:
        wide = convolved.swapaxes(0, 1).reshape(rows, width).astype(WIDE)
        return [(other.astype(WIDE) * wide).astype(SHORT) for other in (gate, cotangent)]
    spec = pl.BlockSpec((rows, channels), lambda g: (0, g))
    return pl.pallas_call(
        finish_kernel,
        grid=(groups,),
        in_specs=[pl.BlockSpec((1, rows, channels), lambda g: (g, 0, 0)), spec, spec],
        out_specs=[spec, spec],
        out_shape=[jax.ShapeDtypeStruct((rows, width), SHORT)] * 2,
        compiler_params=kernel_params(1),
        cost_estimate=cost(2 * rows * width, 10 * rows * width),
    )(convolved, gate, cotangent)


def arrange_kernel(dims, index_ref, *refs):
    outer, inner, far, near, halves, half_rows = dims
    part_refs, out_refs = refs[:inner], refs[inner:]
    channels = part_refs[0].shape[-1]
    tp = far * near
    for s in range(inner):
        lanes = aligned(index_ref[s], channels)
        for ahead in range(tp):
            source = index_ref[inner + ahead]
            for o in range(outer):
                for h in range(halves):
                    place = (ahead * outer + o) * half_rows
                    piece = part_refs[s][o, aligned(source * halves + h, half_rows)]
                    out_refs[h][place : place + half_rows, lanes] = piece


def arrange(parts, inner_places, sources, dims, waits):
    outer, inner, far, near, halves, half_rows = dims
    channels = parts[0].shape[-1]
    tp = far * near
    shape = (tp * outer * half_rows, inner * channels)
    if channels % 128:
        slots = jnp.zeros((inner, *parts[0].shape), SHORT)
        for s in range(inner):
            slots = lax.dynamic_update_index_in_dim(slots, parts[s], inner_places[s], 0)
        slots = slots.reshape(inner, outer, tp, halves, half_rows, channels).transpose(2, 3, 1, 4, 0, 5)
        slots = jnp.stack([pick(slots, sources[a]) for a in range(tp)])
        return [slots[:, h].reshape(shape) for h in range(halves)]
    index = jnp.concatenate([inner_places, sources]).astype(jnp.int32)
    size = math.prod(shape) * 2
    return pl.pallas_call(
        waiting(functools.partial(arrange_kernel, dims), len(waits)),
        in_specs=[pl.BlockSpec(memory_space=pltpu.SMEM)]
        + [ANYWHERE] * len(waits)
        + [pl.BlockSpec(memory_space=pltpu.VMEM)] * inner,
        out_specs=[pl.BlockSpec(memory_space=pltpu.VMEM)] * halves,
        out_shape=[jax.ShapeDtypeStruct(shape, SHORT)] * halves,
        compiler_params=kernel_params(0),
        cost_estimate=cost(0, 2 * halves * size),
    )(index, *waits, *parts)


def assemble_kernel(dims, index_ref, *refs):
    halves, steps, blocks, half_rows, depth = dims
    out_ref = refs[-1]
    for h in range(halves):
        for s in range(steps):
            rows = aligned(index_ref[s] * halves + h, half_rows)
            for b in range(blocks):
                out_ref[rows, aligned(index_ref[steps + b], depth)] = refs[h * steps + s][b]


def assemble(pieces, row_places, block_places, columns):
    halves, steps = len(pieces), len(pieces[0])
    blocks, half_rows, depth = pieces[0][0].shape
    flat = [piece for half in pieces for piece in half]
    rows = halves * steps * half_rows
    return pl.pallas_call(
        functools.partial(assemble_kernel, (halves, steps, blocks, half_rows, depth)),
        in_specs=[pl.BlockSpec(memory_space=pltpu.SMEM)] + [pl.BlockSpec(memory_space=pltpu.VMEM)] * len(flat),
        out_specs=pl.BlockSpec(memory_space=pltpu.VMEM),
        out_shape=jax.ShapeDtypeStruct((rows, columns), SHORT),
        compiler_params=kernel_params(0),
        cost_estimate=cost(0, 4 * rows * columns),
    )(jnp.concatenate([row_places, block_places]).astype(jnp.int32), *flat)


def chunk_kernel(index_ref, in_ref, out_ref):
    out_ref[...] = in_ref[...]


def chunk_of(array, index, count):
    rows, width = array.shape
    chunk = width // count
    block = min(rows, 256)
    if chunk % 128:
        return lax.dynamic_slice_in_dim(array, index * chunk, chunk, 1)
    return pl.pallas_call(
        chunk_kernel,
        grid_spec=pltpu.PrefetchScalarGridSpec(
            num_scalar_prefetch=1,
            grid=(rows // block,),
            in_specs=[pl.BlockSpec((block, chunk), lambda r, index: (r, index[0]))],
            out_specs=pl.BlockSpec((block, chunk), lambda r, _: (r, 0)),
        ),
        out_shape=jax.ShapeDtypeStruct((rows, chunk), array.dtype),
        compiler_params=kernel_params(1),
        cost_estimate=cost(0, 4 * rows * chunk),
    )(index[None].astype(jnp.int32), array)


def join_kernel(index_ref, *refs):
    size = refs[0].shape[0]
    for p, ref in enumerate(refs[:-1]):
        refs[-1][p * size : (p + 1) * size] = ref[...]


def join(parts, waits):
    size, width = parts[0].shape
    rows = len(parts) * size
    if size % 16:
        return jnp.concatenate(parts, axis=0)
    return pl.pallas_call(
        waiting(join_kernel, len(waits)),
        in_specs=[pl.BlockSpec(memory_space=pltpu.SMEM)]
        + [ANYWHERE] * len(waits)
        + [pl.BlockSpec(memory_space=pltpu.VMEM)] * len(parts),
        out_specs=pl.BlockSpec(memory_space=pltpu.VMEM),
        out_shape=jax.ShapeDtypeStruct((rows, width), parts[0].dtype),
        compiler_params=kernel_params(0),
        cost_estimate=cost(0, 4 * rows * width),
    )(jnp.zeros((1,), jnp.int32), *waits, *parts)


def product_kernel(dims, index_ref, *refs):
    inner, outer, pieces, depth, add = dims
    token_refs, weight_refs, out_ref = refs[:pieces], refs[pieces : pieces + inner], refs[-1]
    size = token_refs[0].shape[0] // outer
    parts = [aligned(index_ref[2 + inner + s], size) for s in range(outer)]
    total = refs[-2][...].astype(WIDE) if add else 0.0
    for i in range(inner):
        columns = aligned(index_ref[2 + i], depth)
        tokens = jnp.concatenate([ref[rows, columns] for ref in token_refs for rows in parts], axis=0)
        total = total + wide_dot(tokens, weight_refs[i][...])
    out_ref[...] = total.astype(SHORT).reshape(out_ref.shape)


def product(pieces, in_weight, chunk_index, received, inner_blocks, row_order, running, last, waits):
    inner = len(received) + 1
    outer = row_order.shape[0]
    depth, width = in_weight.shape
    chunk = width // outer
    channels = chunk // inner
    size, whole_depth = pieces[0].shape
    rows = len(pieces) * size
    at_inner = inner_blocks[0]
    if channels % 128:
        tokens = jnp.stack(pieces).reshape(len(pieces), outer, size // outer, whole_depth)
        tokens = jnp.concatenate([pick(tokens, row_order[s], 1)[:, None] for s in range(outer)], axis=1)
        tokens = tokens.reshape(rows, whole_depth)
        weights = [chunk_of(in_weight, chunk_index, outer)] + received
        total = sum(
            wide_dot(lax.dynamic_slice_in_dim(tokens, inner_blocks[i] * depth, depth, 1), weights[i])
            for i in range(inner)
        )
        if running is not None:
            total = total + running.astype(WIDE)
        total = total.astype(SHORT)
        if last:
            total = total.reshape(rows, inner, channels)
            total = jnp.stack([pick(total, (at_inner + i) % inner, 1) for i in range(inner)])
        return total
    if last:
        out_spec = pl.BlockSpec((1, rows, channels), lambda g, index: ((g + inner - index[2]) % inner, 0, 0))
        out_shape = (inner, rows, channels)
    else:
        out_spec = pl.BlockSpec((rows, channels), lambda g, _: (0, g))
        out_shape = (rows, chunk)
    block = pl.BlockSpec((depth, channels), lambda g, _: (0, g))
    index = jnp.concatenate([chunk_index[None], at_inner[None], inner_blocks, row_order]).astype(jnp.int32)
    return pl.pallas_call(
        waiting(
            functools.partial(product_kernel, (inner, outer, len(pieces), depth, running is not None)), len(waits)
        ),
        grid_spec=pltpu.PrefetchScalarGridSpec(
            num_scalar_prefetch=1,
            grid=(inner,),
            in_specs=[ANYWHERE] * len(waits)
            + [pl.BlockSpec((size, whole_depth), lambda g, _: (0, 0)) for _ in pieces]
            + [pl.BlockSpec((depth, channels), lambda g, index: (0, index[0] * inner + g))]
            + [block for _ in received]
            + ([] if running is None else [pl.BlockSpec((rows, channels), lambda g, _: (0, g))]),
            out_specs=out_spec,
        ),
        out_shape=jax.ShapeDtypeStruct(out_shape, SHORT),
        compiler_params=kernel_params(1),
        cost_estimate=cost(2 * rows * whole_depth * chunk, 2 * (rows + chunk) * whole_depth + 4 * rows * chunk),
    )(index, *waits, *pieces, in_weight, *received, *([] if running is None else [running]))


def shares_kernel(dims, index_ref, grad_ref, *refs):
    outer, inner, near, chunk = dims
    own_ref, received_refs = refs[0], refs[1 : 1 + (inner - 1) * outer]
    out_refs, plain_ref = refs[1 + (inner - 1) * outer : -1], refs[-1]
    size = out_refs[0].shape[1]

    @pl.when(pl.program_id(0) == 0)
    def _():
        for o in range(outer):
            plain_ref[:, o * chunk : (o + 1) * chunk] = grad_ref[o]

    for i in range(inner):
        if i == 0:
            total = wide_dot_turned(plain_ref[...], own_ref[...])
        else:
            total = sum(
                wide_dot_turned(grad_ref[index_ref[s]], received_refs[(i - 1) * outer + s][...]) for s in range(outer)
            )
        total = total.astype(SHORT)
        for n in range(near):
            out_refs[n][i] = total[n * size : (n + 1) * size]


def shares(grad_values, in_weight, received, chunks, near, waits):
    outer, rows, chunk = grad_values.shape
    inner = len(received) + 1
    depth, width = in_weight.shape
    if chunk // inner % 128:
        plain = grad_values.swapaxes(0, 1).reshape(rows, width)
        totals = [wide_dot_turned(plain, in_weight)] + [
            sum(wide_dot_turned(pick(grad_values, chunks[s]), held[s]) for s in range(outer)) for held in received
        ]
        total = jnp.stack(totals).astype(SHORT).reshape(inner, near, rows // near, depth)
        return [total[:, n] for n in range(near)]
    block = min(depth, 256)
    flat = [w for held in received for w in held]
    out_spec = pl.BlockSpec((inner, rows // near, block), lambda k, _: (0, 0, k))
    return pl.pallas_call(
        waiting(functools.partial(shares_kernel, (outer, inner, near, chunk)), len(waits)),
        grid_spec=pltpu.PrefetchScalarGridSpec(
            num_scalar_prefetch=1,
            grid=(depth // block,),
            in_specs=[ANYWHERE] * len(waits)
            + [pl.BlockSpec((outer, rows, chunk), lambda k, _: (0, 0, 0))]
            + [pl.BlockSpec((block, width), lambda k, _: (k, 0))]
            + [pl.BlockSpec((block, chunk), lambda k, _: (k, 0)) for _ in flat],
            out_specs=[out_spec] * near,
            scratch_shapes=[pltpu.VMEM((rows, width), SHORT)],
        ),
        out_shape=[jax.ShapeDtypeStruct((inner, rows // near, depth), SHORT)] * near,
        compiler_params=kernel_params(1),
        cost_estimate=cost(
            2 * rows * width * inner * depth, 2 * (inner * depth + rows) * width + 2 * rows * inner * depth
        ),
    )(chunks.astype(jnp.int32), *waits, grad_values, in_weight, *flat)


def shifted(array, axis, shift):
    size = lax.axis_size(axis)
    return lax.ppermute(array, axis, [(at, (at + shift) % size) for at in range(size)])


def pick(array, index, axis=0):
    return lax.dynamic_index_in_dim(array, index, axis, keepdims=False)


def turned(parts, start):
    count = len(parts)
    backwards = jnp.stack(parts[::-1])
    doubled = jnp.concatenate([backwards, backwards], axis=0)
    return lax.dynamic_slice_in_dim(doubled, (count - 1 - start) % count, count, 0)


def per_device(tokens, in_weight, filters, gate, cotangent):
    outer, inner, far, near = (lax.axis_size(a) for a in ("outer", "inner", "far", "near"))
    at_outer, at_inner, at_far, at_near = (lax.axis_index(a) for a in ("outer", "inner", "far", "near"))
    tp = far * near
    at_tp = at_far * near + at_near
    rows, columns = tokens.shape
    fine_rows = rows // tp
    halves = 2 if fine_rows >= 32 else 1
    half_rows = fine_rows // halves
    ctx = ("outer", "inner")
    ctx_size = outer * inner
    cell = ("outer", "far", "near")
    split = tp // outer
    depth, width = in_weight.shape
    channels = width // ctx_size
    tile_blocks = columns // depth
    length = ctx_size * rows
    back_inner = [(at_inner - i) % inner for i in range(inner)]

    def destination(source_outer, source_tp, step):
        part = (source_outer * split + source_tp % split + step) % tp
        return (source_tp // split) * tp + part

    chunks = [(at_outer - s) % outer for s in range(outer)]
    order = [s % outer for s in range(1, outer + 1)]
    received = [[None] * outer for _ in range(1, inner)]
    for s in order:
        sent = chunk_of(in_weight, chunks[s], outer)
        for i in range(1, inner):
            received[i - 1][s] = shifted(sent, "inner", i)

    moved = []
    if split == 1:
        by_far = tokens.reshape(far, near * fine_rows, columns)
        held = [pick(by_far, at_far)] + [shifted(pick(by_far, (at_far + f) % far), "far", f) for f in range(1, far)]
        held = jnp.stack(held).reshape(far, near, fine_rows, columns)
        for step in range(tp):
            pairs = []
            for o in range(outer):
                for g in range(far):
                    for c in range(near):
                        tile, part = (o + step) % tp // near, (o + step) % tp % near
                        pairs.append(((o * far + g) * near + c, ((tile * near + c) * far + g) * near + part))
            number = (at_outer + step) % tp
            part = lax.dynamic_slice(
                held, ((at_far - number // near) % far, number % near, 0, 0), (1, 1, fine_rows, columns)
            )
            moved.append(lax.ppermute(part.reshape(fine_rows, columns), cell, pairs))
        token_part = join(moved, [held[s] for held in received for s in order[:2]])
    else:
        row_parts = tokens.reshape(tp, fine_rows, columns)
        for step in range(tp):
            pairs = [(o * tp + t, destination(o, t, step)) for o in range(outer) for t in range(tp)]
            part = (at_outer * split + at_tp % split + step) % tp
            moved.append(lax.ppermute(pick(row_parts, part), cell, pairs))
        token_part = turned(moved, at_tp).reshape(outer, split, fine_rows, columns).swapaxes(1, 2)
        token_part = token_part.reshape(outer * fine_rows, split * columns)

    prepared = prepare(filters, gate, cotangent, ctx_size, [token_part])
    channel_rows = lax.all_to_all(prepared, ctx, split_axis=0, concat_axis=0, tiled=True)
    table = transform_table(length)

    pieces = [token_part] + [shifted(token_part, "far", f) for f in range(1, far)]
    pieces = pieces + [shifted(piece, "near", n) for n in range(1, near) for piece in pieces]
    places = []
    for n in range(near):
        for f in range(far):
            source_near = (at_near - n) % near
            source = (at_far - f) % far * near + source_near
            for s in range(outer):
                source_outer = (source_near - s) % outer if split == 1 else s
                places.append(source_outer * (inner * tp) + source)
    places = jnp.stack(places).astype(jnp.int32)
    places = jnp.stack([places + back_inner[s] * tp for s in range(inner)])

    grad_values, spectrum = correlate(table, rotation(length), channel_rows)
    by_inner = grad_values.reshape(outer, inner, rows, channels)
    grad_parts = [pick(by_inner, at_inner, 1)]
    for i in range(1, inner):
        grad_parts.append(shifted(pick(by_inner, (at_inner + i) % inner, 1), "inner", i))
    blocks = jnp.stack(back_inner)
    turn = at_outer // near * near if split == 1 else 0
    row_order = jnp.stack([(s + turn) % outer + at_outer * 0 for s in range(outer)])
    running = None
    for s in order:
        if running is not None:
            running = shifted(running, "outer", 1)
        held = [chunk[s] for chunk in received]
        waits = [chunk[(s + 1) % outer] for chunk in received if s != 0]
        if s == 1:
            waits = waits + list(table)
        if s == outer - 1:
            waits = waits + [spectrum]
        if s == 0:
            waits = waits + grad_parts
        running = product(pieces, in_weight, chunks[s], held, blocks, row_order, running, s == 0, waits)
    value_parts = [running[0]] + [shifted(running[i], "inner", i) for i in range(1, inner)]

    sources = [(at_far + f) % far * near + (at_near + n) % near for n in range(near) for f in range(far)]
    arranged = arrange(
        grad_parts, jnp.stack(back_inner), jnp.stack(sources), (outer, inner, far, near, halves, half_rows), [running]
    )

    convolved = convolve(table, spectrum, value_parts, places).reshape(ctx_size, rows, channels)

    sent_back = []
    waits = [convolved]
    for half in arranged:
        gathered = lax.all_gather(half, "outer", axis=0, tiled=False)
        by_near = shares(gathered, in_weight, received, jnp.stack(chunks), near, waits)
        total = by_near[0].astype(WIDE) + sum(shifted(by_near[n], "near", n).astype(WIDE) for n in range(1, near))
        total = total.astype(SHORT).reshape(inner, far, outer * half_rows, depth)
        total = total[:, 0].astype(WIDE) + sum(shifted(total[:, f], "far", f).astype(WIDE) for f in range(1, far))
        total = total.astype(SHORT).reshape(inner, outer, half_rows, depth)
        if split == 1:
            total = total.swapaxes(0, 1)
        else:
            total = turned(list(total), at_inner).reshape(split, tile_blocks, outer, half_rows, depth)
            total = total.transpose(2, 0, 1, 3, 4).reshape(tp, tile_blocks, half_rows, depth)
        back = []
        for step in range(tp):
            pairs = [(destination(o, t, step), o * tp + t) for o in range(outer) for t in range(tp)]
            back.append(lax.ppermute(pick(total, (at_tp - step) % tp), cell, pairs))
        sent_back.append(back)
        waits = back
    row_places = [(at_outer * split + at_tp % split + step) % tp for step in range(tp)]
    block_places = back_inner if split == 1 else [jnp.int32(b) for b in range(tile_blocks)]
    grad_tokens = assemble(sent_back, jnp.stack(row_places), jnp.stack(block_places), columns)

    convolved = lax.all_to_all(convolved, ctx, split_axis=0, concat_axis=0, tiled=True)
    gated_output, grad_gate = finish(convolved, gate, cotangent)
    return (gated_output, grad_gate, grad_tokens)


def solution(mesh):
    ctx_size, tp_size = mesh.shape["ctx"], mesh.shape["tp"]
    inner, near = 1, 2
    while inner * inner * 4 <= ctx_size:
        inner *= 2
    fine_mesh = Mesh(
        np.asarray(mesh.devices).reshape(ctx_size // inner, inner, tp_size // near, near),
        ("outer", "inner", "far", "near"),
    )
    placed = P(("outer", "inner"), ("far", "near"))
    return jax.shard_map(
        per_device,
        mesh=fine_mesh,
        in_specs=(placed,) * 5,
        out_specs=(placed,) * 3,
        check_vma=False,
    )
```

time: 1190 us -> 403 us (0.34)
  waiting for transfers between devices: 804 us -> 152 us
  matrix products: 196 us -> 0 us
  Pallas kernels: 0 us -> 94.8 us
  starting transfers between devices: 4.98 us -> 86.5 us
  blocking collectives: 51.8 us -> 0 us
  local copies, waits for them, and re-layouts: 81.3 us -> 32.9 us
    all_gather x2, waiting for transfers between devices: 672 us -> 34.2 us  [per_device(): gathered = lax.all_gather(half, 'outer', axis=0, tiled=False)]
    dot_general x14 -> x0, matrix products: 196 us -> none  [the longest x1 19.7 us: first_inverse(): jnp.einsum('rq,bjqc->bjrc', cos_table, spectrum[0], precision=PRECISE)]
    ppermute x0 -> x29, waiting for transfers between devices: none -> 115 us  [the longest x17 97.6 us: shifted(): lax.ppermute(array, axis, [(at, (at + shift) % size) for at in range(size)])]
    pallas_call x0 -> x17, Pallas kernels: none -> 94.8 us  [the longest x4 22.4 us: product(): pl.pallas_call(waiting(functools.partial(product_kernel, (inner, outer, l...]
    all_to_all x1 -> x2, waiting for transfers between devices: 92.9 us -> 2.68 us  [the longest x1 2.68 us: per_device(): lax.all_to_all(convolved, ctx, split_axis=0, concat_axis=0, tiled=True)]
    ppermute x0 -> x29, starting transfers between devices: none -> 77.8 us  [the longest x17 50.5 us: shifted(): lax.ppermute(array, axis, [(at, (at + shift) % size) for at in range(size)])]
    all_to_all x1 -> x0, blocking collectives: 51.8 us -> none  [per_device(): lax.all_to_all(shortened(result), 'ctx', split_axis=1, concat_axis=2, til...]
    reduce_scatter x1 -> x0, waiting for transfers between devices: 38.1 us -> none  [per_device(): lax.psum_scatter(partial_value.astype(jnp.bfloat16), 'tp', scatter_dimens...]
  transfers between devices with their start and end apart: 4 -> 33, of which waited for: 4 -> 17; matrix products, arithmetic and copies ran while one was open for 1% -> 7% of each run, Pallas kernels for 0% -> 18%
where the time goes in v1:
time: 403 us; the launch traced here: 401 us
  waiting for transfers between devices  152 us (38%)
  Pallas kernels  94.8 us (24%)
  starting transfers between devices  86.5 us (21%)
  local copies, waits for them, and re-layouts  32.9 us (8%)
  other arithmetic  20.4 us (5%)
  between operations  14.4 us (4%)
    ppermute x17, waiting for transfers between devices, shifted(): lax.ppermute(array, axis, [(at, (at + shift) % size) for at in range(size)])  97.6 us
    ppermute x17, starting transfers between devices, shifted(): lax.ppermute(array, axis, [(at, (at + shift) % size) for at in range(size)])  50.5 us
    all_gather x2, waiting for transfers between devices, per_device(): gathered = lax.all_gather(half, 'outer', axis=0, tiled=False)  34.2 us
    unnamed x56, local copies, waits for them, and re-layouts  24.2 us
    pallas_call x4, Pallas kernels, product(): pl.pallas_call(waiting(functools.partial(product_kernel, (inner, outer, l...  22.4 us
    pallas_call x1, Pallas kernels, correlate(): pl.pallas_call(correlate_kernel, grid=(2, steps), in_specs=[table_spec, t...  20.2 us
    pallas_call x2, Pallas kernels, shares(): pl.pallas_call(waiting(functools.partial(shares_kernel, (outer, inner, ne...  17.4 us
    pallas_call x1, Pallas kernels, convolve(): pl.pallas_call(functools.partial(convolve_kernel, len(parts)), grid_spec=...  16.6 us
  transfers between devices with their start and end apart: 33, of which 17 were waited for; matrix products, arithmetic and copies ran while one was open for 7% of the time, Pallas kernels for 18%

profile of v1, /device:TPU:4, one launch (start us, length us, event | category | flops | bytes accessed | tf_op | source)
XLA Modules:
  0.0 401.4 jit_solution(5526545597224218485)
XLA Ops:
  31.3 6.7 %collective-permute-start.6 = (bf16[64,2048]{1,0:T(8,128)(2,1)S(1)}, bf16[64,2048]{1,0:T(8,128)(2,1)S(1)}, u32[]{:S(2)}, u32[]{:S(2)}) collective-permute-start(bf16[64,2048]{1,0:T(8,128)(2,1)S(1)} %get-tuple-element.37), channel_id=1, source_target_pairs={{0,17},{1,25},{2,19},{3,27},{8,0},{9,8},{10,2},{11,10},{16,1},{17,... | collective-permute-start | bytes 786440 | tf_op jit(solution)/shard_map/ppermute | solution.py:536
  38.0 5.3 %collective-permute-done.4.refs_3_ = bf16[64,2048]{1,0:T(8,128)(2,1)S(1)} collective-permute-done((bf16[64,2048]{1,0:T(8,128)(2,1)S(1)}, bf16[64,2048]{1,0:T(8,128)(2,1)S(1)}, u32[]{:S(2)}, u32[]{:S(2)}) %collective-permute-start.4) | collective-permute-done | bytes 262176 | tf_op jit(solution)/shard_map/ppermute | solution.py:536
  43.3 6.1 %collective-permute-done.5.refs_4_ = bf16[64,2048]{1,0:T(8,128)(2,1)S(1)} collective-permute-done((bf16[64,2048]{1,0:T(8,128)(2,1)S(1)}, bf16[64,2048]{1,0:T(8,128)(2,1)S(1)}, u32[]{:S(2)}, u32[]{:S(2)}) %collective-permute-start.5) | collective-permute-done | bytes 262176 | tf_op jit(solution)/shard_map/ppermute | solution.py:536
  50.3 10.6 %collective-permute-done.1.refs_1_.refs_0_.refs_6_.refs_5_.refs_8_ = bf16[1024,512]{1,0:T(8,128)(2,1)S(1)} collective-permute-done((bf16[1024,512]{1,0:T(8,128)(2,1)}, bf16[1024,512]{1,0:T(8,128)(2,1)S(1)}, u32[]{:S(2)}, u32[]{:S(2)}) %collective-permute-start.1) | collective-permute-done | bytes 1048608 | tf_op jit(solution)/shard_map/ppermute | solution.py:475
  77.0 4.9 %all-to-all-start = ((bf16[8,2,256,256]{3,2,1,0:T(8,128)(2,1)}), bf16[8,2,256,256]{3,2,1,0:T(8,128)(2,1)}, u32[]{:S(2)}, u32[]{:S(2)}) async-start(bf16[8,2,256,256]{3,2,1,0:T(8,128)(2,1)} %copy-done.8), calls=%async_computation | async-start | bytes 4194304 | tf_op jit(solution)/shard_map/all_to_all | solution.py:548
  89.2 9.7 %add_convert_fusion = (bf16[64,32,2048]{2,1,0:T(8,128)(2,1)}, bf16[64,32,2048]{2,1,0:T(8,128)(2,1)}) fusion(f32[32,2048]{1,0:T(8,128)S(1)} %get-tuple-element.20, f32[64,2048]{1,0:T(8,128)} %get-tuple-element.19, f32[32,2048]{1,0:T(8,128)} %get-tuple-element.18, f32[64,2048]{1,0:T(8,128)} %get-tuple-element.17), kind=kLoop, calls=%fused_computation | loop fusion | flops 33554432 | bytes 18350080 | tf_op jit(solution)/shard_map/convert_element_type | solution.py:33
  98.9 5.8 %shard_map.83 = bf16[1024,512]{1,0:T(8,128)(2,1)} custom-call(s32[8]{0:T(128)S(1)} %concatenate.40.index_ref, bf16[1024,512]{1,0:T(8,128)(2,1)S(1)} %copy-done.6, bf16[2048,2048]{1,0:T(8,128)(2,1)} %bitcast.112, bf16[2048,2048]{1,0:T(8,128)(2,1)} %bitcast.109, bf16[256,2048]{1,0:T(8,128)(2,1)S(1)} %shard_map.78.refs_0_.refs_3_.refs_1_.refs_2_, ...), custom_call_target="tpu_custom_call" | custom-call | flops 2147483648 | bytes 8388608 | tf_op jit(solution)/shard_map/pallas_call | solution.py:396
  111.0 29.7 %collective-permute-done.13.refs_7_ = bf16[1024,512]{1,0:T(8,128)(2,1)} collective-permute-done((bf16[1024,512]{1,0:T(8,128)(2,1)}, bf16[1024,512]{1,0:T(8,128)(2,1)}, u32[]{:S(2)}, u32[]{:S(2)}) %collective-permute-start.13) | collective-permute-done | bytes 1048608 | tf_op jit(solution)/shard_map/ppermute | solution.py:475
  140.7 5.8 %shard_map.84 = bf16[1024,512]{1,0:T(8,128)(2,1)} custom-call(s32[8]{0:T(128)S(1)} %concatenate.39.index_ref, bf16[1024,512]{1,0:T(8,128)(2,1)} %collective-permute-done.12.refs_0_.refs_7_.refs_6_.refs_9_, bf16[256,2048]{1,0:T(8,128)(2,1)S(1)} %shard_map.78.refs_0_.refs_3_.refs_1_.refs_2_, ...), custom_call_target="tpu_custom_call" | custom-call | flops 2147483648 | bytes 8388608 | tf_op jit(solution)/shard_map/pallas_call | solution.py:396
  146.6 8.6 %collective-permute-start.14 = (bf16[1024,512]{1,0:T(8,128)(2,1)}, bf16[1024,512]{1,0:T(8,128)(2,1)}, u32[]{:S(2)}, u32[]{:S(2)}) collective-permute-start(bf16[1024,512]{1,0:T(8,128)(2,1)} %shard_map.84), channel_id=1, source_target_pairs={{0,8},{8,16},{16,24},{24,0},{1,9},{9,17},{17,25},{25,1},{2,10},{10... | collective-permute-start | bytes 3145736 | tf_op jit(solution)/shard_map/ppermute | solution.py:475
  156.4 20.2 %shard_map.80 = (bf16[2048,256]{1,0:T(8,128)(2,1)S(1)}, bf16[2,2048,256]{2,1,0:T(8,128)(2,1)S(1)}) custom-call(bf16[2048,2048]{1,0:T(8,128)(2,1)} %bitcast.113, bf16[2048,2048]{1,0:T(8,128)(2,1)} %bitcast.110, f32[2048,2]{1,0:T(8,128)S(1)} %copy-done.21, bf16[8,2,256,256]{3,2,1,0:T(8,128)(2,1)} %all-to-all-done.both_ref), custom_call_target="tpu_custom_call" | custom-call | flops 12884901888 | bytes 33554432 | tf_op jit(solution)/shard_map/pallas_call | solution.py:112
  178.9 5.8 %shard_map.85 = bf16[1024,512]{1,0:T(8,128)(2,1)} custom-call(s32[8]{0:T(128)S(1)} %concatenate.38.index_ref, bf16[1024,512]{1,0:T(8,128)(2,1)} %collective-permute-done.11.refs_0_.refs_7_.refs_3_.refs_6_, bf16[2,2048,256]{2,1,0:T(8,128)(2,1)} %copy-done.17, bf16[256,2048]{1,0:T(8,128)(2,1)S(1)} %shard_map.78.refs_0_.refs_3_.refs_1_.refs_2_, ...), custom_call_target="tpu_custom_call" | custom-call | flops 2147483648 | bytes 8388608 | tf_op jit(solution)/shard_map/pallas_call | solution.py:396
  189.4 17.2 %collective-permute-start.7 = (bf16[4,256,256]{2,1,0:T(8,128)(2,1)}, bf16[4,256,256]{2,1,0:T(8,128)(2,1)}, u32[]{:S(2)}, u32[]{:S(2)}) collective-permute-start(bf16[4,256,256]{2,1,0:T(8,128)(2,1)} %get-tuple-element.35), channel_id=1, source_target_pairs={{0,4},{4,0},{1,5},{5,1},{2,6},{6,2},{3,7},{7,3},{8,12},{12,8},{9,1... | collective-permute-start | bytes 1572872 | tf_op jit(solution)/shard_map/ppermute | solution.py:475
  206.8 11.3 %collective-permute-done.7.refs_1_.refs_2_ = bf16[4,256,256]{2,1,0:T(8,128)(2,1)} collective-permute-done((bf16[4,256,256]{2,1,0:T(8,128)(2,1)}, bf16[4,256,256]{2,1,0:T(8,128)(2,1)}, u32[]{:S(2)}, u32[]{:S(2)}) %collective-permute-start.7) | collective-permute-done | bytes 524320 | tf_op jit(solution)/shard_map/ppermute | solution.py:475
  219.1 5.0 %shard_map.86.refs_0_ = bf16[2,1024,256]{2,1,0:T(8,128)(2,1)S(1)} custom-call(s32[8]{0:T(128)S(1)} %concatenate.37.index_ref, bf16[4,256,256]{2,1,0:T(8,128)(2,1)S(1)} %copy-done.9, bf16[4,256,256]{2,1,0:T(8,128)(2,1)} %collective-permute-done.7.refs_1_.refs_2_, bf16[256,2048]{1,0:T(8,128)(2,1)S(1)} %shard_map.78.refs_0_.refs_3_.refs_1_.refs_2_, ...), custom_call_target="tpu_custom_call" | custom-call | flops 2147483648 | bytes 8388608 | tf_op jit(solution)/shard_map/pallas_call | solution.py:396
  228.6 12.6 %collective-permute-start.16 = (bf16[1024,256]{1,0:T(8,128)(2,1)S(1)}, bf16[1024,256]{1,0:T(8,128)(2,1)S(1)}, u32[]{:S(2)}, u32[]{:S(2)}) collective-permute-start(bf16[1024,256]{1,0:T(8,128)(2,1)S(1)} %get-tuple-element.33), channel_id=1, source_target_pairs={{0,4},{4,0},{1,5},{5,1},{2,6},{6,2},{3,7},{7,3},{8,12},{12,8},{9,1... | collective-permute-start | bytes 1572872 | tf_op jit(solution)/shard_map/ppermute | solution.py:475
  241.4 10.0 %collective-permute-done.16.refs_1_ = bf16[1024,256]{1,0:T(8,128)(2,1)S(1)} collective-permute-done((bf16[1024,256]{1,0:T(8,128)(2,1)S(1)}, bf16[1024,256]{1,0:T(8,128)(2,1)S(1)}, u32[]{:S(2)}, u32[]{:S(2)}) %collective-permute-start.16) | collective-permute-done | bytes 524320 | tf_op jit(solution)/shard_map/ppermute | solution.py:475
  254.8 16.6 %shard_map.87 = bf16[2048,256]{1,0:T(8,128)(2,1)S(1)} custom-call(s32[2,16]{1,0:T(2,128)S(1)} %pad_add_fusion.places_ref, bf16[2048,2048]{1,0:T(8,128)(2,1)} %bitcast.114, bf16[2048,2048]{1,0:T(8,128)(2,1)} %bitcast.111, bf16[2,2048,256]{2,1,0:T(8,128)(2,1)S(1)} %copy-done.18, bf16[1024,256]{1,0:T(8,128)(2,1)S(1)} %get-tuple-element.34.refs_0_, ...), custom_call_target="tpu_custom_call" | custom-call | flops 8589934592 | bytes 33554432 | tf_op jit(solution)/shard_map/pallas_call | solution.py:169
  271.5 11.1 %all-gather.5.cloned.1.call-done = bf16[2048,512]{1,0:T(8,128)(2,1)} async-done(((bf16[512,512]{1,0:T(8,128)(2,1)}), bf16[2048,512]{1,0:T(8,128)(2,1)}) %all-gather.5.cloned.1.call-update) | async-done | bytes 2097168 | tf_op jit(solution)/shard_map/all_gather | solution.py:597
  282.5 8.5 %shard_map.90 = (bf16[2,256,1024]{2,1,0:T(8,128)(2,1)S(1)}, bf16[2,256,1024]{2,1,0:T(8,128)(2,1)S(1)}) custom-call(s32[4]{0:T(128)S(1)} %pad_add_fusion.1.index_ref, bf16[8,256,256]{2,1,0:T(8,128)(2,1)S(1)} %bitcast.106, bf16[4,512,512]{2,1,0:T(8,128)(2,1)} %bitcast.123, bf16[1024,2048]{1,0:T(8,128)(2,1)} %refs_5_.3, ...), custom_call_target="tpu_custom_call" | custom-call | flops 4294967296 | bytes 12582912 | tf_op jit(solution)/shard_map/pallas_call | solution.py:453
  295.9 13.3 %collective-permute-done.18 = bf16[2,128,1024]{2,1,0:T(8,128)(2,1)S(1)} collective-permute-done((bf16[2,128,1024]{2,1,0:T(8,128)(2,1)S(1)}, bf16[2,128,1024]{2,1,0:T(8,128)(2,1)S(1)}, u32[]{:S(2)}, u32[]{:S(2)}) %collective-permute-start.18) | collective-permute-done | bytes 524320 | tf_op jit(solution)/shard_map/ppermute | solution.py:475
  316.8 23.1 %all-gather.7.cloned.1.call-done = bf16[2048,512]{1,0:T(8,128)(2,1)} async-done(((bf16[512,512]{1,0:T(8,128)(2,1)}), bf16[2048,512]{1,0:T(8,128)(2,1)}) %all-gather.7.cloned.1.call-update) | async-done | bytes 2097168 | tf_op jit(solution)/shard_map/all_gather | solution.py:597
  340.0 9.0 %shard_map.91 = (bf16[2,256,1024]{2,1,0:T(8,128)(2,1)S(1)}, bf16[2,256,1024]{2,1,0:T(8,128)(2,1)}) custom-call(s32[4]{0:T(128)S(1)} %pad_add_fusion.1.index_ref, bf16[2,32,1024]{2,1,0:T(8,128)(2,1)S(1)} %collective-permute-done.19.refs_0_, bf16[2,32,1024]{2,1,0:T(8,128)(2,1)S(1)} %collective-permute-done.20.refs_1_, ...), custom_call_target="tpu_custom_call" | custom-call | flops 4294967296 | bytes 12582912 | tf_op jit(solution)/shard_map/pallas_call | solution.py:453
  356.3 13.6 %collective-permute-done.24 = bf16[2,128,1024]{2,1,0:T(8,128)(2,1)S(1)} collective-permute-done((bf16[2,128,1024]{2,1,0:T(8,128)(2,1)S(1)}, bf16[2,128,1024]{2,1,0:T(8,128)(2,1)S(1)}, u32[]{:S(2)}, u32[]{:S(2)}) %collective-permute-start.24) | collective-permute-done | bytes 524320 | tf_op jit(solution)/shard_map/ppermute | solution.py:475
  (148 shorter events, 116.6 us)
Async XLA Ops:
  13.3 36.0 %collective-permute-start = (bf16[1024,512]{1,0:T(8,128)(2,1)}, bf16[1024,512]{1,0:T(8,128)(2,1)S(1)}, u32[]{:S(2)}, u32[]{:S(2)}) collective-permute-start(bf16[1024,512]{1,0:T(8,128)(2,1)} %shard_map.76), channel_id=1, source_target_pairs={{0,4},{4,0},{1,5},{5,1},{2,6},{6,2},{3,7},{7,3},{8,12},{12,8},{9,1... | collective-permute-start | bytes 3145736 | tf_op jit(solution)/shard_map/ppermute | solution.py:475
  19.1 41.8 %collective-permute-start.1 = (bf16[1024,512]{1,0:T(8,128)(2,1)}, bf16[1024,512]{1,0:T(8,128)(2,1)S(1)}, u32[]{:S(2)}, u32[]{:S(2)}) collective-permute-start(bf16[1024,512]{1,0:T(8,128)(2,1)} %shard_map.77), channel_id=1, source_target_pairs={{0,4},{4,0},{1,5},{5,1},{2,6},{6,2},{3,7},{7,3},{8,12},{12,8},{9,1... | collective-permute-start | bytes 3145736 | tf_op jit(solution)/shard_map/ppermute | solution.py:475
  25.7 17.5 %collective-permute-start.4 = (bf16[64,2048]{1,0:T(8,128)(2,1)S(1)}, bf16[64,2048]{1,0:T(8,128)(2,1)S(1)}, u32[]{:S(2)}, u32[]{:S(2)}) collective-permute-start(bf16[64,2048]{1,0:T(8,128)(2,1)S(1)} %get-tuple-element.39), channel_id=1, source_target_pairs={{0,1},{1,9},{2,3},{3,11},{8,16},{9,24},{10,18},{11,26},{16,17},{17... | collective-permute-start | bytes 786440 | tf_op jit(solution)/shard_map/ppermute | solution.py:536
  28.7 20.6 %collective-permute-start.5 = (bf16[64,2048]{1,0:T(8,128)(2,1)S(1)}, bf16[64,2048]{1,0:T(8,128)(2,1)S(1)}, u32[]{:S(2)}, u32[]{:S(2)}) collective-permute-start(bf16[64,2048]{1,0:T(8,128)(2,1)S(1)} %get-tuple-element.40), channel_id=1, source_target_pairs={{0,16},{1,24},{2,18},{3,26},{8,17},{9,25},{10,19},{11,27},{16,0},{... | collective-permute-start | bytes 786440 | tf_op jit(solution)/shard_map/ppermute | solution.py:536
  31.3 18.0 %collective-permute-start.6 = (bf16[64,2048]{1,0:T(8,128)(2,1)S(1)}, bf16[64,2048]{1,0:T(8,128)(2,1)S(1)}, u32[]{:S(2)}, u32[]{:S(2)}) collective-permute-start(bf16[64,2048]{1,0:T(8,128)(2,1)S(1)} %get-tuple-element.37), channel_id=1, source_target_pairs={{0,17},{1,25},{2,19},{3,27},{8,0},{9,8},{10,2},{11,10},{16,1},{17,... | collective-permute-start | bytes 786440 | tf_op jit(solution)/shard_map/ppermute | solution.py:536
  63.2 24.0 %collective-permute-start.8 = (bf16[256,2048]{1,0:T(8,128)(2,1)S(1)}, bf16[256,2048]{1,0:T(8,128)(2,1)S(1)}, u32[]{:S(2)}, u32[]{:S(2)}) collective-permute-start(bf16[256,2048]{1,0:T(8,128)(2,1)S(1)} %shard_map.78.refs_0_.refs_3_.refs_1_.refs_2_), channel_id=1, source_target_pairs={{0,2},{2,0},{1,3},{3,1},{4,6},{6,4},{5,7},{7,5},{8,10},{10,8},{9,1... | collective-permute-start | bytes 3145736 | tf_op jit(solution)/shard_map/ppermute | solution.py:475
  68.7 42.3 %collective-permute-start.12 = (bf16[1024,512]{1,0:T(8,128)(2,1)}, bf16[1024,512]{1,0:T(8,128)(2,1)}, u32[]{:S(2)}, u32[]{:S(2)}) collective-permute-start(bf16[1024,512]{1,0:T(8,128)(2,1)} %shard_map.82), channel_id=1, source_target_pairs={{0,4},{4,0},{1,5},{5,1},{2,6},{6,2},{3,7},{7,3},{8,12},{12,8},{9,1... | collective-permute-start | bytes 3145736 | tf_op jit(solution)/shard_map/ppermute | solution.py:475
  77.0 78.1 %all-to-all-start = ((bf16[8,2,256,256]{3,2,1,0:T(8,128)(2,1)}), bf16[8,2,256,256]{3,2,1,0:T(8,128)(2,1)}, u32[]{:S(2)}, u32[]{:S(2)}) async-start(bf16[8,2,256,256]{3,2,1,0:T(8,128)(2,1)} %copy-done.8), calls=%async_computation | async-start | bytes 4194304 | tf_op jit(solution)/shard_map/all_to_all | solution.py:548
  81.9 200.6 %all-gather.5.cloned.1.call-start = ((), (), s32[]{:S(2)}) async-start(), calls=%async_computation.2 | async-start | bytes 2621440 | tf_op jit(solution)/shard_map/all_gather | solution.py:597
  104.6 36.1 %collective-permute-start.13 = (bf16[1024,512]{1,0:T(8,128)(2,1)}, bf16[1024,512]{1,0:T(8,128)(2,1)}, u32[]{:S(2)}, u32[]{:S(2)}) collective-permute-start(bf16[1024,512]{1,0:T(8,128)(2,1)} %shard_map.83), channel_id=1, source_target_pairs={{0,8},{8,16},{16,24},{24,0},{1,9},{9,17},{17,25},{25,1},{2,10},{10... | collective-permute-start | bytes 3145736 | tf_op jit(solution)/shard_map/ppermute | solution.py:475
  107.7 71.2 %collective-permute-start.11 = (bf16[1024,512]{1,0:T(8,128)(2,1)}, bf16[1024,512]{1,0:T(8,128)(2,1)}, u32[]{:S(2)}, u32[]{:S(2)}) collective-permute-start(bf16[1024,512]{1,0:T(8,128)(2,1)} %shard_map.81), channel_id=1, source_target_pairs={{0,4},{4,0},{1,5},{5,1},{2,6},{6,2},{3,7},{7,3},{8,12},{12,8},{9,1... | collective-permute-start | bytes 3145736 | tf_op jit(solution)/shard_map/ppermute | solution.py:475
  146.6 32.3 %collective-permute-start.14 = (bf16[1024,512]{1,0:T(8,128)(2,1)}, bf16[1024,512]{1,0:T(8,128)(2,1)}, u32[]{:S(2)}, u32[]{:S(2)}) collective-permute-start(bf16[1024,512]{1,0:T(8,128)(2,1)} %shard_map.84), channel_id=1, source_target_pairs={{0,8},{8,16},{16,24},{24,0},{1,9},{9,17},{17,25},{25,1},{2,10},{10... | collective-permute-start | bytes 3145736 | tf_op jit(solution)/shard_map/ppermute | solution.py:475
  184.7 33.4 %collective-permute-start.15 = (bf16[1024,512]{1,0:T(8,128)(2,1)}, bf16[1024,512]{1,0:T(8,128)(2,1)}, u32[]{:S(2)}, u32[]{:S(2)}) collective-permute-start(bf16[1024,512]{1,0:T(8,128)(2,1)} %shard_map.85), channel_id=1, source_target_pairs={{0,8},{8,16},{16,24},{24,0},{1,9},{9,17},{17,25},{25,1},{2,10},{10... | collective-permute-start | bytes 3145736 | tf_op jit(solution)/shard_map/ppermute | solution.py:475
  189.4 28.7 %collective-permute-start.7 = (bf16[4,256,256]{2,1,0:T(8,128)(2,1)}, bf16[4,256,256]{2,1,0:T(8,128)(2,1)}, u32[]{:S(2)}, u32[]{:S(2)}) collective-permute-start(bf16[4,256,256]{2,1,0:T(8,128)(2,1)} %get-tuple-element.35), channel_id=1, source_target_pairs={{0,4},{4,0},{1,5},{5,1},{2,6},{6,2},{3,7},{7,3},{8,12},{12,8},{9,1... | collective-permute-start | bytes 1572872 | tf_op jit(solution)/shard_map/ppermute | solution.py:475
  227.2 112.7 %all-gather.7.cloned.1.call-start = ((), (), s32[]{:S(2)}) async-start(), calls=%async_computation.3 | async-start | bytes 2621440 | tf_op jit(solution)/shard_map/all_gather | solution.py:597
  228.6 22.8 %collective-permute-start.16 = (bf16[1024,256]{1,0:T(8,128)(2,1)S(1)}, bf16[1024,256]{1,0:T(8,128)(2,1)S(1)}, u32[]{:S(2)}, u32[]{:S(2)}) collective-permute-start(bf16[1024,256]{1,0:T(8,128)(2,1)S(1)} %get-tuple-element.33), channel_id=1, source_target_pairs={{0,4},{4,0},{1,5},{5,1},{2,6},{6,2},{3,7},{7,3},{8,12},{12,8},{9,1... | collective-permute-start | bytes 1572872 | tf_op jit(solution)/shard_map/ppermute | solution.py:475
  310.5 29.4 %collective-permute-start.19 = (bf16[2,32,1024]{2,1,0:T(8,128)(2,1)S(1)}, bf16[2,32,1024]{2,1,0:T(8,128)(2,1)S(1)}, u32[]{:S(2)}, u32[]{:S(2)}) collective-permute-start(bf16[2,32,1024]{2,1,0:T(8,128)(2,1)S(1)} %get-tuple-element.50), channel_id=1, source_target_pairs={{0,0},{8,1},{16,2},{24,3},{1,8},{9,9},{17,10},{25,11},{2,16},{10,1... | collective-permute-start | bytes 393224 | tf_op jit(solution)/shard_map/ppermute | solution.py:611
  313.4 26.5 %collective-permute-start.20 = (bf16[2,32,1024]{2,1,0:T(8,128)(2,1)S(1)}, bf16[2,32,1024]{2,1,0:T(8,128)(2,1)S(1)}, u32[]{:S(2)}, u32[]{:S(2)}) collective-permute-start(bf16[2,32,1024]{2,1,0:T(8,128)(2,1)S(1)} %get-tuple-element.49), channel_id=1, source_target_pairs={{1,0},{9,1},{17,2},{25,3},{2,8},{10,9},{18,10},{26,11},{3,16},{11,... | collective-permute-start | bytes 393224 | tf_op jit(solution)/shard_map/ppermute | solution.py:611
  313.6 26.3 %collective-permute-start.21 = (bf16[2,32,1024]{2,1,0:T(8,128)(2,1)S(1)}, bf16[2,32,1024]{2,1,0:T(8,128)(2,1)S(1)}, u32[]{:S(2)}, u32[]{:S(2)}) collective-permute-start(bf16[2,32,1024]{2,1,0:T(8,128)(2,1)S(1)} %get-tuple-element.48), channel_id=1, source_target_pairs={{2,0},{10,1},{18,2},{26,3},{3,8},{11,9},{19,10},{27,11},{0,16},{8,... | collective-permute-start | bytes 393224 | tf_op jit(solution)/shard_map/ppermute | solution.py:611
  316.8 23.2 %collective-permute-start.22 = (bf16[2,32,1024]{2,1,0:T(8,128)(2,1)S(1)}, bf16[2,32,1024]{2,1,0:T(8,128)(2,1)S(1)}, u32[]{:S(2)}, u32[]{:S(2)}) collective-permute-start(bf16[2,32,1024]{2,1,0:T(8,128)(2,1)S(1)} %get-tuple-element.47), channel_id=1, source_target_pairs={{3,0},{11,1},{19,2},{27,3},{0,8},{8,9},{16,10},{24,11},{1,16},{9,1... | collective-permute-start | bytes 393224 | tf_op jit(solution)/shard_map/ppermute | solution.py:611
  349.9 31.9 %all-to-all-start.1 = ((bf16[8,256,256]{2,1,0:T(8,128)(2,1)}), bf16[8,256,256]{2,1,0:T(8,128)(2,1)S(1)}, u32[]{:S(2)}, u32[]{:S(2)}) async-start(bf16[8,256,256]{2,1,0:T(8,128)(2,1)} %bitcast.107), calls=%async_computation.1 | async-start | bytes 2097152 | tf_op jit(solution)/shard_map/all_to_all | solution.py:618
  370.9 18.3 %collective-permute-start.25 = (bf16[2,32,1024]{2,1,0:T(8,128)(2,1)}, bf16[2,32,1024]{2,1,0:T(8,128)(2,1)}, u32[]{:S(2)}, u32[]{:S(2)}) collective-permute-start(bf16[2,32,1024]{2,1,0:T(8,128)(2,1)} %get-tuple-element.46), channel_id=1, source_target_pairs={{0,0},{8,1},{16,2},{24,3},{1,8},{9,9},{17,10},{25,11},{2,16},{10,1... | collective-permute-start | bytes 393224 | tf_op jit(solution)/shard_map/ppermute | solution.py:611
  375.4 15.5 %collective-permute-start.26 = (bf16[2,32,1024]{2,1,0:T(8,128)(2,1)}, bf16[2,32,1024]{2,1,0:T(8,128)(2,1)}, u32[]{:S(2)}, u32[]{:S(2)}) collective-permute-start(bf16[2,32,1024]{2,1,0:T(8,128)(2,1)} %get-tuple-element.45), channel_id=1, source_target_pairs={{1,0},{9,1},{17,2},{25,3},{2,8},{10,9},{18,10},{26,11},{3,16},{11,... | collective-permute-start | bytes 393224 | tf_op jit(solution)/shard_map/ppermute | solution.py:611
  375.4 16.0 %collective-permute-start.27 = (bf16[2,32,1024]{2,1,0:T(8,128)(2,1)}, bf16[2,32,1024]{2,1,0:T(8,128)(2,1)}, u32[]{:S(2)}, u32[]{:S(2)}) collective-permute-start(bf16[2,32,1024]{2,1,0:T(8,128)(2,1)} %get-tuple-element.44), channel_id=1, source_target_pairs={{2,0},{10,1},{18,2},{26,3},{3,8},{11,9},{19,10},{27,11},{0,16},{8,... | collective-permute-start | bytes 393224 | tf_op jit(solution)/shard_map/ppermute | solution.py:611
  (37 other events, 369.9 us)
Sparse Core Ops, SparseCore 0:
  227.4 55.1 all-gather.4
  284.1 55.7 all-gather.6

commit v2 on v1

--- a/solution.py
+++ b/solution.py
@@ -17,21 +17,14 @@
 
 def transform_table(length):
     period = 16 * length
-    fine_count = 32
-    fine = jnp.arange(fine_count, dtype=jnp.int32)[:, None]
-    coarse = jnp.arange(length // fine_count, dtype=jnp.int32)[:, None]
-    time = 4 * jnp.arange(length, dtype=jnp.int32)[None, :] + 1
-    scale = TWO_PI / period
-    fine_angle = ((4 * fine + 1) * time % period).astype(WIDE) * scale
-    coarse_angle = (4 * fine_count * coarse * time % period).astype(WIDE) * scale
-    fine_cos, fine_sin, coarse_cos, coarse_sin = lax.optimization_barrier(
-        (jnp.cos(fine_angle), jnp.sin(fine_angle), jnp.cos(coarse_angle), jnp.sin(coarse_angle))
-    )
-    fine_cos, fine_sin = fine_cos[None], fine_sin[None]
-    coarse_cos, coarse_sin = coarse_cos[:, None], coarse_sin[:, None]
-    cos_part = (coarse_cos * fine_cos - coarse_sin * fine_sin).astype(SHORT)
-    sin_part = (coarse_sin * fine_cos + coarse_cos * fine_sin).astype(SHORT)
-    return cos_part.reshape(length, length), sin_part.reshape(length, length)
+    if length > 2048:
+        points = 4 * jnp.arange(length, dtype=jnp.int32) + 1
+        angles = (points[:, None] * points[None, :] % period).astype(WIDE) * (TWO_PI / period)
+        return [jnp.cos(angles).astype(SHORT), jnp.sin(angles).astype(SHORT)]
+    points = 4 * np.arange(length, dtype=np.int64) + 1
+    turns = points[:, None] * points[None, :] % period
+    angles = np.arange(period) * (TWO_PI / period)
+    return [jnp.asarray(wave(angles).astype(SHORT)[turns]) for wave in (np.cos, np.sin)]
 
 
 def table_block(length):
@@ -57,8 +50,7 @@
     )
 
 
-def cost(flops, bytes_accessed):
-    return pl.CostEstimate(flops=flops, bytes_accessed=bytes_accessed, transcendentals=0)
+NO_COST = pl.CostEstimate(flops=0, bytes_accessed=0, transcendentals=0)
 
 
 ANYWHERE = pl.BlockSpec(memory_space=pl.ANY)
@@ -68,11 +60,27 @@
     return lambda index_ref, *refs: kernel(index_ref, *refs[count:])
 
 
+def release_kernel(index_ref, in_ref, out_ref):
+    pass
+
+
+def release(array, waits):
+    return pl.pallas_call(
+        waiting(release_kernel, len(waits)),
+        in_specs=[pl.BlockSpec(memory_space=pltpu.SMEM)] + [ANYWHERE] * (len(waits) + 1),
+        out_specs=ANYWHERE,
+        out_shape=jax.ShapeDtypeStruct(array.shape, array.dtype),
+        input_output_aliases={1 + len(waits): 0},
+        compiler_params=kernel_params(0),
+        cost_estimate=NO_COST,
+    )(jnp.zeros((1,), jnp.int32), *waits, array)
+
+
 def aligned(index, size):
     return pl.ds(pl.multiple_of(index * size, size), size)
 
 
-def correlate_kernel(cos_ref, sin_ref, turn_ref, both_ref, out_ref, spectrum_ref, signal_ref, mix_ref):
+def correlate_kernel(index_ref, cos_ref, sin_ref, turn_ref, both_ref, out_ref, spectrum_ref, signal_ref, mix_ref):
     phase, step = pl.program_id(0), pl.program_id(1)
     block = cos_ref.shape[0]
     length, channels = mix_ref.shape[1:]
@@ -103,16 +111,18 @@
         out_ref[...] = (total * (1.0 / length)).astype(out_ref.dtype)
 
 
-def correlate(table, turn, both):
+def correlate(table, turn, both, waits):
     parts, _, rows, channels = both.shape
     length = parts * rows
     block = table_block(length)
     steps = length // block
     table_spec = pl.BlockSpec((block, length), lambda p, s: (s, 0))
     return pl.pallas_call(
-        correlate_kernel,
+        waiting(correlate_kernel, len(waits)),
         grid=(2, steps),
         in_specs=[
+            pl.BlockSpec(memory_space=pltpu.SMEM),
+            *[ANYWHERE] * len(waits),
             table_spec,
             table_spec,
             pl.BlockSpec((block, 2), lambda p, s: (s, 0)),
@@ -128,8 +138,8 @@
         ],
         scratch_shapes=[pltpu.VMEM((length, 2 * channels), SHORT), pltpu.VMEM((2, length, channels), SHORT)],
         compiler_params=kernel_params(2),
-        cost_estimate=cost(12 * length * length * channels, 8 * length * length),
-    )(table[0], table[1], turn, both)
+        cost_estimate=NO_COST,
+    )(jnp.zeros((1,), jnp.int32), *waits, table[0], table[1], turn, both)
 
 
 def convolve_kernel(inner, places_ref, cos_ref, sin_ref, spectrum_ref, *refs):
@@ -182,7 +192,7 @@
         ),
         out_shape=jax.ShapeDtypeStruct((length, channels), SHORT),
         compiler_params=kernel_params(2),
-        cost_estimate=cost(8 * length * length * channels, 8 * length * length),
+        cost_estimate=NO_COST,
     )(places, table[0], table[1], spectrum, *parts)
 
 
@@ -205,7 +215,7 @@
         out_specs=pl.BlockSpec((1, 2, rows, channels), lambda g: (g, 0, 0, 0)),
         out_shape=jax.ShapeDtypeStruct((groups, 2, rows, channels), SHORT),
         compiler_params=kernel_params(1),
-        cost_estimate=cost(2 * rows * width, 12 * rows * width),
+        cost_estimate=NO_COST,
     )(jnp.zeros((1,), jnp.int32), *waits, filters, gate, cotangent)
 
 
@@ -229,7 +239,7 @@
         out_specs=[spec, spec],
         out_shape=[jax.ShapeDtypeStruct((rows, width), SHORT)] * 2,
         compiler_params=kernel_params(1),
-        cost_estimate=cost(2 * rows * width, 10 * rows * width),
+        cost_estimate=NO_COST,
     )(convolved, gate, cotangent)
 
 
@@ -271,7 +281,7 @@
         out_specs=[pl.BlockSpec(memory_space=pltpu.VMEM)] * halves,
         out_shape=[jax.ShapeDtypeStruct(shape, SHORT)] * halves,
         compiler_params=kernel_params(0),
-        cost_estimate=cost(0, 2 * halves * size),
+        cost_estimate=NO_COST,
     )(index, *waits, *parts)
 
 
@@ -296,7 +306,7 @@
         out_specs=pl.BlockSpec(memory_space=pltpu.VMEM),
         out_shape=jax.ShapeDtypeStruct((rows, columns), SHORT),
         compiler_params=kernel_params(0),
-        cost_estimate=cost(0, 4 * rows * columns),
+        cost_estimate=NO_COST,
     )(jnp.concatenate([row_places, block_places]).astype(jnp.int32), *flat)
 
 
@@ -304,24 +314,43 @@
     out_ref[...] = in_ref[...]
 
 
-def chunk_of(array, index, count):
+def chunks_of(array, indices, count, waits=()):
     rows, width = array.shape
     chunk = width // count
     block = min(rows, 256)
     if chunk % 128:
-        return lax.dynamic_slice_in_dim(array, index * chunk, chunk, 1)
-    return pl.pallas_call(
-        chunk_kernel,
+        return jnp.concatenate([lax.dynamic_slice_in_dim(array, i * chunk, chunk, 1) for i in indices], axis=1)
+    return pl.pallas_call(
+        waiting(chunk_kernel, len(waits)),
         grid_spec=pltpu.PrefetchScalarGridSpec(
             num_scalar_prefetch=1,
-            grid=(rows // block,),
-            in_specs=[pl.BlockSpec((block, chunk), lambda r, index: (r, index[0]))],
-            out_specs=pl.BlockSpec((block, chunk), lambda r, _: (r, 0)),
+            grid=(rows // block, len(indices)),
+            in_specs=[ANYWHERE] * len(waits) + [pl.BlockSpec((block, chunk), lambda r, c, index: (r, index[c]))],
+            out_specs=pl.BlockSpec((block, chunk), lambda r, c, _: (r, c)),
         ),
-        out_shape=jax.ShapeDtypeStruct((rows, chunk), array.dtype),
+        out_shape=jax.ShapeDtypeStruct((rows, len(indices) * chunk), array.dtype),
+        compiler_params=kernel_params(2),
+        cost_estimate=NO_COST,
+    )(jnp.stack(indices).astype(jnp.int32), *waits, array)
+
+
+def row_part(array, index, count, waits):
+    rows, width = array.shape
+    size = rows // count
+    if size % 16 or width % 128:
+        return lax.dynamic_slice_in_dim(array, index * size, size, 0)
+    return pl.pallas_call(
+        waiting(chunk_kernel, len(waits)),
+        grid_spec=pltpu.PrefetchScalarGridSpec(
+            num_scalar_prefetch=1,
+            grid=(1,),
+            in_specs=[ANYWHERE] * len(waits) + [pl.BlockSpec((size, width), lambda r, index: (index[0], 0))],
+            out_specs=pl.BlockSpec((size, width), lambda r, _: (0, 0)),
+        ),
+        out_shape=jax.ShapeDtypeStruct((size, width), array.dtype),
         compiler_params=kernel_params(1),
-        cost_estimate=cost(0, 4 * rows * chunk),
-    )(index[None].astype(jnp.int32), array)
+        cost_estimate=NO_COST,
+    )(index[None].astype(jnp.int32), *waits, array)
 
 
 def join_kernel(index_ref, *refs):
@@ -343,7 +372,7 @@
         out_specs=pl.BlockSpec(memory_space=pltpu.VMEM),
         out_shape=jax.ShapeDtypeStruct((rows, width), parts[0].dtype),
         compiler_params=kernel_params(0),
-        cost_estimate=cost(0, 4 * rows * width),
+        cost_estimate=NO_COST,
     )(jnp.zeros((1,), jnp.int32), *waits, *parts)
 
 
@@ -373,7 +402,8 @@
         tokens = jnp.stack(pieces).reshape(len(pieces), outer, size // outer, whole_depth)
         tokens = jnp.concatenate([pick(tokens, row_order[s], 1)[:, None] for s in range(outer)], axis=1)
         tokens = tokens.reshape(rows, whole_depth)
-        weights = [chunk_of(in_weight, chunk_index, outer)] + received
+        weights = [chunks_of(in_weight, [chunk_index], outer)]
+        weights += [held[:, at * chunk : (at + 1) * chunk] for held, at in received]
         total = sum(
             wide_dot(lax.dynamic_slice_in_dim(tokens, inner_blocks[i] * depth, depth, 1), weights[i])
             for i in range(inner)
@@ -391,7 +421,6 @@
     else:
         out_spec = pl.BlockSpec((rows, channels), lambda g, _: (0, g))
         out_shape = (rows, chunk)
-    block = pl.BlockSpec((depth, channels), lambda g, _: (0, g))
     index = jnp.concatenate([chunk_index[None], at_inner[None], inner_blocks, row_order]).astype(jnp.int32)
     return pl.pallas_call(
         waiting(
@@ -403,14 +432,16 @@
             in_specs=[ANYWHERE] * len(waits)
             + [pl.BlockSpec((size, whole_depth), lambda g, _: (0, 0)) for _ in pieces]
             + [pl.BlockSpec((depth, channels), lambda g, index: (0, index[0] * inner + g))]
-            + [block for _ in received]
+            + [
+                pl.BlockSpec((depth, channels), lambda g, _, at=at: (0, at * inner + g)) for _, at in received
+            ]
             + ([] if running is None else [pl.BlockSpec((rows, channels), lambda g, _: (0, g))]),
             out_specs=out_spec,
         ),
         out_shape=jax.ShapeDtypeStruct(out_shape, SHORT),
         compiler_params=kernel_params(1),
-        cost_estimate=cost(2 * rows * whole_depth * chunk, 2 * (rows + chunk) * whole_depth + 4 * rows * chunk),
-    )(index, *waits, *pieces, in_weight, *received, *([] if running is None else [running]))
+        cost_estimate=NO_COST,
+    )(index, *waits, *pieces, in_weight, *[held for held, _ in received], *([] if running is None else [running]))
 
 
 def shares_kernel(dims, index_ref, grad_ref, *refs):
@@ -443,7 +474,11 @@
     if chunk // inner % 128:
         plain = grad_values.swapaxes(0, 1).reshape(rows, width)
         totals = [wide_dot_turned(plain, in_weight)] + [
-            sum(wide_dot_turned(pick(grad_values, chunks[s]), held[s]) for s in range(outer)) for held in received
+            sum(
+                wide_dot_turned(pick(grad_values, chunks[s]), held[s][0][:, held[s][1] * chunk : (held[s][1] + 1) * chunk])
+                for s in range(outer)
+            )
+            for held in received
         ]
         total = jnp.stack(totals).astype(SHORT).reshape(inner, near, rows // near, depth)
         return [total[:, n] for n in range(near)]
@@ -458,16 +493,14 @@
             in_specs=[ANYWHERE] * len(waits)
             + [pl.BlockSpec((outer, rows, chunk), lambda k, _: (0, 0, 0))]
             + [pl.BlockSpec((block, width), lambda k, _: (k, 0))]
-            + [pl.BlockSpec((block, chunk), lambda k, _: (k, 0)) for _ in flat],
+            + [pl.BlockSpec((block, chunk), lambda k, _, at=at: (k, at)) for _, at in flat],
             out_specs=[out_spec] * near,
             scratch_shapes=[pltpu.VMEM((rows, width), SHORT)],
         ),
         out_shape=[jax.ShapeDtypeStruct((inner, rows // near, depth), SHORT)] * near,
         compiler_params=kernel_params(1),
-        cost_estimate=cost(
-            2 * rows * width * inner * depth, 2 * (inner * depth + rows) * width + 2 * rows * inner * depth
-        ),
-    )(chunks.astype(jnp.int32), *waits, grad_values, in_weight, *flat)
+        cost_estimate=NO_COST,
+    )(chunks.astype(jnp.int32), *waits, grad_values, in_weight, *[held for held, _ in flat])
 
 
 def shifted(array, axis, shift):
@@ -512,15 +545,23 @@
     chunks = [(at_outer - s) % outer for s in range(outer)]
     order = [s % outer for s in range(1, outer + 1)]
     received = [[None] * outer for _ in range(1, inner)]
-    for s in order:
-        sent = chunk_of(in_weight, chunks[s], outer)
+    arrivals = []
+
+    def send_pair(waits):
+        pair = order[2 * len(arrivals) : 2 * len(arrivals) + 2]
+        sent = chunks_of(in_weight, [chunks[s] for s in pair], outer, waits)
+        arrivals.append([shifted(sent, "inner", i) for i in range(1, inner)])
         for i in range(1, inner):
-            received[i - 1][s] = shifted(sent, "inner", i)
+            for at, s in enumerate(pair):
+                received[i - 1][s] = (arrivals[-1][i - 1], at)
+        return sent
 
     moved = []
     if split == 1:
-        by_far = tokens.reshape(far, near * fine_rows, columns)
-        held = [pick(by_far, at_far)] + [shifted(pick(by_far, (at_far + f) % far), "far", f) for f in range(1, far)]
+        by_far = [row_part(tokens, (at_far + f) % far, far, []) for f in range(far)]
+        sent = send_pair(by_far)
+        prepared = prepare(filters, gate, cotangent, ctx_size, [sent])
+        held = [by_far[0]] + [shifted(by_far[f], "far", f) for f in range(1, far)]
         held = jnp.stack(held).reshape(far, near, fine_rows, columns)
         for step in range(tp):
             pairs = []
@@ -534,8 +575,9 @@
                 held, ((at_far - number // near) % far, number % near, 0, 0), (1, 1, fine_rows, columns)
             )
             moved.append(lax.ppermute(part.reshape(fine_rows, columns), cell, pairs))
-        token_part = join(moved, [held[s] for held in received for s in order[:2]])
+        token_part = join(moved, arrivals[0] + [prepared])
     else:
+        prepared = prepare(filters, gate, cotangent, ctx_size, [send_pair([tokens])])
         row_parts = tokens.reshape(tp, fine_rows, columns)
         for step in range(tp):
             pairs = [(o * tp + t, destination(o, t, step)) for o in range(outer) for t in range(tp)]
@@ -544,8 +586,10 @@
         token_part = turned(moved, at_tp).reshape(outer, split, fine_rows, columns).swapaxes(1, 2)
         token_part = token_part.reshape(outer * fine_rows, split * columns)
 
-    prepared = prepare(filters, gate, cotangent, ctx_size, [token_part])
-    channel_rows = lax.all_to_all(prepared, ctx, split_axis=0, concat_axis=0, tiled=True)
+    channel_rows = lax.all_to_all(release(prepared, [token_part]), ctx, split_axis=0, concat_axis=0, tiled=True)
+    sent = token_part
+    while len(arrivals) < outer // 2:
+        sent = send_pair([sent, *arrivals[-1]])
     table = transform_table(length)
 
     pieces = [token_part] + [shifted(token_part, "far", f) for f in range(1, far)]
@@ -561,43 +605,42 @@
     places = jnp.stack(places).astype(jnp.int32)
     places = jnp.stack([places + back_inner[s] * tp for s in range(inner)])
 
-    grad_values, spectrum = correlate(table, rotation(length), channel_rows)
-    by_inner = grad_values.reshape(outer, inner, rows, channels)
-    grad_parts = [pick(by_inner, at_inner, 1)]
-    for i in range(1, inner):
-        grad_parts.append(shifted(pick(by_inner, (at_inner + i) % inner, 1), "inner", i))
     blocks = jnp.stack(back_inner)
     turn = at_outer // near * near if split == 1 else 0
     row_order = jnp.stack([(s + turn) % outer + at_outer * 0 for s in range(outer)])
     running = None
+    waits = [sent]
     for s in order:
         if running is not None:
             running = shifted(running, "outer", 1)
         held = [chunk[s] for chunk in received]
-        waits = [chunk[(s + 1) % outer] for chunk in received if s != 0]
-        if s == 1:
-            waits = waits + list(table)
+        running = product(pieces, in_weight, chunks[s], held, blocks, row_order, running, s == 0, waits)
+        waits = []
+        if s == outer - 2:
+            grad_values, spectrum = correlate(table, rotation(length), channel_rows, [running])
+            by_inner = grad_values.reshape(outer, inner, rows, channels)
+            grad_parts = [pick(by_inner, at_inner, 1)]
+            for i in range(1, inner):
+                grad_parts.append(shifted(pick(by_inner, (at_inner + i) % inner, 1), "inner", i))
+            waits = [spectrum]
         if s == outer - 1:
-            waits = waits + [spectrum]
-        if s == 0:
-            waits = waits + grad_parts
-        running = product(pieces, in_weight, chunks[s], held, blocks, row_order, running, s == 0, waits)
+            sources = [(at_far + f) % far * near + (at_near + n) % near for n in range(near) for f in range(far)]
+            arranged = arrange(
+                grad_parts, jnp.stack(back_inner), jnp.stack(sources), (outer, inner, far, near, halves, half_rows), [running]
+            )
+            gathered = [lax.all_gather(half, "outer", axis=0, tiled=False) for half in arranged]
+            waits = list(arranged)
     value_parts = [running[0]] + [shifted(running[i], "inner", i) for i in range(1, inner)]
-
-    sources = [(at_far + f) % far * near + (at_near + n) % near for n in range(near) for f in range(far)]
-    arranged = arrange(
-        grad_parts, jnp.stack(back_inner), jnp.stack(sources), (outer, inner, far, near, halves, half_rows), [running]
-    )
 
     convolved = convolve(table, spectrum, value_parts, places).reshape(ctx_size, rows, channels)
 
     sent_back = []
     waits = [convolved]
-    for half in arranged:
-        gathered = lax.all_gather(half, "outer", axis=0, tiled=False)
-        by_near = shares(gathered, in_weight, received, jnp.stack(chunks), near, waits)
+    for half in gathered:
+        by_near = shares(half, in_weight, received, jnp.stack(chunks), near, waits)
         total = by_near[0].astype(WIDE) + sum(shifted(by_near[n], "near", n).astype(WIDE) for n in range(1, near))
         total = total.astype(SHORT).reshape(inner, far, outer * half_rows, depth)
+        waits = [total]
         total = total[:, 0].astype(WIDE) + sum(shifted(total[:, f], "far", f).astype(WIDE) for f in range(1, far))
         total = total.astype(SHORT).reshape(inner, outer, half_rows, depth)
         if split == 1:
@@ -610,13 +653,12 @@
             pairs = [(destination(o, t, step), o * tp + t) for o in range(outer) for t in range(tp)]
             back.append(lax.ppermute(pick(total, (at_tp - step) % tp), cell, pairs))
         sent_back.append(back)
-        waits = back
     row_places = [(at_outer * split + at_tp % split + step) % tp for step in range(tp)]
     block_places = back_inner if split == 1 else [jnp.int32(b) for b in range(tile_blocks)]
     grad_tokens = assemble(sent_back, jnp.stack(row_places), jnp.stack(block_places), columns)
 
-    convolved = lax.all_to_all(convolved, ctx, split_axis=0, concat_axis=0, tiled=True)
-    gated_output, grad_gate = finish(convolved, gate, cotangent)
+    exchanged = lax.all_to_all(convolved, ctx, split_axis=0, concat_axis=0, tiled=True)
+    gated_output, grad_gate = finish(exchanged, gate, cotangent)
     return (gated_output, grad_gate, grad_tokens)
 
 

time: 403 us -> 369 us (0.916)
  starting transfers between devices: 86.5 us -> 46.1 us
  waiting for transfers between devices: 152 us -> 180 us
  other arithmetic: 20.4 us -> 6.4 us
  local copies, waits for them, and re-layouts: 32.9 us -> 20.4 us
  Pallas kernels: 94.8 us -> 101 us
    ppermute x17 -> x15, waiting for transfers between devices: 97.6 us -> 135 us  [shifted(): lax.ppermute(array, axis, [(at, (at + shift) % size) for at in range(size)])]
    ppermute x17 -> x15, starting transfers between devices: 50.5 us -> 17.5 us  [shifted(): lax.ppermute(array, axis, [(at, (at + shift) % size) for at in range(size)])]
    all_gather x2, waiting for transfers between devices: 34.2 us -> 20.4 us  [per_device(): lax.all_gather(half, 'outer', axis=0, tiled=False)]
    unnamed x56 -> x40, local copies, waits for them, and re-layouts: 24.2 us -> 13.3 us
    convert_element_type x1 -> x0, other arithmetic: 9.68 us -> none  [transform_table(): sin_part = (coarse_sin * fine_cos + coarse_cos * fine_sin).astype(SHORT)]
    ppermute x4, starting transfers between devices: 12.9 us -> 6.25 us  [per_device(): moved.append(lax.ppermute(part.reshape(fine_rows, columns), cell, pairs))]
    ppermute x8, waiting for transfers between devices: 6.43 us -> 11.7 us  [per_device(): back.append(lax.ppermute(pick(total, (at_tp - step) % tp), cell, pairs))]
    sin x2 -> x0, other arithmetic: 5.06 us -> none  [the longest x1 3.22 us: transform_table(): jnp.sin(coarse_angle)]
  transfers between devices with their start and end apart: 33 -> 31, of which waited for: 17 -> 19; matrix products, arithmetic and copies ran while one was open for 7% -> 4% of each run, Pallas kernels for 18% -> 22%
where the time goes in v2:
time: 369 us; the launch traced here: 368 us
  waiting for transfers between devices  180 us (49%)
  Pallas kernels  101 us (27%)
  starting transfers between devices  46.1 us (12%)
  local copies, waits for them, and re-layouts  20.4 us (6%)
  between operations  14.4 us (4%)
  other arithmetic  6.4 us (2%)
    ppermute x15, waiting for transfers between devices, shifted(): lax.ppermute(array, axis, [(at, (at + shift) % size) for at in range(size)])  135 us
    pallas_call x4, Pallas kernels, product(): pl.pallas_call(waiting(functools.partial(product_kernel, (inner, outer, l...  24 us
    all_gather x2, waiting for transfers between devices, per_device(): lax.all_gather(half, 'outer', axis=0, tiled=False)  20.4 us
    pallas_call x1, Pallas kernels, correlate(): pl.pallas_call(waiting(correlate_kernel, len(waits)), grid=(2, steps), in...  20.2 us
    pallas_call x1, Pallas kernels, convolve(): pl.pallas_call(functools.partial(convolve_kernel, len(parts)), grid_spec=...  17.6 us
    ppermute x15, starting transfers between devices, shifted(): lax.ppermute(array, axis, [(at, (at + shift) % size) for at in range(size)])  17.5 us
    pallas_call x2, Pallas kernels, shares(): pl.pallas_call(waiting(functools.partial(shares_kernel, (outer, inner, ne...  16.4 us
    unnamed x40, local copies, waits for them, and re-layouts  13.3 us
  transfers between devices with their start and end apart: 31, of which 19 were waited for; matrix products, arithmetic and copies ran while one was open for 4% of the time, Pallas kernels for 22%

profile of v2, /device:TPU:4, one launch (start us, length us, event | category | flops | bytes accessed | tf_op | source)
XLA Modules:
  0.0 368.0 jit_solution(760920018515161456)
XLA Ops:
  9.8 6.3 %shard_map.96.refs_0_ = bf16[1024,1024]{1,0:T(8,128)(2,1)} custom-call(s32[2]{0:T(128)S(1)} %pad_add_fusion.1.index_ref, bf16[128,2048]{1,0:T(8,128)(2,1)S(1)} %shard_map.94.refs_0_, bf16[128,2048]{1,0:T(8,128)(2,1)S(1)} %shard_map.95.refs_1_, bf16[1024,2048]{1,0:T(8,128)(2,1)} %refs_2_.10), custom_call_target="tpu_custom_call" | custom-call | tf_op jit(solution)/shard_map/pallas_call | solution.py:323
  18.1 13.0 %collective-permute-done.1 = bf16[128,2048]{1,0:T(8,128)(2,1)} collective-permute-done((bf16[128,2048]{1,0:T(8,128)(2,1)S(1)}, bf16[128,2048]{1,0:T(8,128)(2,1)}, u32[]{:S(2)}, u32[]{:S(2)}) %collective-permute-start.1) | collective-permute-done | bytes 524320 | tf_op jit(solution)/shard_map/ppermute | solution.py:508
  44.3 6.4 %collective-permute-done.3.refs_3_ = bf16[64,2048]{1,0:T(8,128)(2,1)S(1)} collective-permute-done((bf16[64,2048]{1,0:T(8,128)(2,1)S(1)}, bf16[64,2048]{1,0:T(8,128)(2,1)S(1)}, u32[]{:S(2)}, u32[]{:S(2)}) %collective-permute-start.3) | collective-permute-done | bytes 262176 | tf_op jit(solution)/shard_map/ppermute | solution.py:577
  50.7 6.0 %collective-permute-done.4.refs_4_ = bf16[64,2048]{1,0:T(8,128)(2,1)S(1)} collective-permute-done((bf16[64,2048]{1,0:T(8,128)(2,1)S(1)}, bf16[64,2048]{1,0:T(8,128)(2,1)S(1)}, u32[]{:S(2)}, u32[]{:S(2)}) %collective-permute-start.4) | collective-permute-done | bytes 262176 | tf_op jit(solution)/shard_map/ppermute | solution.py:577
  56.8 6.9 %collective-permute-done.refs_0_.refs_1_.refs_6_.refs_5_.refs_4_ = bf16[1024,1024]{1,0:T(8,128)(2,1)S(1)} collective-permute-done((bf16[1024,1024]{1,0:T(8,128)(2,1)}, bf16[1024,1024]{1,0:T(8,128)(2,1)S(1)}, u32[]{:S(2)}, u32[]{:S(2)}) %collective-permute-start) | collective-permute-done | bytes 2097184 | tf_op jit(solution)/shard_map/ppermute | solution.py:508
  65.2 5.8 %all-to-all-start = ((bf16[8,2,256,256]{3,2,1,0:T(8,128)(2,1)}), bf16[8,2,256,256]{3,2,1,0:T(8,128)(2,1)}, u32[]{:S(2)}, u32[]{:S(2)}) async-start(bf16[8,2,256,256]{3,2,1,0:T(8,128)(2,1)} %copy-done.3), calls=%async_computation | async-start | bytes 4194304 | tf_op jit(solution)/shard_map/all_to_all | solution.py:589
  71.6 23.3 %collective-permute-done.6.refs_2_.refs_1_.refs_3_ = bf16[256,2048]{1,0:T(8,128)(2,1)} collective-permute-done((bf16[256,2048]{1,0:T(8,128)(2,1)S(1)}, bf16[256,2048]{1,0:T(8,128)(2,1)}, u32[]{:S(2)}, u32[]{:S(2)}) %collective-permute-start.6) | collective-permute-done | bytes 1048608 | tf_op jit(solution)/shard_map/ppermute | solution.py:508
  95.2 4.7 %shard_map.99.refs_0_ = bf16[1024,1024]{1,0:T(8,128)(2,1)S(1)} custom-call(s32[2]{0:T(128)S(1)} %pad_add_fusion.2.index_ref, bf16[256,2048]{1,0:T(8,128)(2,1)S(1)} %shard_map.98.refs_0_.refs_1_.refs_2_, bf16[1024,1024]{1,0:T(8,128)(2,1)S(1)} %collective-permute-done.refs_0_.refs_1_.refs_6_.refs_5_.refs_4_, bf16[1024,2048]{1,0:T(8,128)(2,1)} %refs_2_.10), custom_call_target="tpu_custom_call" | custom-call | tf_op jit(solution)/shard_map/pallas_call | solution.py:323
  101.2 6.2 %shard_map.100 = bf16[1024,512]{1,0:T(8,128)(2,1)} custom-call(s32[8]{0:T(128)S(1)} %concatenate.38.index_ref, bf16[1024,1024]{1,0:T(8,128)(2,1)} %copy-done.4, bf16[256,2048]{1,0:T(8,128)(2,1)S(1)} %shard_map.98.refs_0_.refs_1_.refs_2_, bf16[256,2048]{1,0:T(8,128)(2,1)} %collective-permute-done.6.refs_2_.refs_1_.refs_3_, ...), custom_call_target="tpu_custom_call" | custom-call | tf_op jit(solution)/shard_map/pallas_call | solution.py:425
  110.6 24.6 %collective-permute-done.9.refs_6_ = bf16[1024,512]{1,0:T(8,128)(2,1)} collective-permute-done((bf16[1024,512]{1,0:T(8,128)(2,1)}, bf16[1024,512]{1,0:T(8,128)(2,1)}, u32[]{:S(2)}, u32[]{:S(2)}) %collective-permute-start.9) | collective-permute-done | bytes 1048608 | tf_op jit(solution)/shard_map/ppermute | solution.py:508
  135.2 6.5 %shard_map.101.refs_0_ = bf16[1024,512]{1,0:T(8,128)(2,1)} custom-call(s32[8]{0:T(128)S(1)} %concatenate.37.index_ref, bf16[256,2048]{1,0:T(8,128)(2,1)S(1)} %shard_map.98.refs_0_.refs_1_.refs_2_, bf16[256,2048]{1,0:T(8,128)(2,1)} %collective-permute-done.6.refs_2_.refs_1_.refs_3_, bf16[256,2048]{1,0:T(8,128)(2,1)} %collective-permute-done.7.refs_3_.refs_2_.refs_4_, ...), custom_call_target="tpu_custom_call" | custom-call | tf_op jit(solution)/shard_map/pallas_call | solution.py:425
  149.1 20.2 %shard_map.103 = (bf16[2048,256]{1,0:T(8,128)(2,1)S(1)}, bf16[2,2048,256]{2,1,0:T(8,128)(2,1)S(1)}) custom-call(s32[1]{0:T(128)} %constant.361.clone.1.index_ref, bf16[1024,512]{1,0:T(8,128)(2,1)} %shard_map.101.refs_0_, bf16[2048,2048]{1,0:T(8,128)(2,1)} %constant.364.clone.refs_1_.cos_ref, bf16[2048,2048]{1,0:T(8,128)(2,1)} %constant.365.clone.refs_2_.sin_ref, ...), custom_call_target="tpu_custom_call" | custom-call | tf_op jit(solution)/shard_map/pallas_call | solution.py:120
  173.3 5.7 %shard_map.104.refs_0_ = bf16[1024,512]{1,0:T(8,128)(2,1)S(1)} custom-call(s32[8]{0:T(128)S(1)} %concatenate.41.index_ref, bf16[2,2048,256]{2,1,0:T(8,128)(2,1)} %copy-done.6, bf16[256,2048]{1,0:T(8,128)(2,1)S(1)} %shard_map.98.refs_0_.refs_1_.refs_2_, bf16[256,2048]{1,0:T(8,128)(2,1)} %collective-permute-done.6.refs_2_.refs_1_.refs_3_, ...), custom_call_target="tpu_custom_call" | custom-call | tf_op jit(solution)/shard_map/pallas_call | solution.py:425
  179.0 6.7 %collective-permute-done.12.refs_2_ = bf16[4,256,256]{2,1,0:T(8,128)(2,1)} collective-permute-done((bf16[4,256,256]{2,1,0:T(8,128)(2,1)}, bf16[4,256,256]{2,1,0:T(8,128)(2,1)}, u32[]{:S(2)}, u32[]{:S(2)}) %collective-permute-start.12) | collective-permute-done | bytes 524320 | tf_op jit(solution)/shard_map/ppermute | solution.py:508
  190.7 38.4 %collective-permute-done.13.refs_8_ = bf16[1024,512]{1,0:T(8,128)(2,1)} collective-permute-done((bf16[1024,512]{1,0:T(8,128)(2,1)S(1)}, bf16[1024,512]{1,0:T(8,128)(2,1)}, u32[]{:S(2)}, u32[]{:S(2)}) %collective-permute-start.13) | collective-permute-done | bytes 1048608 | tf_op jit(solution)/shard_map/ppermute | solution.py:508
  229.1 5.7 %shard_map.106 = bf16[2,1024,256]{2,1,0:T(8,128)(2,1)S(1)} custom-call(s32[8]{0:T(128)S(1)} %concatenate.39.index_ref, bf16[512,512]{1,0:T(8,128)(2,1)} %get-tuple-element.15.refs_0_, bf16[512,512]{1,0:T(8,128)(2,1)} %get-tuple-element.16.refs_1_, bf16[256,2048]{1,0:T(8,128)(2,1)S(1)} %shard_map.98.refs_0_.refs_1_.refs_2_, ...), custom_call_target="tpu_custom_call" | custom-call | tf_op jit(solution)/shard_map/pallas_call | solution.py:425
  237.0 8.1 %collective-permute-done.14.refs_1_ = bf16[1024,256]{1,0:T(8,128)(2,1)S(1)} collective-permute-done((bf16[1024,256]{1,0:T(8,128)(2,1)}, bf16[1024,256]{1,0:T(8,128)(2,1)S(1)}, u32[]{:S(2)}, u32[]{:S(2)}) %collective-permute-start.14) | collective-permute-done | bytes 524320 | tf_op jit(solution)/shard_map/ppermute | solution.py:508
  245.0 17.6 %shard_map.107 = bf16[2048,256]{1,0:T(8,128)(2,1)} custom-call(s32[2,16]{1,0:T(2,128)S(1)} %pad_add_fusion.places_ref, bf16[2048,2048]{1,0:T(8,128)(2,1)} %constant.364.clone.refs_1_.cos_ref, bf16[2048,2048]{1,0:T(8,128)(2,1)} %constant.365.clone.refs_2_.sin_ref, bf16[2,2048,256]{2,1,0:T(8,128)(2,1)S(1)} %copy-done.7, ...), custom_call_target="tpu_custom_call" | custom-call | tf_op jit(solution)/shard_map/pallas_call | solution.py:179
  264.2 7.8 %shard_map.109 = (bf16[2,256,1024]{2,1,0:T(8,128)(2,1)S(1)}, bf16[2,256,1024]{2,1,0:T(8,128)(2,1)S(1)}) custom-call(s32[4]{0:T(128)S(1)} %pad_add_fusion.3.index_ref, bf16[8,256,256]{2,1,0:T(8,128)(2,1)} %bitcast.43.refs_0_, bf16[4,512,512]{2,1,0:T(8,128)(2,1)S(1)} %bitcast.114, bf16[1024,2048]{1,0:T(8,128)(2,1)} %refs_2_.10, ...), custom_call_target="tpu_custom_call" | custom-call | tf_op jit(solution)/shard_map/pallas_call | solution.py:488
  275.2 20.4 %all-gather.7.cloned.1.call-done = bf16[2048,512]{1,0:T(8,128)(2,1)} async-done(((bf16[512,512]{1,0:T(8,128)(2,1)}), bf16[2048,512]{1,0:T(8,128)(2,1)}) %all-gather.7.cloned.1.call-update) | async-done | bytes 2097168 | tf_op jit(solution)/shard_map/all_gather | solution.py:631
  297.1 8.5 %shard_map.110 = (bf16[2,256,1024]{2,1,0:T(8,128)(2,1)S(1)}, bf16[2,256,1024]{2,1,0:T(8,128)(2,1)}) custom-call(s32[4]{0:T(128)S(1)} %pad_add_fusion.3.index_ref, bf16[2,2,128,1024]{3,2,1,0:T(8,128)(2,1)S(1)} %bitcast.109, bf16[4,512,512]{2,1,0:T(8,128)(2,1)S(1)} %bitcast.113, bf16[1024,2048]{1,0:T(8,128)(2,1)} %refs_2_.10, ...), custom_call_target="tpu_custom_call" | custom-call | tf_op jit(solution)/shard_map/pallas_call | solution.py:488
  315.6 9.6 %collective-permute-done.16 = bf16[2,128,1024]{2,1,0:T(8,128)(2,1)} collective-permute-done((bf16[2,128,1024]{2,1,0:T(8,128)(2,1)}, bf16[2,128,1024]{2,1,0:T(8,128)(2,1)}, u32[]{:S(2)}, u32[]{:S(2)}) %collective-permute-start.16) | collective-permute-done | bytes 524320 | tf_op jit(solution)/shard_map/ppermute | solution.py:508
  327.1 4.8 %collective-permute-start.17 = (bf16[2,32,1024]{2,1,0:T(8,128)(2,1)S(1)}, bf16[2,32,1024]{2,1,0:T(8,128)(2,1)S(1)}, u32[]{:S(2)}, u32[]{:S(2)}) collective-permute-start(bf16[2,32,1024]{2,1,0:T(8,128)(2,1)S(1)} %get-tuple-element.38), channel_id=1, source_target_pairs={{0,0},{8,1},{16,2},{24,3},{1,8},{9,9},{17,10},{25,11},{2,16},{10,1... | collective-permute-start | bytes 393224 | tf_op jit(solution)/shard_map/ppermute | solution.py:654
  344.8 4.8 %collective-permute-done.18.refs_1_ = bf16[2,32,1024]{2,1,0:T(8,128)(2,1)S(1)} collective-permute-done((bf16[2,32,1024]{2,1,0:T(8,128)(2,1)S(1)}, bf16[2,32,1024]{2,1,0:T(8,128)(2,1)S(1)}, u32[]{:S(2)}, u32[]{:S(2)}) %collective-permute-start.18) | collective-permute-done | bytes 131104 | tf_op jit(solution)/shard_map/ppermute | solution.py:654
  (124 shorter events, 85.7 us)
Async XLA Ops:
  16.1 47.6 %collective-permute-start = (bf16[1024,1024]{1,0:T(8,128)(2,1)}, bf16[1024,1024]{1,0:T(8,128)(2,1)S(1)}, u32[]{:S(2)}, u32[]{:S(2)}) collective-permute-start(bf16[1024,1024]{1,0:T(8,128)(2,1)} %shard_map.96.refs_0_), channel_id=1, source_target_pairs={{0,4},{4,0},{1,5},{5,1},{2,6},{6,2},{3,7},{7,3},{8,12},{12,8},{9,1... | collective-permute-start | bytes 6291464 | tf_op jit(solution)/shard_map/ppermute | solution.py:508
  17.6 13.5 %collective-permute-start.1 = (bf16[128,2048]{1,0:T(8,128)(2,1)S(1)}, bf16[128,2048]{1,0:T(8,128)(2,1)}, u32[]{:S(2)}, u32[]{:S(2)}) collective-permute-start(bf16[128,2048]{1,0:T(8,128)(2,1)S(1)} %shard_map.95.refs_1_), channel_id=1, source_target_pairs={{0,2},{2,0},{1,3},{3,1},{4,6},{6,4},{5,7},{7,5},{8,10},{10,8},{9,1... | collective-permute-start | bytes 1572872 | tf_op jit(solution)/shard_map/ppermute | solution.py:508
  33.2 17.5 %collective-permute-start.3 = (bf16[64,2048]{1,0:T(8,128)(2,1)S(1)}, bf16[64,2048]{1,0:T(8,128)(2,1)S(1)}, u32[]{:S(2)}, u32[]{:S(2)}) collective-permute-start(bf16[64,2048]{1,0:T(8,128)(2,1)S(1)} %get-tuple-element.29), channel_id=1, source_target_pairs={{0,1},{1,9},{2,3},{3,11},{8,16},{9,24},{10,18},{11,26},{16,17},{17... | collective-permute-start | bytes 786440 | tf_op jit(solution)/shard_map/ppermute | solution.py:577
  36.2 20.6 %collective-permute-start.4 = (bf16[64,2048]{1,0:T(8,128)(2,1)S(1)}, bf16[64,2048]{1,0:T(8,128)(2,1)S(1)}, u32[]{:S(2)}, u32[]{:S(2)}) collective-permute-start(bf16[64,2048]{1,0:T(8,128)(2,1)S(1)} %get-tuple-element.30), channel_id=1, source_target_pairs={{0,16},{1,24},{2,18},{3,26},{8,17},{9,25},{10,19},{11,27},{16,0},{... | collective-permute-start | bytes 786440 | tf_op jit(solution)/shard_map/ppermute | solution.py:577
  38.7 18.0 %collective-permute-start.5 = (bf16[64,2048]{1,0:T(8,128)(2,1)S(1)}, bf16[64,2048]{1,0:T(8,128)(2,1)S(1)}, u32[]{:S(2)}, u32[]{:S(2)}) collective-permute-start(bf16[64,2048]{1,0:T(8,128)(2,1)S(1)} %get-tuple-element.27), channel_id=1, source_target_pairs={{0,17},{1,25},{2,19},{3,27},{8,0},{9,8},{10,2},{11,10},{16,1},{17,... | collective-permute-start | bytes 786440 | tf_op jit(solution)/shard_map/ppermute | solution.py:577
  65.2 82.7 %all-to-all-start = ((bf16[8,2,256,256]{3,2,1,0:T(8,128)(2,1)}), bf16[8,2,256,256]{3,2,1,0:T(8,128)(2,1)}, u32[]{:S(2)}, u32[]{:S(2)}) async-start(bf16[8,2,256,256]{3,2,1,0:T(8,128)(2,1)} %copy-done.3), calls=%async_computation | async-start | bytes 4194304 | tf_op jit(solution)/shard_map/all_to_all | solution.py:589
  71.0 191.6 %all-gather.5.cloned.1.call-start = ((), (), s32[]{:S(2)}) async-start(), calls=%async_computation.2 | async-start | bytes 2621440 | tf_op jit(solution)/shard_map/all_gather | solution.py:631
  71.1 23.9 %collective-permute-start.6 = (bf16[256,2048]{1,0:T(8,128)(2,1)S(1)}, bf16[256,2048]{1,0:T(8,128)(2,1)}, u32[]{:S(2)}, u32[]{:S(2)}) collective-permute-start(bf16[256,2048]{1,0:T(8,128)(2,1)S(1)} %shard_map.98.refs_0_.refs_1_.refs_2_), channel_id=1, source_target_pairs={{0,2},{2,0},{1,3},{3,1},{4,6},{6,4},{5,7},{7,5},{8,10},{10,8},{9,1... | collective-permute-start | bytes 3145736 | tf_op jit(solution)/shard_map/ppermute | solution.py:508
  71.6 29.6 %collective-permute-start.7 = (bf16[256,2048]{1,0:T(8,128)(2,1)S(1)}, bf16[256,2048]{1,0:T(8,128)(2,1)}, u32[]{:S(2)}, u32[]{:S(2)}) collective-permute-start(bf16[256,2048]{1,0:T(8,128)(2,1)S(1)} %shard_map.98.refs_0_.refs_1_.refs_2_), channel_id=1, source_target_pairs={{0,1},{1,0},{2,3},{3,2},{4,5},{5,4},{6,7},{7,6},{8,9},{9,8},{10,11... | collective-permute-start | bytes 3145736 | tf_op jit(solution)/shard_map/ppermute | solution.py:508
  107.4 27.8 %collective-permute-start.9 = (bf16[1024,512]{1,0:T(8,128)(2,1)}, bf16[1024,512]{1,0:T(8,128)(2,1)}, u32[]{:S(2)}, u32[]{:S(2)}) collective-permute-start(bf16[1024,512]{1,0:T(8,128)(2,1)} %shard_map.100), channel_id=1, source_target_pairs={{0,8},{8,16},{16,24},{24,0},{1,9},{9,17},{17,25},{25,1},{2,10},{10... | collective-permute-start | bytes 3145736 | tf_op jit(solution)/shard_map/ppermute | solution.py:508
  109.0 64.2 %collective-permute-start.10 = (bf16[1024,1024]{1,0:T(8,128)(2,1)S(1)}, bf16[1024,1024]{1,0:T(8,128)(2,1)}, u32[]{:S(2)}, u32[]{:S(2)}) collective-permute-start(bf16[1024,1024]{1,0:T(8,128)(2,1)S(1)} %copy-done.5), channel_id=1, source_target_pairs={{0,4},{4,0},{1,5},{5,1},{2,6},{6,2},{3,7},{7,3},{8,12},{12,8},{9,1... | collective-permute-start | bytes 6291464 | tf_op jit(solution)/shard_map/ppermute | solution.py:508
  141.6 31.6 %collective-permute-start.11 = (bf16[1024,512]{1,0:T(8,128)(2,1)}, bf16[1024,512]{1,0:T(8,128)(2,1)}, u32[]{:S(2)}, u32[]{:S(2)}) collective-permute-start(bf16[1024,512]{1,0:T(8,128)(2,1)} %shard_map.101.refs_0_), channel_id=1, source_target_pairs={{0,8},{8,16},{16,24},{24,0},{1,9},{9,17},{17,25},{25,1},{2,10},{10... | collective-permute-start | bytes 3145736 | tf_op jit(solution)/shard_map/ppermute | solution.py:508
  171.8 13.9 %collective-permute-start.12 = (bf16[4,256,256]{2,1,0:T(8,128)(2,1)}, bf16[4,256,256]{2,1,0:T(8,128)(2,1)}, u32[]{:S(2)}, u32[]{:S(2)}) collective-permute-start(bf16[4,256,256]{2,1,0:T(8,128)(2,1)} %get-tuple-element.25), channel_id=1, source_target_pairs={{0,4},{4,0},{1,5},{5,1},{2,6},{6,2},{3,7},{7,3},{8,12},{12,8},{9,1... | collective-permute-start | bytes 1572872 | tf_op jit(solution)/shard_map/ppermute | solution.py:508
  187.8 107.8 %all-gather.7.cloned.1.call-start = ((), (), s32[]{:S(2)}) async-start(), calls=%async_computation.3 | async-start | bytes 2621440 | tf_op jit(solution)/shard_map/all_gather | solution.py:631
  187.9 41.2 %collective-permute-start.13 = (bf16[1024,512]{1,0:T(8,128)(2,1)S(1)}, bf16[1024,512]{1,0:T(8,128)(2,1)}, u32[]{:S(2)}, u32[]{:S(2)}) collective-permute-start(bf16[1024,512]{1,0:T(8,128)(2,1)S(1)} %shard_map.104.refs_0_), channel_id=1, source_target_pairs={{0,8},{8,16},{16,24},{24,0},{1,9},{9,17},{17,25},{25,1},{2,10},{10... | collective-permute-start | bytes 3145736 | tf_op jit(solution)/shard_map/ppermute | solution.py:508
  305.7 43.9 %all-to-all-start.1 = ((bf16[8,256,256]{2,1,0:T(8,128)(2,1)}), bf16[8,256,256]{2,1,0:T(8,128)(2,1)S(1)}, u32[]{:S(2)}, u32[]{:S(2)}) async-start(bf16[8,256,256]{2,1,0:T(8,128)(2,1)} %bitcast.43.refs_0_), calls=%async_computation.1 | async-start | bytes 2097152 | tf_op jit(solution)/shard_map/all_to_all | solution.py:660
  310.1 15.0 %collective-permute-start.16 = (bf16[2,128,1024]{2,1,0:T(8,128)(2,1)}, bf16[2,128,1024]{2,1,0:T(8,128)(2,1)}, u32[]{:S(2)}, u32[]{:S(2)}) collective-permute-start(bf16[2,128,1024]{2,1,0:T(8,128)(2,1)} %slice_bitcast_fusion.2), channel_id=1, source_target_pairs={{0,2},{2,0},{1,3},{3,1},{4,6},{6,4},{5,7},{7,5},{8,10},{10,8},{9,1... | collective-permute-start | bytes 1572872 | tf_op jit(solution)/shard_map/ppermute | solution.py:508
  314.1 23.3 %collective-permute-start.22 = (bf16[2,128,1024]{2,1,0:T(8,128)(2,1)}, bf16[2,128,1024]{2,1,0:T(8,128)(2,1)}, u32[]{:S(2)}, u32[]{:S(2)}) collective-permute-start(bf16[2,128,1024]{2,1,0:T(8,128)(2,1)} %slice_bitcast_fusion), channel_id=1, source_target_pairs={{0,2},{2,0},{1,3},{3,1},{4,6},{6,4},{5,7},{7,5},{8,10},{10,8},{9,1... | collective-permute-start | bytes 1572872 | tf_op jit(solution)/shard_map/ppermute | solution.py:508
  327.1 17.7 %collective-permute-start.17 = (bf16[2,32,1024]{2,1,0:T(8,128)(2,1)S(1)}, bf16[2,32,1024]{2,1,0:T(8,128)(2,1)S(1)}, u32[]{:S(2)}, u32[]{:S(2)}) collective-permute-start(bf16[2,32,1024]{2,1,0:T(8,128)(2,1)S(1)} %get-tuple-element.38), channel_id=1, source_target_pairs={{0,0},{8,1},{16,2},{24,3},{1,8},{9,9},{17,10},{25,11},{2,16},{10,1... | collective-permute-start | bytes 393224 | tf_op jit(solution)/shard_map/ppermute | solution.py:654
  331.8 17.7 %collective-permute-start.18 = (bf16[2,32,1024]{2,1,0:T(8,128)(2,1)S(1)}, bf16[2,32,1024]{2,1,0:T(8,128)(2,1)S(1)}, u32[]{:S(2)}, u32[]{:S(2)}) collective-permute-start(bf16[2,32,1024]{2,1,0:T(8,128)(2,1)S(1)} %get-tuple-element.37), channel_id=1, source_target_pairs={{1,0},{9,1},{17,2},{25,3},{2,8},{10,9},{18,10},{26,11},{3,16},{11,... | collective-permute-start | bytes 393224 | tf_op jit(solution)/shard_map/ppermute | solution.py:654
  331.9 17.6 %collective-permute-start.19 = (bf16[2,32,1024]{2,1,0:T(8,128)(2,1)S(1)}, bf16[2,32,1024]{2,1,0:T(8,128)(2,1)S(1)}, u32[]{:S(2)}, u32[]{:S(2)}) collective-permute-start(bf16[2,32,1024]{2,1,0:T(8,128)(2,1)S(1)} %get-tuple-element.36), channel_id=1, source_target_pairs={{2,0},{10,1},{18,2},{26,3},{3,8},{11,9},{19,10},{27,11},{0,16},{8,... | collective-permute-start | bytes 393224 | tf_op jit(solution)/shard_map/ppermute | solution.py:654
  333.4 19.5 %collective-permute-start.20 = (bf16[2,32,1024]{2,1,0:T(8,128)(2,1)}, bf16[2,32,1024]{2,1,0:T(8,128)(2,1)}, u32[]{:S(2)}, u32[]{:S(2)}) collective-permute-start(bf16[2,32,1024]{2,1,0:T(8,128)(2,1)} %get-tuple-element.35), channel_id=1, source_target_pairs={{3,0},{11,1},{19,2},{27,3},{0,8},{8,9},{16,10},{24,11},{1,16},{9,1... | collective-permute-start | bytes 393224 | tf_op jit(solution)/shard_map/ppermute | solution.py:654
  339.4 16.6 %collective-permute-start.23 = (bf16[2,32,1024]{2,1,0:T(8,128)(2,1)}, bf16[2,32,1024]{2,1,0:T(8,128)(2,1)}, u32[]{:S(2)}, u32[]{:S(2)}) collective-permute-start(bf16[2,32,1024]{2,1,0:T(8,128)(2,1)} %get-tuple-element.34), channel_id=1, source_target_pairs={{0,0},{8,1},{16,2},{24,3},{1,8},{9,9},{17,10},{25,11},{2,16},{10,1... | collective-permute-start | bytes 393224 | tf_op jit(solution)/shard_map/ppermute | solution.py:654
  344.7 13.3 %collective-permute-start.24 = (bf16[2,32,1024]{2,1,0:T(8,128)(2,1)}, bf16[2,32,1024]{2,1,0:T(8,128)(2,1)}, u32[]{:S(2)}, u32[]{:S(2)}) collective-permute-start(bf16[2,32,1024]{2,1,0:T(8,128)(2,1)} %get-tuple-element.33), channel_id=1, source_target_pairs={{1,0},{9,1},{17,2},{25,3},{2,8},{10,9},{18,10},{26,11},{3,16},{11,... | collective-permute-start | bytes 393224 | tf_op jit(solution)/shard_map/ppermute | solution.py:654
  (27 other events, 258.4 us)
Sparse Core Ops, SparseCore 0:
  187.9 60.1 all-gather.4
  250.3 45.2 all-gather.6

commit v3 on v2

--- a/solution.py
+++ b/solution.py
@@ -171,17 +171,18 @@
         out_ref[...] = (total * (1.0 / length)).astype(out_ref.dtype)
 
 
-def convolve(table, spectrum, parts, places):
+def convolve(table, spectrum, parts, places, waits):
     length, channels = spectrum.shape[1:]
     block = table_block(length)
     steps = length // block
     table_spec = pl.BlockSpec((block, length), lambda p, s, _: (s, 0))
     return pl.pallas_call(
-        functools.partial(convolve_kernel, len(parts)),
+        waiting(functools.partial(convolve_kernel, len(parts)), len(waits)),
         grid_spec=pltpu.PrefetchScalarGridSpec(
             num_scalar_prefetch=1,
             grid=(2, steps),
             in_specs=[
+                *[ANYWHERE] * len(waits),
                 table_spec,
                 table_spec,
                 pl.BlockSpec((2, block, channels), lambda p, s, _: (0, s + p * (steps - 1 - s), 0)),
@@ -193,7 +194,7 @@
         out_shape=jax.ShapeDtypeStruct((length, channels), SHORT),
         compiler_params=kernel_params(2),
         cost_estimate=NO_COST,
-    )(places, table[0], table[1], spectrum, *parts)
+    )(places, *waits, table[0], table[1], spectrum, *parts)
 
 
 def prepare_kernel(index_ref, filters_ref, gate_ref, cotangent_ref, out_ref):
@@ -317,7 +318,7 @@
 def chunks_of(array, indices, count, waits=()):
     rows, width = array.shape
     chunk = width // count
-    block = min(rows, 256)
+    block = min(rows, 1024)
     if chunk % 128:
         return jnp.concatenate([lax.dynamic_slice_in_dim(array, i * chunk, chunk, 1) for i in indices], axis=1)
     return pl.pallas_call(
@@ -334,25 +335,6 @@
     )(jnp.stack(indices).astype(jnp.int32), *waits, array)
 
 
-def row_part(array, index, count, waits):
-    rows, width = array.shape
-    size = rows // count
-    if size % 16 or width % 128:
-        return lax.dynamic_slice_in_dim(array, index * size, size, 0)
-    return pl.pallas_call(
-        waiting(chunk_kernel, len(waits)),
-        grid_spec=pltpu.PrefetchScalarGridSpec(
-            num_scalar_prefetch=1,
-            grid=(1,),
-            in_specs=[ANYWHERE] * len(waits) + [pl.BlockSpec((size, width), lambda r, index: (index[0], 0))],
-            out_specs=pl.BlockSpec((size, width), lambda r, _: (0, 0)),
-        ),
-        out_shape=jax.ShapeDtypeStruct((size, width), array.dtype),
-        compiler_params=kernel_params(1),
-        cost_estimate=NO_COST,
-    )(index[None].astype(jnp.int32), *waits, array)
-
-
 def join_kernel(index_ref, *refs):
     size = refs[0].shape[0]
     for p, ref in enumerate(refs[:-1]):
@@ -378,14 +360,21 @@
 
 def product_kernel(dims, index_ref, *refs):
     inner, outer, pieces, depth, add = dims
-    token_refs, weight_refs, out_ref = refs[:pieces], refs[pieces : pieces + inner], refs[-1]
+    token_refs, weight_refs, (out_ref, joined_ref) = refs[:pieces], refs[pieces : pieces + inner], refs[-2:]
     size = token_refs[0].shape[0] // outer
-    parts = [aligned(index_ref[2 + inner + s], size) for s in range(outer)]
-    total = refs[-2][...].astype(WIDE) if add else 0.0
+
+    @pl.when(pl.program_id(0) == 0)
+    def _():
+        for p in range(pieces):
+            for o in range(outer):
+                rows = aligned(index_ref[2 + inner + o], size)
+                place = (p * outer + o) * size
+                joined_ref[place : place + size] = token_refs[p][rows]
+
+    total = refs[-3][...].astype(WIDE) if add else 0.0
     for i in range(inner):
         columns = aligned(index_ref[2 + i], depth)
-        tokens = jnp.concatenate([ref[rows, columns] for ref in token_refs for rows in parts], axis=0)
-        total = total + wide_dot(tokens, weight_refs[i][...])
+        total = total + wide_dot(joined_ref[:, columns], weight_refs[i][...])
     out_ref[...] = total.astype(SHORT).reshape(out_ref.shape)
 
 
@@ -437,6 +426,7 @@
             ]
             + ([] if running is None else [pl.BlockSpec((rows, channels), lambda g, _: (0, g))]),
             out_specs=out_spec,
+            scratch_shapes=[pltpu.VMEM((rows, whole_depth), SHORT)],
         ),
         out_shape=jax.ShapeDtypeStruct(out_shape, SHORT),
         compiler_params=kernel_params(1),
@@ -547,19 +537,19 @@
     received = [[None] * outer for _ in range(1, inner)]
     arrivals = []
 
-    def send_pair(waits):
-        pair = order[2 * len(arrivals) : 2 * len(arrivals) + 2]
-        sent = chunks_of(in_weight, [chunks[s] for s in pair], outer, waits)
+    def send_chunks(some, waits):
+        sent = chunks_of(in_weight, [chunks[s] for s in some], outer, waits)
         arrivals.append([shifted(sent, "inner", i) for i in range(1, inner)])
         for i in range(1, inner):
-            for at, s in enumerate(pair):
+            for at, s in enumerate(some):
                 received[i - 1][s] = (arrivals[-1][i - 1], at)
         return sent
 
     moved = []
     if split == 1:
-        by_far = [row_part(tokens, (at_far + f) % far, far, []) for f in range(far)]
-        sent = send_pair(by_far)
+        by_far = tokens.reshape(far, near * fine_rows, columns)
+        by_far = [pick(by_far, (at_far + f) % far) for f in range(far)]
+        sent = send_chunks(order[:2], by_far[1:])
         prepared = prepare(filters, gate, cotangent, ctx_size, [sent])
         held = [by_far[0]] + [shifted(by_far[f], "far", f) for f in range(1, far)]
         held = jnp.stack(held).reshape(far, near, fine_rows, columns)
@@ -575,9 +565,10 @@
                 held, ((at_far - number // near) % far, number % near, 0, 0), (1, 1, fine_rows, columns)
             )
             moved.append(lax.ppermute(part.reshape(fine_rows, columns), cell, pairs))
-        token_part = join(moved, arrivals[0] + [prepared])
+        token_part = join(moved, [prepared, *arrivals[0]])
     else:
-        prepared = prepare(filters, gate, cotangent, ctx_size, [send_pair([tokens])])
+        sent = send_chunks(order[:2], [])
+        prepared = prepare(filters, gate, cotangent, ctx_size, [sent])
         row_parts = tokens.reshape(tp, fine_rows, columns)
         for step in range(tp):
             pairs = [(o * tp + t, destination(o, t, step)) for o in range(outer) for t in range(tp)]
@@ -587,9 +578,7 @@
         token_part = token_part.reshape(outer * fine_rows, split * columns)
 
     channel_rows = lax.all_to_all(release(prepared, [token_part]), ctx, split_axis=0, concat_axis=0, tiled=True)
-    sent = token_part
-    while len(arrivals) < outer // 2:
-        sent = send_pair([sent, *arrivals[-1]])
+    sent = send_chunks(order[2:], [token_part, *arrivals[0]])
     table = transform_table(length)
 
     pieces = [token_part] + [shifted(token_part, "far", f) for f in range(1, far)]
@@ -632,17 +621,20 @@
             waits = list(arranged)
     value_parts = [running[0]] + [shifted(running[i], "inner", i) for i in range(1, inner)]
 
-    convolved = convolve(table, spectrum, value_parts, places).reshape(ctx_size, rows, channels)
-
     sent_back = []
-    waits = [convolved]
-    for half in gathered:
+    waits = [running]
+    for at, half in enumerate(gathered):
         by_near = shares(half, in_weight, received, jnp.stack(chunks), near, waits)
         total = by_near[0].astype(WIDE) + sum(shifted(by_near[n], "near", n).astype(WIDE) for n in range(1, near))
         total = total.astype(SHORT).reshape(inner, far, outer * half_rows, depth)
-        waits = [total]
-        total = total[:, 0].astype(WIDE) + sum(shifted(total[:, f], "far", f).astype(WIDE) for f in range(1, far))
+        if at == 0:
+            convolved = convolve(table, spectrum, value_parts, places, [total])
+            convolved = convolved.reshape(ctx_size, rows, channels)
+            exchanged = lax.all_to_all(convolved, ctx, split_axis=0, concat_axis=0, tiled=True)
+        others = [shifted(total[:, f], "far", f) for f in range(1, far)]
+        total = total[:, 0].astype(WIDE) + sum(other.astype(WIDE) for other in others)
         total = total.astype(SHORT).reshape(inner, outer, half_rows, depth)
+        waits = [convolved, total]
         if split == 1:
             total = total.swapaxes(0, 1)
         else:
@@ -657,7 +649,6 @@
     block_places = back_inner if split == 1 else [jnp.int32(b) for b in range(tile_blocks)]
     grad_tokens = assemble(sent_back, jnp.stack(row_places), jnp.stack(block_places), columns)
 
-    exchanged = lax.all_to_all(convolved, ctx, split_axis=0, concat_axis=0, tiled=True)
     gated_output, grad_gate = finish(exchanged, gate, cotangent)
     return (gated_output, grad_gate, grad_tokens)
 

time: 369 us -> 371 us (level)
    ppermute x8, waiting for transfers between devices: 11.7 us -> 20.7 us  [per_device(): back.append(lax.ppermute(pick(total, (at_tp - step) % tp), cell, pairs))]
    all_gather x2, waiting for transfers between devices: 20.4 us -> 14.7 us  [per_device(): lax.all_gather(half, 'outer', axis=0, tiled=False)]
    pallas_call x2, Pallas kernels: 11 us -> 5.52 us  [chunks_of(): pl.pallas_call(waiting(chunk_kernel, len(waits)), grid_spec=pltpu.Prefetc...]
    ppermute x15, waiting for transfers between devices: 135 us -> 131 us  [shifted(): lax.ppermute(array, axis, [(at, (at + shift) % size) for at in range(size)])]
    unnamed x40 -> x32, local copies, waits for them, and re-layouts: 13.3 us -> 10.9 us
    pallas_call x3 -> x1, Pallas kernels: 17.6 us -> 17.6 us  [convolve(): pl.pallas_call(waiting(functools.partial(convolve_kernel, len(parts)), le...]
  transfers between devices with their start and end apart: 31 -> 31, of which waited for: 19 -> 18; matrix products, arithmetic and copies ran while one was open for 4% -> 4% of each run, Pallas kernels for 22% -> 22%
where the time goes in v3:
time: 371 us; the launch traced here: 370 us
  waiting for transfers between devices  180 us (49%)
  Pallas kernels  97.5 us (26%)
  starting transfers between devices  49.8 us (13%)
  local copies, waits for them, and re-layouts  20.7 us (6%)
  between operations  14.4 us (4%)
  other arithmetic  7.55 us (2%)
    ppermute x15, waiting for transfers between devices, shifted(): lax.ppermute(array, axis, [(at, (at + shift) % size) for at in range(size)])  131 us
    pallas_call x4, Pallas kernels, product(): pl.pallas_call(waiting(functools.partial(product_kernel, (inner, outer, l...  25.1 us
    ppermute x8, waiting for transfers between devices, per_device(): back.append(lax.ppermute(pick(total, (at_tp - step) % tp), cell, pairs))  20.7 us
    pallas_call x1, Pallas kernels, correlate(): pl.pallas_call(waiting(correlate_kernel, len(waits)), grid=(2, steps), in...  20.2 us
    ppermute x15, starting transfers between devices, shifted(): lax.ppermute(array, axis, [(at, (at + shift) % size) for at in range(size)])  19.1 us
    pallas_call x1, Pallas kernels, convolve(): pl.pallas_call(waiting(functools.partial(convolve_kernel, len(parts)), le...  17.6 us
    pallas_call x2, Pallas kernels, shares(): pl.pallas_call(waiting(functools.partial(shares_kernel, (outer, inner, ne...  15.7 us
    all_gather x2, waiting for transfers between devices, per_device(): lax.all_gather(half, 'outer', axis=0, tiled=False)  14.7 us
  transfers between devices with their start and end apart: 31, of which 18 were waited for; matrix products, arithmetic and copies ran while one was open for 4% of the time, Pallas kernels for 22%

profile of v3, /device:TPU:4, one launch (start us, length us, event | category | flops | bytes accessed | tf_op | source)
XLA Modules:
  0.0 370.1 jit_solution(15166095995062677588)
XLA Ops:
  14.8 13.2 %collective-permute-done.1 = bf16[128,2048]{1,0:T(8,128)(2,1)} collective-permute-done((bf16[128,2048]{1,0:T(8,128)(2,1)}, bf16[128,2048]{1,0:T(8,128)(2,1)}, u32[]{:S(2)}, u32[]{:S(2)}) %collective-permute-start.1) | collective-permute-done | bytes 524320 | tf_op jit(solution)/shard_map/ppermute | solution.py:498
  40.1 7.8 %collective-permute-done.3.refs_3_ = bf16[64,2048]{1,0:T(8,128)(2,1)S(1)} collective-permute-done((bf16[64,2048]{1,0:T(8,128)(2,1)S(1)}, bf16[64,2048]{1,0:T(8,128)(2,1)S(1)}, u32[]{:S(2)}, u32[]{:S(2)}) %collective-permute-start.3) | collective-permute-done | bytes 262176 | tf_op jit(solution)/shard_map/ppermute | solution.py:567
  47.8 6.1 %collective-permute-done.4.refs_4_ = bf16[64,2048]{1,0:T(8,128)(2,1)S(1)} collective-permute-done((bf16[64,2048]{1,0:T(8,128)(2,1)S(1)}, bf16[64,2048]{1,0:T(8,128)(2,1)S(1)}, u32[]{:S(2)}, u32[]{:S(2)}) %collective-permute-start.4) | collective-permute-done | bytes 262176 | tf_op jit(solution)/shard_map/ppermute | solution.py:567
  53.9 6.5 %collective-permute-done.refs_1_.refs_6_.refs_5_.refs_4_ = bf16[1024,1024]{1,0:T(8,128)(2,1)S(1)} collective-permute-done((bf16[1024,1024]{1,0:T(8,128)(2,1)}, bf16[1024,1024]{1,0:T(8,128)(2,1)S(1)}, u32[]{:S(2)}, u32[]{:S(2)}) %collective-permute-start) | collective-permute-done | bytes 2097184 | tf_op jit(solution)/shard_map/ppermute | solution.py:498
  63.2 5.9 %all-to-all-start = ((bf16[8,2,256,256]{3,2,1,0:T(8,128)(2,1)}), bf16[8,2,256,256]{3,2,1,0:T(8,128)(2,1)}, u32[]{:S(2)}, u32[]{:S(2)}) async-start(bf16[8,2,256,256]{3,2,1,0:T(8,128)(2,1)} %copy-done.2), calls=%async_computation | async-start | bytes 4194304 | tf_op jit(solution)/shard_map/all_to_all | solution.py:580
  69.8 23.3 %collective-permute-done.6.refs_2_.refs_1_.refs_3_ = bf16[256,2048]{1,0:T(8,128)(2,1)} collective-permute-done((bf16[256,2048]{1,0:T(8,128)(2,1)S(1)}, bf16[256,2048]{1,0:T(8,128)(2,1)}, u32[]{:S(2)}, u32[]{:S(2)}) %collective-permute-start.6) | collective-permute-done | bytes 1048608 | tf_op jit(solution)/shard_map/ppermute | solution.py:498
  96.9 6.4 %shard_map.98 = bf16[1024,512]{1,0:T(8,128)(2,1)} custom-call(s32[8]{0:T(128)S(1)} %concatenate.41.index_ref, bf16[1024,1024]{1,0:T(8,128)(2,1)} %copy-done.3, bf16[256,2048]{1,0:T(8,128)(2,1)S(1)} %shard_map.96.refs_0_.refs_1_.refs_2_, bf16[256,2048]{1,0:T(8,128)(2,1)} %collective-permute-done.6.refs_2_.refs_1_.refs_3_, ...), custom_call_target="tpu_custom_call" | custom-call | tf_op jit(solution)/shard_map/pallas_call | solution.py:414
  106.5 24.6 %collective-permute-done.9.refs_6_ = bf16[1024,512]{1,0:T(8,128)(2,1)} collective-permute-done((bf16[1024,512]{1,0:T(8,128)(2,1)}, bf16[1024,512]{1,0:T(8,128)(2,1)}, u32[]{:S(2)}, u32[]{:S(2)}) %collective-permute-start.9) | collective-permute-done | bytes 1048608 | tf_op jit(solution)/shard_map/ppermute | solution.py:498
  131.1 6.7 %shard_map.99.refs_0_ = bf16[1024,512]{1,0:T(8,128)(2,1)} custom-call(s32[8]{0:T(128)S(1)} %concatenate.40.index_ref, bf16[256,2048]{1,0:T(8,128)(2,1)S(1)} %shard_map.96.refs_0_.refs_1_.refs_2_, bf16[256,2048]{1,0:T(8,128)(2,1)} %collective-permute-done.6.refs_2_.refs_1_.refs_3_, bf16[256,2048]{1,0:T(8,128)(2,1)} %collective-permute-done.7.refs_3_.refs_2_.refs_4_, ...), custom_call_target="tpu_custom_call" | custom-call | tf_op jit(solution)/shard_map/pallas_call | solution.py:414
  137.8 6.8 %collective-permute-start.11 = (bf16[1024,512]{1,0:T(8,128)(2,1)}, bf16[1024,512]{1,0:T(8,128)(2,1)}, u32[]{:S(2)}, u32[]{:S(2)}) collective-permute-start(bf16[1024,512]{1,0:T(8,128)(2,1)} %shard_map.99.refs_0_), channel_id=1, source_target_pairs={{0,8},{8,16},{16,24},{24,0},{1,9},{9,17},{17,25},{25,1},{2,10},{10... | collective-permute-start | bytes 3145736 | tf_op jit(solution)/shard_map/ppermute | solution.py:498
  147.5 20.2 %shard_map.101 = (bf16[2048,256]{1,0:T(8,128)(2,1)S(1)}, bf16[2,2048,256]{2,1,0:T(8,128)(2,1)S(1)}) custom-call(s32[1]{0:T(128)} %constant.368.clone.1.index_ref, bf16[1024,512]{1,0:T(8,128)(2,1)} %shard_map.99.refs_0_, bf16[2048,2048]{1,0:T(8,128)(2,1)} %constant.370.clone.refs_1_, bf16[2048,2048]{1,0:T(8,128)(2,1)} %constant.371.clone.refs_2_, ...), custom_call_target="tpu_custom_call" | custom-call | tf_op jit(solution)/shard_map/pallas_call | solution.py:120
  171.7 6.0 %shard_map.102.refs_0_ = bf16[1024,512]{1,0:T(8,128)(2,1)S(1)} custom-call(s32[8]{0:T(128)S(1)} %concatenate.39.index_ref, bf16[2,2048,256]{2,1,0:T(8,128)(2,1)} %copy-done.5, bf16[256,2048]{1,0:T(8,128)(2,1)S(1)} %shard_map.96.refs_0_.refs_1_.refs_2_, bf16[256,2048]{1,0:T(8,128)(2,1)} %collective-permute-done.6.refs_2_.refs_1_.refs_3_, ...), custom_call_target="tpu_custom_call" | custom-call | tf_op jit(solution)/shard_map/pallas_call | solution.py:414
  177.7 6.4 %collective-permute-done.12.refs_2_ = bf16[4,256,256]{2,1,0:T(8,128)(2,1)} collective-permute-done((bf16[4,256,256]{2,1,0:T(8,128)(2,1)}, bf16[4,256,256]{2,1,0:T(8,128)(2,1)}, u32[]{:S(2)}, u32[]{:S(2)}) %collective-permute-start.12) | collective-permute-done | bytes 524320 | tf_op jit(solution)/shard_map/ppermute | solution.py:498
  189.1 38.8 %collective-permute-done.13.refs_8_ = bf16[1024,512]{1,0:T(8,128)(2,1)} collective-permute-done((bf16[1024,512]{1,0:T(8,128)(2,1)S(1)}, bf16[1024,512]{1,0:T(8,128)(2,1)}, u32[]{:S(2)}, u32[]{:S(2)}) %collective-permute-start.13) | collective-permute-done | bytes 1048608 | tf_op jit(solution)/shard_map/ppermute | solution.py:498
  228.0 6.0 %shard_map.104.refs_0_ = bf16[2,1024,256]{2,1,0:T(8,128)(2,1)S(1)} custom-call(s32[8]{0:T(128)S(1)} %concatenate.37.index_ref, bf16[512,512]{1,0:T(8,128)(2,1)} %get-tuple-element.15.refs_0_, bf16[512,512]{1,0:T(8,128)(2,1)} %get-tuple-element.16.refs_1_, bf16[256,2048]{1,0:T(8,128)(2,1)S(1)} %shard_map.96.refs_0_.refs_1_.refs_2_, ...), custom_call_target="tpu_custom_call" | custom-call | tf_op jit(solution)/shard_map/pallas_call | solution.py:414
  233.9 12.6 %all-gather.5.cloned.1.call-done = bf16[2048,512]{1,0:T(8,128)(2,1)} async-done(((bf16[512,512]{1,0:T(8,128)(2,1)}), bf16[2048,512]{1,0:T(8,128)(2,1)}) %all-gather.5.cloned.1.call-update) | async-done | bytes 2097168 | tf_op jit(solution)/shard_map/all_gather | solution.py:620
  248.1 7.8 %shard_map.105 = (bf16[2,256,1024]{2,1,0:T(8,128)(2,1)S(1)}, bf16[2,256,1024]{2,1,0:T(8,128)(2,1)S(1)}) custom-call(s32[4]{0:T(128)S(1)} %pad_add_fusion.1.index_ref, bf16[2,1024,256]{2,1,0:T(8,128)(2,1)S(1)} %shard_map.104.refs_0_, bf16[4,512,512]{2,1,0:T(8,128)(2,1)S(1)} %bitcast.108, bf16[1024,2048]{1,0:T(8,128)(2,1)} %refs_3_.3, ...), custom_call_target="tpu_custom_call" | custom-call | tf_op jit(solution)/shard_map/pallas_call | solution.py:478
  260.7 11.1 %collective-permute-done.15.refs_5_ = bf16[1024,256]{1,0:T(8,128)(2,1)} collective-permute-done((bf16[1024,256]{1,0:T(8,128)(2,1)}, bf16[1024,256]{1,0:T(8,128)(2,1)}, u32[]{:S(2)}, u32[]{:S(2)}) %collective-permute-start.15) | collective-permute-done | bytes 524320 | tf_op jit(solution)/shard_map/ppermute | solution.py:498
  272.8 17.6 %shard_map.106 = bf16[2048,256]{1,0:T(8,128)(2,1)} custom-call(s32[2,16]{1,0:T(2,128)S(1)} %pad_add_fusion.index_ref, bf16[2,2,128,1024]{3,2,1,0:T(8,128)(2,1)S(1)} %bitcast.103, bf16[2048,2048]{1,0:T(8,128)(2,1)} %constant.370.clone.refs_1_, bf16[2048,2048]{1,0:T(8,128)(2,1)} %constant.371.clone.refs_2_, bf16[2,2048,256]{2,1,0:T(8,128)(2,1)S(1)} %copy-done.6, ...), custom_call_target="tpu_custom_call" | custom-call | tf_op jit(solution)/shard_map/pallas_call | solution.py:179
  295.2 7.8 %shard_map.108 = (bf16[2,256,1024]{2,1,0:T(8,128)(2,1)S(1)}, bf16[2,256,1024]{2,1,0:T(8,128)(2,1)S(1)}) custom-call(s32[4]{0:T(128)S(1)} %pad_add_fusion.1.index_ref, bf16[8,256,256]{2,1,0:T(8,128)(2,1)} %bitcast.45.refs_0_, bf16[2,4,32,1024]{3,2,1,0:T(8,128)(2,1)S(1)} %bitcast.105, bf16[4,512,512]{2,1,0:T(8,128)(2,1)S(1)} %bitcast.107, ...), custom_call_target="tpu_custom_call" | custom-call | tf_op jit(solution)/shard_map/pallas_call | solution.py:478
  303.1 6.4 %all-to-all-start.1 = ((bf16[8,256,256]{2,1,0:T(8,128)(2,1)}), bf16[8,256,256]{2,1,0:T(8,128)(2,1)}, u32[]{:S(2)}, u32[]{:S(2)}) async-start(bf16[8,256,256]{2,1,0:T(8,128)(2,1)} %bitcast.45.refs_0_), calls=%async_computation.1 | async-start | bytes 2097152 | tf_op jit(solution)/shard_map/all_to_all | solution.py:633
  314.6 5.8 %collective-permute-start.17 = (bf16[2,32,1024]{2,1,0:T(8,128)(2,1)S(1)}, bf16[2,32,1024]{2,1,0:T(8,128)(2,1)S(1)}, u32[]{:S(2)}, u32[]{:S(2)}) collective-permute-start(bf16[2,32,1024]{2,1,0:T(8,128)(2,1)S(1)} %get-tuple-element.40), channel_id=1, source_target_pairs={{0,0},{8,1},{16,2},{24,3},{1,8},{9,9},{17,10},{25,11},{2,16},{10,1... | collective-permute-start | bytes 393224 | tf_op jit(solution)/shard_map/ppermute | solution.py:646
  323.2 6.7 %collective-permute-done.22 = bf16[2,128,1024]{2,1,0:T(8,128)(2,1)S(1)} collective-permute-done((bf16[2,128,1024]{2,1,0:T(8,128)(2,1)}, bf16[2,128,1024]{2,1,0:T(8,128)(2,1)S(1)}, u32[]{:S(2)}, u32[]{:S(2)}) %collective-permute-start.22) | collective-permute-done | bytes 524320 | tf_op jit(solution)/shard_map/ppermute | solution.py:498
  335.3 12.8 %collective-permute-done.17.refs_0_ = bf16[2,32,1024]{2,1,0:T(8,128)(2,1)S(1)} collective-permute-done((bf16[2,32,1024]{2,1,0:T(8,128)(2,1)S(1)}, bf16[2,32,1024]{2,1,0:T(8,128)(2,1)S(1)}, u32[]{:S(2)}, u32[]{:S(2)}) %collective-permute-start.17) | collective-permute-done | bytes 131104 | tf_op jit(solution)/shard_map/ppermute | solution.py:646
  (115 shorter events, 82.4 us)
Async XLA Ops:
  12.8 47.6 %collective-permute-start = (bf16[1024,1024]{1,0:T(8,128)(2,1)}, bf16[1024,1024]{1,0:T(8,128)(2,1)S(1)}, u32[]{:S(2)}, u32[]{:S(2)}) collective-permute-start(bf16[1024,1024]{1,0:T(8,128)(2,1)} %shard_map.94.refs_0_), channel_id=1, source_target_pairs={{0,4},{4,0},{1,5},{5,1},{2,6},{6,2},{3,7},{7,3},{8,12},{12,8},{9,1... | collective-permute-start | bytes 6291464 | tf_op jit(solution)/shard_map/ppermute | solution.py:498
  14.3 13.7 %collective-permute-start.1 = (bf16[128,2048]{1,0:T(8,128)(2,1)}, bf16[128,2048]{1,0:T(8,128)(2,1)}, u32[]{:S(2)}, u32[]{:S(2)}) collective-permute-start(bf16[128,2048]{1,0:T(8,128)(2,1)} %get-tuple-element.32.refs_0_), channel_id=1, source_target_pairs={{0,2},{2,0},{1,3},{3,1},{4,6},{6,4},{5,7},{7,5},{8,10},{10,8},{9,1... | collective-permute-start | bytes 1572872 | tf_op jit(solution)/shard_map/ppermute | solution.py:498
  30.3 17.5 %collective-permute-start.3 = (bf16[64,2048]{1,0:T(8,128)(2,1)S(1)}, bf16[64,2048]{1,0:T(8,128)(2,1)S(1)}, u32[]{:S(2)}, u32[]{:S(2)}) collective-permute-start(bf16[64,2048]{1,0:T(8,128)(2,1)S(1)} %get-tuple-element.29), channel_id=1, source_target_pairs={{0,1},{1,9},{2,3},{3,11},{8,16},{9,24},{10,18},{11,26},{16,17},{17... | collective-permute-start | bytes 786440 | tf_op jit(solution)/shard_map/ppermute | solution.py:567
  33.3 20.6 %collective-permute-start.4 = (bf16[64,2048]{1,0:T(8,128)(2,1)S(1)}, bf16[64,2048]{1,0:T(8,128)(2,1)S(1)}, u32[]{:S(2)}, u32[]{:S(2)}) collective-permute-start(bf16[64,2048]{1,0:T(8,128)(2,1)S(1)} %get-tuple-element.30), channel_id=1, source_target_pairs={{0,16},{1,24},{2,18},{3,26},{8,17},{9,25},{10,19},{11,27},{16,0},{... | collective-permute-start | bytes 786440 | tf_op jit(solution)/shard_map/ppermute | solution.py:567
  35.8 18.0 %collective-permute-start.5 = (bf16[64,2048]{1,0:T(8,128)(2,1)S(1)}, bf16[64,2048]{1,0:T(8,128)(2,1)S(1)}, u32[]{:S(2)}, u32[]{:S(2)}) collective-permute-start(bf16[64,2048]{1,0:T(8,128)(2,1)S(1)} %get-tuple-element.27), channel_id=1, source_target_pairs={{0,17},{1,25},{2,19},{3,27},{8,0},{9,8},{10,2},{11,10},{16,1},{17,... | collective-permute-start | bytes 786440 | tf_op jit(solution)/shard_map/ppermute | solution.py:567
  63.2 83.1 %all-to-all-start = ((bf16[8,2,256,256]{3,2,1,0:T(8,128)(2,1)}), bf16[8,2,256,256]{3,2,1,0:T(8,128)(2,1)}, u32[]{:S(2)}, u32[]{:S(2)}) async-start(bf16[8,2,256,256]{3,2,1,0:T(8,128)(2,1)} %copy-done.2), calls=%async_computation | async-start | bytes 4194304 | tf_op jit(solution)/shard_map/all_to_all | solution.py:580
  69.1 177.4 %all-gather.5.cloned.1.call-start = ((), (), s32[]{:S(2)}) async-start(), calls=%async_computation.2 | async-start | bytes 2621440 | tf_op jit(solution)/shard_map/all_gather | solution.py:620
  69.2 23.9 %collective-permute-start.6 = (bf16[256,2048]{1,0:T(8,128)(2,1)S(1)}, bf16[256,2048]{1,0:T(8,128)(2,1)}, u32[]{:S(2)}, u32[]{:S(2)}) collective-permute-start(bf16[256,2048]{1,0:T(8,128)(2,1)S(1)} %shard_map.96.refs_0_.refs_1_.refs_2_), channel_id=1, source_target_pairs={{0,2},{2,0},{1,3},{3,1},{4,6},{6,4},{5,7},{7,5},{8,10},{10,8},{9,1... | collective-permute-start | bytes 3145736 | tf_op jit(solution)/shard_map/ppermute | solution.py:498
  69.8 27.2 %collective-permute-start.7 = (bf16[256,2048]{1,0:T(8,128)(2,1)S(1)}, bf16[256,2048]{1,0:T(8,128)(2,1)}, u32[]{:S(2)}, u32[]{:S(2)}) collective-permute-start(bf16[256,2048]{1,0:T(8,128)(2,1)S(1)} %shard_map.96.refs_0_.refs_1_.refs_2_), channel_id=1, source_target_pairs={{0,1},{1,0},{2,3},{3,2},{4,5},{5,4},{6,7},{7,6},{8,9},{9,8},{10,11... | collective-permute-start | bytes 3145736 | tf_op jit(solution)/shard_map/ppermute | solution.py:498
  103.4 27.8 %collective-permute-start.9 = (bf16[1024,512]{1,0:T(8,128)(2,1)}, bf16[1024,512]{1,0:T(8,128)(2,1)}, u32[]{:S(2)}, u32[]{:S(2)}) collective-permute-start(bf16[1024,512]{1,0:T(8,128)(2,1)} %shard_map.98), channel_id=1, source_target_pairs={{0,8},{8,16},{16,24},{24,0},{1,9},{9,17},{17,25},{25,1},{2,10},{10... | collective-permute-start | bytes 3145736 | tf_op jit(solution)/shard_map/ppermute | solution.py:498
  105.0 66.7 %collective-permute-start.10 = (bf16[1024,1024]{1,0:T(8,128)(2,1)S(1)}, bf16[1024,1024]{1,0:T(8,128)(2,1)}, u32[]{:S(2)}, u32[]{:S(2)}) collective-permute-start(bf16[1024,1024]{1,0:T(8,128)(2,1)S(1)} %copy-done.4), channel_id=1, source_target_pairs={{0,4},{4,0},{1,5},{5,1},{2,6},{6,2},{3,7},{7,3},{8,12},{12,8},{9,1... | collective-permute-start | bytes 6291464 | tf_op jit(solution)/shard_map/ppermute | solution.py:498
  137.8 33.8 %collective-permute-start.11 = (bf16[1024,512]{1,0:T(8,128)(2,1)}, bf16[1024,512]{1,0:T(8,128)(2,1)}, u32[]{:S(2)}, u32[]{:S(2)}) collective-permute-start(bf16[1024,512]{1,0:T(8,128)(2,1)} %shard_map.99.refs_0_), channel_id=1, source_target_pairs={{0,8},{8,16},{16,24},{24,0},{1,9},{9,17},{17,25},{25,1},{2,10},{10... | collective-permute-start | bytes 3145736 | tf_op jit(solution)/shard_map/ppermute | solution.py:498
  170.2 13.9 %collective-permute-start.12 = (bf16[4,256,256]{2,1,0:T(8,128)(2,1)}, bf16[4,256,256]{2,1,0:T(8,128)(2,1)}, u32[]{:S(2)}, u32[]{:S(2)}) collective-permute-start(bf16[4,256,256]{2,1,0:T(8,128)(2,1)} %get-tuple-element.25), channel_id=1, source_target_pairs={{0,4},{4,0},{1,5},{5,1},{2,6},{6,2},{3,7},{7,3},{8,12},{12,8},{9,1... | collective-permute-start | bytes 1572872 | tf_op jit(solution)/shard_map/ppermute | solution.py:498
  186.2 107.5 %all-gather.7.cloned.1.call-start = ((), (), s32[]{:S(2)}) async-start(), calls=%async_computation.3 | async-start | bytes 2621440 | tf_op jit(solution)/shard_map/all_gather | solution.py:620
  186.2 41.7 %collective-permute-start.13 = (bf16[1024,512]{1,0:T(8,128)(2,1)S(1)}, bf16[1024,512]{1,0:T(8,128)(2,1)}, u32[]{:S(2)}, u32[]{:S(2)}) collective-permute-start(bf16[1024,512]{1,0:T(8,128)(2,1)S(1)} %shard_map.102.refs_0_), channel_id=1, source_target_pairs={{0,8},{8,16},{16,24},{24,0},{1,9},{9,17},{17,25},{25,1},{2,10},{10... | collective-permute-start | bytes 3145736 | tf_op jit(solution)/shard_map/ppermute | solution.py:498
  257.1 14.6 %collective-permute-start.15 = (bf16[1024,256]{1,0:T(8,128)(2,1)}, bf16[1024,256]{1,0:T(8,128)(2,1)}, u32[]{:S(2)}, u32[]{:S(2)}) collective-permute-start(bf16[1024,256]{1,0:T(8,128)(2,1)} %get-tuple-element.23), channel_id=1, source_target_pairs={{0,4},{4,0},{1,5},{5,1},{2,6},{6,2},{3,7},{7,3},{8,12},{12,8},{9,1... | collective-permute-start | bytes 1572872 | tf_op jit(solution)/shard_map/ppermute | solution.py:498
  259.9 30.4 %collective-permute-start.16 = (bf16[2,128,1024]{2,1,0:T(8,128)(2,1)}, bf16[2,128,1024]{2,1,0:T(8,128)(2,1)}, u32[]{:S(2)}, u32[]{:S(2)}) collective-permute-start(bf16[2,128,1024]{2,1,0:T(8,128)(2,1)} %slice_bitcast_fusion.2), channel_id=1, source_target_pairs={{0,2},{2,0},{1,3},{3,1},{4,6},{6,4},{5,7},{7,5},{8,10},{10,8},{9,1... | collective-permute-start | bytes 1572872 | tf_op jit(solution)/shard_map/ppermute | solution.py:498
  303.1 47.4 %all-to-all-start.1 = ((bf16[8,256,256]{2,1,0:T(8,128)(2,1)}), bf16[8,256,256]{2,1,0:T(8,128)(2,1)}, u32[]{:S(2)}, u32[]{:S(2)}) async-start(bf16[8,256,256]{2,1,0:T(8,128)(2,1)} %bitcast.45.refs_0_), calls=%async_computation.1 | async-start | bytes 2097152 | tf_op jit(solution)/shard_map/all_to_all | solution.py:633
  314.0 15.9 %collective-permute-start.22 = (bf16[2,128,1024]{2,1,0:T(8,128)(2,1)}, bf16[2,128,1024]{2,1,0:T(8,128)(2,1)S(1)}, u32[]{:S(2)}, u32[]{:S(2)}) collective-permute-start(bf16[2,128,1024]{2,1,0:T(8,128)(2,1)} %slice_bitcast_fusion), channel_id=1, source_target_pairs={{0,2},{2,0},{1,3},{3,1},{4,6},{6,4},{5,7},{7,5},{8,10},{10,8},{9,1... | collective-permute-start | bytes 1572872 | tf_op jit(solution)/shard_map/ppermute | solution.py:498
  314.6 33.6 %collective-permute-start.17 = (bf16[2,32,1024]{2,1,0:T(8,128)(2,1)S(1)}, bf16[2,32,1024]{2,1,0:T(8,128)(2,1)S(1)}, u32[]{:S(2)}, u32[]{:S(2)}) collective-permute-start(bf16[2,32,1024]{2,1,0:T(8,128)(2,1)S(1)} %get-tuple-element.40), channel_id=1, source_target_pairs={{0,0},{8,1},{16,2},{24,3},{1,8},{9,9},{17,10},{25,11},{2,16},{10,1... | collective-permute-start | bytes 393224 | tf_op jit(solution)/shard_map/ppermute | solution.py:646
  320.4 30.1 %collective-permute-start.18 = (bf16[2,32,1024]{2,1,0:T(8,128)(2,1)S(1)}, bf16[2,32,1024]{2,1,0:T(8,128)(2,1)S(1)}, u32[]{:S(2)}, u32[]{:S(2)}) collective-permute-start(bf16[2,32,1024]{2,1,0:T(8,128)(2,1)S(1)} %get-tuple-element.39), channel_id=1, source_target_pairs={{1,0},{9,1},{17,2},{25,3},{2,8},{10,9},{18,10},{26,11},{3,16},{11,... | collective-permute-start | bytes 393224 | tf_op jit(solution)/shard_map/ppermute | solution.py:646
  320.4 30.0 %collective-permute-start.19 = (bf16[2,32,1024]{2,1,0:T(8,128)(2,1)S(1)}, bf16[2,32,1024]{2,1,0:T(8,128)(2,1)S(1)}, u32[]{:S(2)}, u32[]{:S(2)}) collective-permute-start(bf16[2,32,1024]{2,1,0:T(8,128)(2,1)S(1)} %get-tuple-element.38), channel_id=1, source_target_pairs={{2,0},{10,1},{18,2},{26,3},{3,8},{11,9},{19,10},{27,11},{0,16},{8,... | collective-permute-start | bytes 393224 | tf_op jit(solution)/shard_map/ppermute | solution.py:646
  321.9 34.2 %collective-permute-start.20 = (bf16[2,32,1024]{2,1,0:T(8,128)(2,1)S(1)}, bf16[2,32,1024]{2,1,0:T(8,128)(2,1)S(1)}, u32[]{:S(2)}, u32[]{:S(2)}) collective-permute-start(bf16[2,32,1024]{2,1,0:T(8,128)(2,1)S(1)} %get-tuple-element.37), channel_id=1, source_target_pairs={{3,0},{11,1},{19,2},{27,3},{0,8},{8,9},{16,10},{24,11},{1,16},{9,1... | collective-permute-start | bytes 393224 | tf_op jit(solution)/shard_map/ppermute | solution.py:646
  332.0 24.6 %collective-permute-start.23 = (bf16[2,32,1024]{2,1,0:T(8,128)(2,1)}, bf16[2,32,1024]{2,1,0:T(8,128)(2,1)S(1)}, u32[]{:S(2)}, u32[]{:S(2)}) collective-permute-start(bf16[2,32,1024]{2,1,0:T(8,128)(2,1)} %get-tuple-element.36), channel_id=1, source_target_pairs={{0,0},{8,1},{16,2},{24,3},{1,8},{9,9},{17,10},{25,11},{2,16},{10,1... | collective-permute-start | bytes 393224 | tf_op jit(solution)/shard_map/ppermute | solution.py:646
  (23 other events, 248.3 us)
Sparse Core Ops, SparseCore 0:
  186.3 60.1 all-gather.4
  248.7 44.9 all-gather.6

commit v4 on v3

--- a/solution.py
+++ b/solution.py
@@ -80,7 +80,8 @@
     return pl.ds(pl.multiple_of(index * size, size), size)
 
 
-def correlate_kernel(index_ref, cos_ref, sin_ref, turn_ref, both_ref, out_ref, spectrum_ref, signal_ref, mix_ref):
+def correlate_kernel(index_ref, cos_ref, sin_ref, turn_ref, *refs):
+    both_refs, (out_ref, spectrum_ref, signal_ref, mix_ref) = refs[:2], refs[2:]
     phase, step = pl.program_id(0), pl.program_id(1)
     block = cos_ref.shape[0]
     length, channels = mix_ref.shape[1:]
@@ -89,7 +90,7 @@
     @pl.when((phase == 0) & (step == 0))
     def _():
         for which in range(2):
-            signal_ref[:, which * channels : (which + 1) * channels] = both_ref[:, which].reshape(length, channels)
+            signal_ref[:, which * channels : (which + 1) * channels] = both_refs[which][...].reshape(length, channels)
 
     @pl.when(phase == 0)
     def _():
@@ -111,8 +112,8 @@
         out_ref[...] = (total * (1.0 / length)).astype(out_ref.dtype)
 
 
-def correlate(table, turn, both, waits):
-    parts, _, rows, channels = both.shape
+def correlate(table, turn, filters, signal, waits):
+    parts, rows, channels = filters.shape
     length = parts * rows
     block = table_block(length)
     steps = length // block
@@ -126,7 +127,8 @@
             table_spec,
             table_spec,
             pl.BlockSpec((block, 2), lambda p, s: (s, 0)),
-            pl.BlockSpec((parts, 2, rows, channels), lambda p, s: (0, 0, 0, 0)),
+            pl.BlockSpec((parts, rows, channels), lambda p, s: (0, 0, 0)),
+            pl.BlockSpec((parts, rows, channels), lambda p, s: (0, 0, 0)),
         ],
         out_specs=[
             pl.BlockSpec((block, channels), lambda p, s: (p * s, 0)),
@@ -139,7 +141,7 @@
         scratch_shapes=[pltpu.VMEM((length, 2 * channels), SHORT), pltpu.VMEM((2, length, channels), SHORT)],
         compiler_params=kernel_params(2),
         cost_estimate=NO_COST,
-    )(jnp.zeros((1,), jnp.int32), *waits, table[0], table[1], turn, both)
+    )(jnp.zeros((1,), jnp.int32), *waits, table[0], table[1], turn, filters, signal)
 
 
 def convolve_kernel(inner, places_ref, cos_ref, sin_ref, spectrum_ref, *refs):
@@ -197,27 +199,29 @@
     )(places, *waits, table[0], table[1], spectrum, *parts)
 
 
-def prepare_kernel(index_ref, filters_ref, gate_ref, cotangent_ref, out_ref):
-    out_ref[0, 0] = filters_ref[...].astype(SHORT)
-    out_ref[0, 1] = (cotangent_ref[...].astype(WIDE) * gate_ref[...].astype(WIDE)).astype(SHORT)
-
-
-def prepare(filters, gate, cotangent, groups, waits):
-    rows, width = filters.shape
+def prepare_kernel(index_ref, *refs):
+    total = refs[0][...].astype(WIDE)
+    for ref in refs[1:-1]:
+        total = total * ref[...].astype(WIDE)
+    refs[-1][0] = total.astype(SHORT)
+
+
+def prepare(factors, groups, waits):
+    rows, width = factors[0].shape
     channels = width // groups
     if channels % 128:
-        both = jnp.stack([filters, cotangent.astype(WIDE) * gate.astype(WIDE)]).astype(SHORT)
-        return both.reshape(2, rows, groups, channels).transpose(2, 0, 1, 3)
+        total = functools.reduce(lambda x, y: x * y, [factor.astype(WIDE) for factor in factors])
+        return total.astype(SHORT).reshape(rows, groups, channels).swapaxes(0, 1)
     spec = pl.BlockSpec((rows, channels), lambda g: (0, g))
     return pl.pallas_call(
         waiting(prepare_kernel, len(waits)),
         grid=(groups,),
-        in_specs=[pl.BlockSpec(memory_space=pltpu.SMEM)] + [ANYWHERE] * len(waits) + [spec] * 3,
-        out_specs=pl.BlockSpec((1, 2, rows, channels), lambda g: (g, 0, 0, 0)),
-        out_shape=jax.ShapeDtypeStruct((groups, 2, rows, channels), SHORT),
+        in_specs=[pl.BlockSpec(memory_space=pltpu.SMEM)] + [ANYWHERE] * len(waits) + [spec] * len(factors),
+        out_specs=pl.BlockSpec((1, rows, channels), lambda g: (g, 0, 0)),
+        out_shape=jax.ShapeDtypeStruct((groups, rows, channels), SHORT),
         compiler_params=kernel_params(1),
         cost_estimate=NO_COST,
-    )(jnp.zeros((1,), jnp.int32), *waits, filters, gate, cotangent)
+    )(jnp.zeros((1,), jnp.int32), *waits, *factors)
 
 
 def finish_kernel(convolved_ref, gate_ref, cotangent_ref, output_ref, grad_ref):
@@ -549,8 +553,10 @@
     if split == 1:
         by_far = tokens.reshape(far, near * fine_rows, columns)
         by_far = [pick(by_far, (at_far + f) % far) for f in range(far)]
-        sent = send_chunks(order[:2], by_far[1:])
-        prepared = prepare(filters, gate, cotangent, ctx_size, [sent])
+        own_filters = prepare([filters], ctx_size, by_far[1:])
+        all_filters = lax.all_to_all(own_filters, ctx, split_axis=0, concat_axis=0, tiled=True)
+        sent = send_chunks(order[:2], [own_filters])
+        prepared = prepare([cotangent, gate], ctx_size, [sent])
         held = [by_far[0]] + [shifted(by_far[f], "far", f) for f in range(1, far)]
         held = jnp.stack(held).reshape(far, near, fine_rows, columns)
         for step in range(tp):
@@ -565,10 +571,12 @@
                 held, ((at_far - number // near) % far, number % near, 0, 0), (1, 1, fine_rows, columns)
             )
             moved.append(lax.ppermute(part.reshape(fine_rows, columns), cell, pairs))
-        token_part = join(moved, [prepared, *arrivals[0]])
+        token_part = join(moved, [prepared, all_filters, *arrivals[0]])
     else:
-        sent = send_chunks(order[:2], [])
-        prepared = prepare(filters, gate, cotangent, ctx_size, [sent])
+        own_filters = prepare([filters], ctx_size, [])
+        all_filters = lax.all_to_all(own_filters, ctx, split_axis=0, concat_axis=0, tiled=True)
+        sent = send_chunks(order[:2], [own_filters])
+        prepared = prepare([cotangent, gate], ctx_size, [sent])
         row_parts = tokens.reshape(tp, fine_rows, columns)
         for step in range(tp):
             pairs = [(o * tp + t, destination(o, t, step)) for o in range(outer) for t in range(tp)]
@@ -577,8 +585,10 @@
         token_part = turned(moved, at_tp).reshape(outer, split, fine_rows, columns).swapaxes(1, 2)
         token_part = token_part.reshape(outer * fine_rows, split * columns)
 
-    channel_rows = lax.all_to_all(release(prepared, [token_part]), ctx, split_axis=0, concat_axis=0, tiled=True)
-    sent = send_chunks(order[2:], [token_part, *arrivals[0]])
+    signal_rows = lax.all_to_all(release(prepared, [token_part]), ctx, split_axis=0, concat_axis=0, tiled=True)
+    sent = token_part
+    for s in order[2:]:
+        sent = send_chunks([s], [sent, *arrivals[0]])
     table = transform_table(length)
 
     pieces = [token_part] + [shifted(token_part, "far", f) for f in range(1, far)]
@@ -605,20 +615,20 @@
         held = [chunk[s] for chunk in received]
         running = product(pieces, in_weight, chunks[s], held, blocks, row_order, running, s == 0, waits)
         waits = []
-        if s == outer - 2:
-            grad_values, spectrum = correlate(table, rotation(length), channel_rows, [running])
+        if s == 1:
+            grad_values, spectrum = correlate(table, rotation(length), all_filters, signal_rows, [running])
             by_inner = grad_values.reshape(outer, inner, rows, channels)
             grad_parts = [pick(by_inner, at_inner, 1)]
             for i in range(1, inner):
                 grad_parts.append(shifted(pick(by_inner, (at_inner + i) % inner, 1), "inner", i))
-            waits = [spectrum]
-        if s == outer - 1:
+            waits = [spectrum, *arrivals[1]]
+        if s == 2:
             sources = [(at_far + f) % far * near + (at_near + n) % near for n in range(near) for f in range(far)]
             arranged = arrange(
                 grad_parts, jnp.stack(back_inner), jnp.stack(sources), (outer, inner, far, near, halves, half_rows), [running]
             )
             gathered = [lax.all_gather(half, "outer", axis=0, tiled=False) for half in arranged]
-            waits = list(arranged)
+            waits = list(arranged) + arrivals[-1]
     value_parts = [running[0]] + [shifted(running[i], "inner", i) for i in range(1, inner)]
 
     sent_back = []

time: 371 us -> 387 us (1.043)
  starting transfers between devices: 49.8 us -> 72.8 us
  waiting for transfers between devices: 180 us -> 167 us
  local copies, waits for them, and re-layouts: 20.7 us -> 30.1 us
    all_gather x2, waiting for transfers between devices: 14.7 us -> 0.04 us  [per_device(): lax.all_gather(half, 'outer', axis=0, tiled=False)]
    ppermute x15 -> x16, waiting for transfers between devices: 131 us -> 117 us  [shifted(): lax.ppermute(array, axis, [(at, (at + shift) % size) for at in range(size)])]
    all_to_all x1, starting transfers between devices: 6.39 us -> 16.3 us  [per_device(): lax.all_to_all(convolved, ctx, split_axis=0, concat_axis=0, tiled=True)]
    unnamed x32 -> x70, local copies, waits for them, and re-layouts: 10.9 us -> 20.8 us
    ppermute x15 -> x16, starting transfers between devices: 19.1 us -> 28.1 us  [shifted(): lax.ppermute(array, axis, [(at, (at + shift) % size) for at in range(size)])]
    all_to_all x0 -> x1, waiting for transfers between devices: none -> 7.01 us  [per_device(): lax.all_to_all(own_filters, ctx, split_axis=0, concat_axis=0, tiled=True)]
    ppermute x4, waiting for transfers between devices: 13.8 us -> 20.5 us  [per_device(): moved.append(lax.ppermute(part.reshape(fine_rows, columns), cell, pairs))]
    all_to_all x0 -> x1, starting transfers between devices: none -> 4.88 us  [per_device(): lax.all_to_all(own_filters, ctx, split_axis=0, concat_axis=0, tiled=True)]
  transfers between devices with their start and end apart: 31 -> 33, of which waited for: 18 -> 18; matrix products, arithmetic and copies ran while one was open for 4% -> 4% of each run, Pallas kernels for 22% -> 20%
where the time goes in v4:
time: 387 us; the launch traced here: 386 us
  waiting for transfers between devices  167 us (43%)
  Pallas kernels  95.4 us (25%)
  starting transfers between devices  72.8 us (19%)
  local copies, waits for them, and re-layouts  30.1 us (8%)
  between operations  14.5 us (4%)
  other arithmetic  6.66 us (2%)
    ppermute x16, waiting for transfers between devices, shifted(): lax.ppermute(array, axis, [(at, (at + shift) % size) for at in range(size)])  117 us
    ppermute x16, starting transfers between devices, shifted(): lax.ppermute(array, axis, [(at, (at + shift) % size) for at in range(size)])  28.1 us
    pallas_call x4, Pallas kernels, product(): pl.pallas_call(waiting(functools.partial(product_kernel, (inner, outer, l...  24.4 us
    ppermute x8, waiting for transfers between devices, per_device(): back.append(lax.ppermute(pick(total, (at_tp - step) % tp), cell, pairs))  22.7 us
    unnamed x70, local copies, waits for them, and re-layouts  20.8 us
    pallas_call x1, Pallas kernels, correlate(): pl.pallas_call(waiting(correlate_kernel, len(waits)), grid=(2, steps), in...  20.5 us
    ppermute x4, waiting for transfers between devices, per_device(): moved.append(lax.ppermute(part.reshape(fine_rows, columns), cell, pairs))  20.5 us
    pallas_call x2, Pallas kernels, shares(): pl.pallas_call(waiting(functools.partial(shares_kernel, (outer, inner, ne...  18.3 us
  transfers between devices with their start and end apart: 33, of which 18 were waited for; matrix products, arithmetic and copies ran while one was open for 4% of the time, Pallas kernels for 20%

profile of v4, /device:TPU:4, one launch (start us, length us, event | category | flops | bytes accessed | tf_op | source)
XLA Modules:
  0.0 386.4 jit_solution(16531411733167822006)
XLA Ops:
  15.5 4.9 %all-to-all-start = ((bf16[8,256,256]{2,1,0:T(8,128)(2,1)}), bf16[8,256,256]{2,1,0:T(8,128)(2,1)S(1)}, u32[]{:S(2)}, u32[]{:S(2)}) async-start(bf16[8,256,256]{2,1,0:T(8,128)(2,1)} %copy-done.11), calls=%async_computation | async-start | bytes 2097152 | tf_op jit(solution)/shard_map/all_to_all | solution.py:557
  20.9 12.9 %collective-permute-done.1 = bf16[128,2048]{1,0:T(8,128)(2,1)} collective-permute-done((bf16[128,2048]{1,0:T(8,128)(2,1)}, bf16[128,2048]{1,0:T(8,128)(2,1)}, u32[]{:S(2)}, u32[]{:S(2)}) %collective-permute-start.1) | collective-permute-done | bytes 524320 | tf_op jit(solution)/shard_map/ppermute | solution.py:502
  43.2 10.4 %collective-permute-done.3.refs_4_ = bf16[64,2048]{1,0:T(8,128)(2,1)S(1)} collective-permute-done((bf16[64,2048]{1,0:T(8,128)(2,1)S(1)}, bf16[64,2048]{1,0:T(8,128)(2,1)S(1)}, u32[]{:S(2)}, u32[]{:S(2)}) %collective-permute-start.3) | collective-permute-done | bytes 262176 | tf_op jit(solution)/shard_map/ppermute | solution.py:573
  54.3 10.1 %collective-permute-done.4.refs_5_ = bf16[64,2048]{1,0:T(8,128)(2,1)S(1)} collective-permute-done((bf16[64,2048]{1,0:T(8,128)(2,1)S(1)}, bf16[64,2048]{1,0:T(8,128)(2,1)S(1)}, u32[]{:S(2)}, u32[]{:S(2)}) %collective-permute-start.4) | collective-permute-done | bytes 262176 | tf_op jit(solution)/shard_map/ppermute | solution.py:573
  65.8 7.0 %all-to-all-done.refs_1_.refs_4_ = bf16[8,256,256]{2,1,0:T(8,128)(2,1)S(1)} async-done(((bf16[8,256,256]{2,1,0:T(8,128)(2,1)}), bf16[8,256,256]{2,1,0:T(8,128)(2,1)S(1)}, u32[]{:S(2)}, u32[]{:S(2)}) %all-to-all-start) | async-done | bytes 1048608 | tf_op jit(solution)/shard_map/all_to_all | solution.py:557
  82.6 5.8 %all-to-all-start.1 = ((bf16[8,256,256]{2,1,0:T(8,128)(2,1)}), bf16[8,256,256]{2,1,0:T(8,128)(2,1)}, u32[]{:S(2)}, u32[]{:S(2)}) async-start(bf16[8,256,256]{2,1,0:T(8,128)(2,1)} %copy-done.5), calls=%async_computation.1 | async-start | bytes 2097152 | tf_op jit(solution)/shard_map/all_to_all | solution.py:588
  88.5 16.2 %collective-permute-done.6.refs_2_.refs_3_.refs_4_.refs_1_ = bf16[256,2048]{1,0:T(8,128)(2,1)} collective-permute-done((bf16[256,2048]{1,0:T(8,128)(2,1)S(1)}, bf16[256,2048]{1,0:T(8,128)(2,1)}, u32[]{:S(2)}, u32[]{:S(2)}) %collective-permute-start.6) | collective-permute-done | bytes 1048608 | tf_op jit(solution)/shard_map/ppermute | solution.py:502
  109.8 5.7 %shard_map.100.refs_0_ = bf16[1024,512]{1,0:T(8,128)(2,1)S(1)} custom-call(s32[8]{0:T(128)S(1)} %concatenate.41.index_ref, bf16[1024,512]{1,0:T(8,128)(2,1)S(1)} %shard_map.99.refs_0_, bf16[256,2048]{1,0:T(8,128)(2,1)S(1)} %shard_map.97.refs_0_.refs_1_.refs_2_.refs_3_, bf16[256,2048]{1,0:T(8,128)(2,1)} %collective-permute-done.6.refs_2_.refs_3_.refs_4_.refs_1_, ...), custom_call_target="tpu_custom_call" | custom-call | tf_op jit(solution)/shard_map/pallas_call | solution.py:418
  120.1 20.5 %shard_map.102 = (bf16[2048,256]{1,0:T(8,128)(2,1)S(1)}, bf16[2,2048,256]{2,1,0:T(8,128)(2,1)}) custom-call(s32[1]{0:T(128)} %constant.368.clone.1.index_ref, bf16[1024,512]{1,0:T(8,128)(2,1)S(1)} %shard_map.100.refs_0_, bf16[2048,2048]{1,0:T(8,128)(2,1)} %constant.370.clone.refs_1_, bf16[2048,2048]{1,0:T(8,128)(2,1)} %constant.371.clone.refs_2_, ...), custom_call_target="tpu_custom_call" | custom-call | tf_op jit(solution)/shard_map/pallas_call | solution.py:121
  142.9 6.0 %shard_map.103.refs_0_ = bf16[1024,512]{1,0:T(8,128)(2,1)S(1)} custom-call(s32[8]{0:T(128)S(1)} %concatenate.40.index_ref, bf16[2,2048,256]{2,1,0:T(8,128)(2,1)} %get-tuple-element.13.refs_0_.refs_3_, bf16[1024,512]{1,0:T(8,128)(2,1)} %collective-permute-done.10.refs_1_.refs_8_.refs_6_.refs_7_, ...), custom_call_target="tpu_custom_call" | custom-call | tf_op jit(solution)/shard_map/pallas_call | solution.py:418
  148.9 6.6 %collective-permute-done.12.refs_2_ = bf16[4,256,256]{2,1,0:T(8,128)(2,1)S(1)} collective-permute-done((bf16[4,256,256]{2,1,0:T(8,128)(2,1)}, bf16[4,256,256]{2,1,0:T(8,128)(2,1)S(1)}, u32[]{:S(2)}, u32[]{:S(2)}) %collective-permute-start.12) | collective-permute-done | bytes 524320 | tf_op jit(solution)/shard_map/ppermute | solution.py:502
  161.0 22.0 %collective-permute-done.9.refs_2_.refs_5_.refs_3_.refs_4_ = bf16[1024,512]{1,0:T(8,128)(2,1)S(1)} collective-permute-done((bf16[1024,512]{1,0:T(8,128)(2,1)S(1)}, bf16[1024,512]{1,0:T(8,128)(2,1)S(1)}, u32[]{:S(2)}, u32[]{:S(2)}) %collective-permute-start.9) | collective-permute-done | bytes 1048608 | tf_op jit(solution)/shard_map/ppermute | solution.py:502
  183.0 19.4 %collective-permute-done.13.refs_9_ = bf16[1024,512]{1,0:T(8,128)(2,1)} collective-permute-done((bf16[1024,512]{1,0:T(8,128)(2,1)}, bf16[1024,512]{1,0:T(8,128)(2,1)}, u32[]{:S(2)}, u32[]{:S(2)}) %collective-permute-start.13) | collective-permute-done | bytes 1048608 | tf_op jit(solution)/shard_map/ppermute | solution.py:502
  203.4 6.7 %shard_map.105 = bf16[1024,512]{1,0:T(8,128)(2,1)} custom-call(s32[8]{0:T(128)S(1)} %concatenate.38.index_ref, bf16[512,512]{1,0:T(8,128)(2,1)} %get-tuple-element.15.refs_0_, bf16[512,512]{1,0:T(8,128)(2,1)S(1)} %copy-done.25, bf16[1024,512]{1,0:T(8,128)(2,1)S(1)} %collective-permute-done.9.refs_2_.refs_5_.refs_3_.refs_4_, ...), custom_call_target="tpu_custom_call" | custom-call | tf_op jit(solution)/shard_map/pallas_call | solution.py:418
  210.1 15.9 %collective-permute-start.14 = (bf16[1024,512]{1,0:T(8,128)(2,1)}, bf16[1024,512]{1,0:T(8,128)(2,1)}, u32[]{:S(2)}, u32[]{:S(2)}) collective-permute-start(bf16[1024,512]{1,0:T(8,128)(2,1)} %shard_map.105), channel_id=1, source_target_pairs={{0,8},{8,16},{16,24},{24,0},{1,9},{9,17},{17,25},{25,1},{2,10},{10... | collective-permute-start | bytes 3145736 | tf_op jit(solution)/shard_map/ppermute | solution.py:502
  226.3 21.7 %collective-permute-done.14.refs_6_ = bf16[1024,512]{1,0:T(8,128)(2,1)} collective-permute-done((bf16[1024,512]{1,0:T(8,128)(2,1)}, bf16[1024,512]{1,0:T(8,128)(2,1)}, u32[]{:S(2)}, u32[]{:S(2)}) %collective-permute-start.14) | collective-permute-done | bytes 1048608 | tf_op jit(solution)/shard_map/ppermute | solution.py:502
  248.0 6.0 %shard_map.106.refs_0_ = bf16[2,1024,256]{2,1,0:T(8,128)(2,1)S(1)} custom-call(s32[8]{0:T(128)S(1)} %concatenate.37.index_ref, bf16[256,2048]{1,0:T(8,128)(2,1)S(1)} %shard_map.97.refs_0_.refs_1_.refs_2_.refs_3_, bf16[256,2048]{1,0:T(8,128)(2,1)} %collective-permute-done.6.refs_2_.refs_3_.refs_4_.refs_1_, ...), custom_call_target="tpu_custom_call" | custom-call | tf_op jit(solution)/shard_map/pallas_call | solution.py:418
  254.0 8.8 %shard_map.107 = (bf16[2,256,1024]{2,1,0:T(8,128)(2,1)S(1)}, bf16[2,256,1024]{2,1,0:T(8,128)(2,1)S(1)}) custom-call(s32[4]{0:T(128)S(1)} %pad_add_fusion.1.index_ref, bf16[2,1024,256]{2,1,0:T(8,128)(2,1)S(1)} %shard_map.106.refs_0_, bf16[4,512,512]{2,1,0:T(8,128)(2,1)} %bitcast.112, bf16[1024,2048]{1,0:T(8,128)(2,1)} %refs_3_.1, ...), custom_call_target="tpu_custom_call" | custom-call | tf_op jit(solution)/shard_map/pallas_call | solution.py:482
  267.4 11.1 %collective-permute-done.16.refs_5_ = bf16[1024,256]{1,0:T(8,128)(2,1)S(1)} collective-permute-done((bf16[1024,256]{1,0:T(8,128)(2,1)}, bf16[1024,256]{1,0:T(8,128)(2,1)S(1)}, u32[]{:S(2)}, u32[]{:S(2)}) %collective-permute-start.16) | collective-permute-done | bytes 524320 | tf_op jit(solution)/shard_map/ppermute | solution.py:502
  280.1 17.4 %shard_map.108 = bf16[2048,256]{1,0:T(8,128)(2,1)} custom-call(s32[2,16]{1,0:T(2,128)S(1)} %pad_add_fusion.index_ref, bf16[2,2,128,1024]{3,2,1,0:T(8,128)(2,1)S(1)} %bitcast.103, bf16[2048,2048]{1,0:T(8,128)(2,1)} %constant.370.clone.refs_1_, bf16[2048,2048]{1,0:T(8,128)(2,1)} %constant.371.clone.refs_2_, bf16[2,2048,256]{2,1,0:T(8,128)(2,1)S(1)} %copy-done.12, ...), custom_call_target="tpu_custom_call" | custom-call | tf_op jit(solution)/shard_map/pallas_call | solution.py:181
  298.7 9.5 %shard_map.110 = (bf16[2,256,1024]{2,1,0:T(8,128)(2,1)S(1)}, bf16[2,256,1024]{2,1,0:T(8,128)(2,1)}) custom-call(s32[4]{0:T(128)S(1)} %pad_add_fusion.1.index_ref, bf16[8,256,256]{2,1,0:T(8,128)(2,1)} %bitcast.45.refs_0_, bf16[2,4,32,1024]{3,2,1,0:T(8,128)(2,1)S(1)} %bitcast.105, bf16[4,512,512]{2,1,0:T(8,128)(2,1)} %bitcast.111, bf16[1024,2048]{1,0:T(8,128)(2,1)} %refs_3_.1, ...), custom_call_target="tpu_custom_call" | custom-call | tf_op jit(solution)/shard_map/pallas_call | solution.py:482
  309.2 16.3 %all-to-all-start.2 = ((bf16[8,256,256]{2,1,0:T(8,128)(2,1)}), bf16[8,256,256]{2,1,0:T(8,128)(2,1)S(1)}, u32[]{:S(2)}, u32[]{:S(2)}) async-start(bf16[8,256,256]{2,1,0:T(8,128)(2,1)} %bitcast.45.refs_0_), calls=%async_computation.2 | async-start | bytes 2097152 | tf_op jit(solution)/shard_map/all_to_all | solution.py:643
  340.2 6.1 %collective-permute-done.23 = bf16[2,128,1024]{2,1,0:T(8,128)(2,1)} collective-permute-done((bf16[2,128,1024]{2,1,0:T(8,128)(2,1)}, bf16[2,128,1024]{2,1,0:T(8,128)(2,1)}, u32[]{:S(2)}, u32[]{:S(2)}) %collective-permute-start.23) | collective-permute-done | bytes 524320 | tf_op jit(solution)/shard_map/ppermute | solution.py:502
  351.3 14.0 %collective-permute-done.18.refs_0_ = bf16[2,32,1024]{2,1,0:T(8,128)(2,1)S(1)} collective-permute-done((bf16[2,32,1024]{2,1,0:T(8,128)(2,1)S(1)}, bf16[2,32,1024]{2,1,0:T(8,128)(2,1)S(1)}, u32[]{:S(2)}, u32[]{:S(2)}) %collective-permute-start.18) | collective-permute-done | bytes 131104 | tf_op jit(solution)/shard_map/ppermute | solution.py:656
  (158 shorter events, 91.0 us)
Async XLA Ops:
  14.0 59.8 %collective-permute-start = (bf16[1024,1024]{1,0:T(8,128)(2,1)}, bf16[1024,1024]{1,0:T(8,128)(2,1)S(1)}, u32[]{:S(2)}, u32[]{:S(2)}) collective-permute-start(bf16[1024,1024]{1,0:T(8,128)(2,1)} %shard_map.95.refs_0_), channel_id=1, source_target_pairs={{0,4},{4,0},{1,5},{5,1},{2,6},{6,2},{3,7},{7,3},{8,12},{12,8},{9,1... | collective-permute-start | bytes 6291464 | tf_op jit(solution)/shard_map/ppermute | solution.py:502
  15.5 57.3 %all-to-all-start = ((bf16[8,256,256]{2,1,0:T(8,128)(2,1)}), bf16[8,256,256]{2,1,0:T(8,128)(2,1)S(1)}, u32[]{:S(2)}, u32[]{:S(2)}) async-start(bf16[8,256,256]{2,1,0:T(8,128)(2,1)} %copy-done.11), calls=%async_computation | async-start | bytes 2097152 | tf_op jit(solution)/shard_map/all_to_all | solution.py:557
  36.0 17.6 %collective-permute-start.3 = (bf16[64,2048]{1,0:T(8,128)(2,1)S(1)}, bf16[64,2048]{1,0:T(8,128)(2,1)S(1)}, u32[]{:S(2)}, u32[]{:S(2)}) collective-permute-start(bf16[64,2048]{1,0:T(8,128)(2,1)S(1)} %get-tuple-element.29), channel_id=1, source_target_pairs={{0,1},{1,9},{2,3},{3,11},{8,16},{9,24},{10,18},{11,26},{16,17},{17... | collective-permute-start | bytes 786440 | tf_op jit(solution)/shard_map/ppermute | solution.py:573
  39.2 25.2 %collective-permute-start.4 = (bf16[64,2048]{1,0:T(8,128)(2,1)S(1)}, bf16[64,2048]{1,0:T(8,128)(2,1)S(1)}, u32[]{:S(2)}, u32[]{:S(2)}) collective-permute-start(bf16[64,2048]{1,0:T(8,128)(2,1)S(1)} %get-tuple-element.30), channel_id=1, source_target_pairs={{0,16},{1,24},{2,18},{3,26},{8,17},{9,25},{10,19},{11,27},{16,0},{... | collective-permute-start | bytes 786440 | tf_op jit(solution)/shard_map/ppermute | solution.py:573
  41.5 23.5 %collective-permute-start.5 = (bf16[64,2048]{1,0:T(8,128)(2,1)S(1)}, bf16[64,2048]{1,0:T(8,128)(2,1)S(1)}, u32[]{:S(2)}, u32[]{:S(2)}) collective-permute-start(bf16[64,2048]{1,0:T(8,128)(2,1)S(1)} %get-tuple-element.27), channel_id=1, source_target_pairs={{0,17},{1,25},{2,19},{3,27},{8,0},{9,8},{10,2},{11,10},{16,1},{17,... | collective-permute-start | bytes 786440 | tf_op jit(solution)/shard_map/ppermute | solution.py:573
  80.5 24.2 %collective-permute-start.6 = (bf16[256,2048]{1,0:T(8,128)(2,1)S(1)}, bf16[256,2048]{1,0:T(8,128)(2,1)}, u32[]{:S(2)}, u32[]{:S(2)}) collective-permute-start(bf16[256,2048]{1,0:T(8,128)(2,1)S(1)} %shard_map.97.refs_0_.refs_1_.refs_2_.refs_3_), channel_id=1, source_target_pairs={{0,2},{2,0},{1,3},{3,1},{4,6},{6,4},{5,7},{7,5},{8,10},{10,8},{9,1... | collective-permute-start | bytes 3145736 | tf_op jit(solution)/shard_map/ppermute | solution.py:502
  82.6 36.3 %all-to-all-start.1 = ((bf16[8,256,256]{2,1,0:T(8,128)(2,1)}), bf16[8,256,256]{2,1,0:T(8,128)(2,1)}, u32[]{:S(2)}, u32[]{:S(2)}) async-start(bf16[8,256,256]{2,1,0:T(8,128)(2,1)} %copy-done.5), calls=%async_computation.1 | async-start | bytes 2097152 | tf_op jit(solution)/shard_map/all_to_all | solution.py:588
  88.4 165.6 %all-gather.5.cloned.1.call-start = ((), (), s32[]{:S(2)}) async-start(), calls=%async_computation.3 | async-start | bytes 2621440 | tf_op jit(solution)/shard_map/all_gather | solution.py:630
  88.4 21.4 %collective-permute-start.7 = (bf16[256,2048]{1,0:T(8,128)(2,1)S(1)}, bf16[256,2048]{1,0:T(8,128)(2,1)}, u32[]{:S(2)}, u32[]{:S(2)}) collective-permute-start(bf16[256,2048]{1,0:T(8,128)(2,1)S(1)} %shard_map.97.refs_0_.refs_1_.refs_2_.refs_3_), channel_id=1, source_target_pairs={{0,1},{1,0},{2,3},{3,2},{4,5},{5,4},{6,7},{7,6},{8,9},{9,8},{10,11... | collective-permute-start | bytes 3145736 | tf_op jit(solution)/shard_map/ppermute | solution.py:502
  107.0 35.2 %collective-permute-start.10 = (bf16[1024,512]{1,0:T(8,128)(2,1)}, bf16[1024,512]{1,0:T(8,128)(2,1)}, u32[]{:S(2)}, u32[]{:S(2)}) collective-permute-start(bf16[1024,512]{1,0:T(8,128)(2,1)} %shard_map.98.refs_0_), channel_id=1, source_target_pairs={{0,4},{4,0},{1,5},{5,1},{2,6},{6,2},{3,7},{7,3},{8,12},{12,8},{9,1... | collective-permute-start | bytes 3145736 | tf_op jit(solution)/shard_map/ppermute | solution.py:502
  115.6 27.3 %collective-permute-start.11 = (bf16[1024,512]{1,0:T(8,128)(2,1)S(1)}, bf16[1024,512]{1,0:T(8,128)(2,1)}, u32[]{:S(2)}, u32[]{:S(2)}) collective-permute-start(bf16[1024,512]{1,0:T(8,128)(2,1)S(1)} %shard_map.100.refs_0_), channel_id=1, source_target_pairs={{0,8},{8,16},{16,24},{24,0},{1,9},{9,17},{17,25},{25,1},{2,10},{10... | collective-permute-start | bytes 3145736 | tf_op jit(solution)/shard_map/ppermute | solution.py:502
  158.7 140.0 %all-gather.7.cloned.1.call-start = ((), (), s32[]{:S(2)}) async-start(), calls=%async_computation.4 | async-start | bytes 2621440 | tf_op jit(solution)/shard_map/all_gather | solution.py:630
  158.8 24.2 %collective-permute-start.9 = (bf16[1024,512]{1,0:T(8,128)(2,1)S(1)}, bf16[1024,512]{1,0:T(8,128)(2,1)S(1)}, u32[]{:S(2)}, u32[]{:S(2)}) collective-permute-start(bf16[1024,512]{1,0:T(8,128)(2,1)S(1)} %copy-done.14), channel_id=1, source_target_pairs={{0,4},{4,0},{1,5},{5,1},{2,6},{6,2},{3,7},{7,3},{8,12},{12,8},{9,1... | collective-permute-start | bytes 3145736 | tf_op jit(solution)/shard_map/ppermute | solution.py:502
  159.4 43.0 %collective-permute-start.13 = (bf16[1024,512]{1,0:T(8,128)(2,1)}, bf16[1024,512]{1,0:T(8,128)(2,1)}, u32[]{:S(2)}, u32[]{:S(2)}) collective-permute-start(bf16[1024,512]{1,0:T(8,128)(2,1)} %copy-done.15), channel_id=1, source_target_pairs={{0,8},{8,16},{16,24},{24,0},{1,9},{9,17},{17,25},{25,1},{2,10},{10... | collective-permute-start | bytes 3145736 | tf_op jit(solution)/shard_map/ppermute | solution.py:502
  210.1 37.9 %collective-permute-start.14 = (bf16[1024,512]{1,0:T(8,128)(2,1)}, bf16[1024,512]{1,0:T(8,128)(2,1)}, u32[]{:S(2)}, u32[]{:S(2)}) collective-permute-start(bf16[1024,512]{1,0:T(8,128)(2,1)} %shard_map.105), channel_id=1, source_target_pairs={{0,8},{8,16},{16,24},{24,0},{1,9},{9,17},{17,25},{25,1},{2,10},{10... | collective-permute-start | bytes 3145736 | tf_op jit(solution)/shard_map/ppermute | solution.py:502
  266.8 30.7 %collective-permute-start.17 = (bf16[2,128,1024]{2,1,0:T(8,128)(2,1)}, bf16[2,128,1024]{2,1,0:T(8,128)(2,1)}, u32[]{:S(2)}, u32[]{:S(2)}) collective-permute-start(bf16[2,128,1024]{2,1,0:T(8,128)(2,1)} %slice_bitcast_fusion.2), channel_id=1, source_target_pairs={{0,2},{2,0},{1,3},{3,1},{4,6},{6,4},{5,7},{7,5},{8,10},{10,8},{9,1... | collective-permute-start | bytes 1572872 | tf_op jit(solution)/shard_map/ppermute | solution.py:502
  309.2 16.3 %collective-permute-start.22 = (bf16[2,256,1024]{2,1,0:T(8,128)(2,1)}, bf16[2,256,1024]{2,1,0:T(8,128)(2,1)}, u32[]{:S(2)}, u32[]{:S(2)}) collective-permute-start(bf16[2,256,1024]{2,1,0:T(8,128)(2,1)} %get-tuple-element.22), channel_id=1, source_target_pairs={{0,1},{1,0},{2,3},{3,2},{4,5},{5,4},{6,7},{7,6},{8,9},{9,8},{10,11... | collective-permute-start | bytes 3145736 | tf_op jit(solution)/shard_map/ppermute | solution.py:502
  309.2 57.2 %all-to-all-start.2 = ((bf16[8,256,256]{2,1,0:T(8,128)(2,1)}), bf16[8,256,256]{2,1,0:T(8,128)(2,1)S(1)}, u32[]{:S(2)}, u32[]{:S(2)}) async-start(bf16[8,256,256]{2,1,0:T(8,128)(2,1)} %bitcast.45.refs_0_), calls=%async_computation.2 | async-start | bytes 2097152 | tf_op jit(solution)/shard_map/all_to_all | solution.py:643
  329.0 17.3 %collective-permute-start.23 = (bf16[2,128,1024]{2,1,0:T(8,128)(2,1)}, bf16[2,128,1024]{2,1,0:T(8,128)(2,1)}, u32[]{:S(2)}, u32[]{:S(2)}) collective-permute-start(bf16[2,128,1024]{2,1,0:T(8,128)(2,1)} %slice_bitcast_fusion), channel_id=1, source_target_pairs={{0,2},{2,0},{1,3},{3,1},{4,6},{6,4},{5,7},{7,5},{8,10},{10,8},{9,1... | collective-permute-start | bytes 1572872 | tf_op jit(solution)/shard_map/ppermute | solution.py:502
  331.6 33.7 %collective-permute-start.18 = (bf16[2,32,1024]{2,1,0:T(8,128)(2,1)S(1)}, bf16[2,32,1024]{2,1,0:T(8,128)(2,1)S(1)}, u32[]{:S(2)}, u32[]{:S(2)}) collective-permute-start(bf16[2,32,1024]{2,1,0:T(8,128)(2,1)S(1)} %get-tuple-element.40), channel_id=1, source_target_pairs={{0,0},{8,1},{16,2},{24,3},{1,8},{9,9},{17,10},{25,11},{2,16},{10,1... | collective-permute-start | bytes 393224 | tf_op jit(solution)/shard_map/ppermute | solution.py:656
  336.1 30.2 %collective-permute-start.19 = (bf16[2,32,1024]{2,1,0:T(8,128)(2,1)S(1)}, bf16[2,32,1024]{2,1,0:T(8,128)(2,1)S(1)}, u32[]{:S(2)}, u32[]{:S(2)}) collective-permute-start(bf16[2,32,1024]{2,1,0:T(8,128)(2,1)S(1)} %get-tuple-element.39), channel_id=1, source_target_pairs={{1,0},{9,1},{17,2},{25,3},{2,8},{10,9},{18,10},{26,11},{3,16},{11,... | collective-permute-start | bytes 393224 | tf_op jit(solution)/shard_map/ppermute | solution.py:656
  336.2 30.2 %collective-permute-start.20 = (bf16[2,32,1024]{2,1,0:T(8,128)(2,1)S(1)}, bf16[2,32,1024]{2,1,0:T(8,128)(2,1)S(1)}, u32[]{:S(2)}, u32[]{:S(2)}) collective-permute-start(bf16[2,32,1024]{2,1,0:T(8,128)(2,1)S(1)} %get-tuple-element.38), channel_id=1, source_target_pairs={{2,0},{10,1},{18,2},{26,3},{3,8},{11,9},{19,10},{27,11},{0,16},{8,... | collective-permute-start | bytes 393224 | tf_op jit(solution)/shard_map/ppermute | solution.py:656
  338.4 31.3 %collective-permute-start.21 = (bf16[2,32,1024]{2,1,0:T(8,128)(2,1)}, bf16[2,32,1024]{2,1,0:T(8,128)(2,1)}, u32[]{:S(2)}, u32[]{:S(2)}) collective-permute-start(bf16[2,32,1024]{2,1,0:T(8,128)(2,1)} %get-tuple-element.37), channel_id=1, source_target_pairs={{3,0},{11,1},{19,2},{27,3},{0,8},{8,9},{16,10},{24,11},{1,16},{9,1... | collective-permute-start | bytes 393224 | tf_op jit(solution)/shard_map/ppermute | solution.py:656
  348.6 25.3 %collective-permute-start.24 = (bf16[2,32,1024]{2,1,0:T(8,128)(2,1)}, bf16[2,32,1024]{2,1,0:T(8,128)(2,1)}, u32[]{:S(2)}, u32[]{:S(2)}) collective-permute-start(bf16[2,32,1024]{2,1,0:T(8,128)(2,1)} %get-tuple-element.36), channel_id=1, source_target_pairs={{0,0},{8,1},{16,2},{24,3},{1,8},{9,9},{17,10},{25,11},{2,16},{10,1... | collective-permute-start | bytes 393224 | tf_op jit(solution)/shard_map/ppermute | solution.py:656
  (44 other events, 363.0 us)
Sparse Core Ops, SparseCore 0:
  158.8 60.9 all-gather.4
  226.2 49.9 all-gather.6

commit v5 on v4

--- a/solution.py
+++ b/solution.py
@@ -629,12 +629,16 @@
             )
             gathered = [lax.all_gather(half, "outer", axis=0, tiled=False) for half in arranged]
             waits = list(arranged) + arrivals[-1]
+        if s == outer - 1:
+            first_shares = shares(gathered[0], in_weight, received, jnp.stack(chunks), near, [running])
+            waits = [first_shares[0]]
     value_parts = [running[0]] + [shifted(running[i], "inner", i) for i in range(1, inner)]
 
     sent_back = []
-    waits = [running]
     for at, half in enumerate(gathered):
-        by_near = shares(half, in_weight, received, jnp.stack(chunks), near, waits)
+        by_near = first_shares
+        if at > 0:
+            by_near = shares(half, in_weight, received, jnp.stack(chunks), near, waits)
         total = by_near[0].astype(WIDE) + sum(shifted(by_near[n], "near", n).astype(WIDE) for n in range(1, near))
         total = total.astype(SHORT).reshape(inner, far, outer * half_rows, depth)
         if at == 0:

time: 387 us -> 387 us (level)
  waiting for transfers between devices: 167 us -> 163 us
  transfers between devices with their start and end apart: 33 -> 33, of which waited for: 18 -> 17; matrix products, arithmetic and copies ran while one was open for 4% -> 4% of each run, Pallas kernels for 20% -> 21%
where the time goes in v5:
time: 387 us; the launch traced here: 386 us
  waiting for transfers between devices  163 us (42%)
  Pallas kernels  95.8 us (25%)
  starting transfers between devices  73.2 us (19%)
  local copies, waits for them, and re-layouts  31.2 us (8%)
  between operations  14.4 us (4%)
  other arithmetic  7.81 us (2%)
    ppermute x16, waiting for transfers between devices, shifted(): lax.ppermute(array, axis, [(at, (at + shift) % size) for at in range(size)])  113 us
    ppermute x16, starting transfers between devices, shifted(): lax.ppermute(array, axis, [(at, (at + shift) % size) for at in range(size)])  26.6 us
    pallas_call x4, Pallas kernels, product(): pl.pallas_call(waiting(functools.partial(product_kernel, (inner, outer, l...  24.4 us
    unnamed x70, local copies, waits for them, and re-layouts  22.7 us
    ppermute x8, waiting for transfers between devices, per_device(): back.append(lax.ppermute(pick(total, (at_tp - step) % tp), cell, pairs))  22.2 us
    pallas_call x1, Pallas kernels, correlate(): pl.pallas_call(waiting(correlate_kernel, len(waits)), grid=(2, steps), in...  20.5 us
    ppermute x4, waiting for transfers between devices, per_device(): moved.append(lax.ppermute(part.reshape(fine_rows, columns), cell, pairs))  20.5 us
    pallas_call x2, Pallas kernels, shares(): pl.pallas_call(waiting(functools.partial(shares_kernel, (outer, inner, ne...  19.3 us
  transfers between devices with their start and end apart: 33, of which 17 were waited for; matrix products, arithmetic and copies ran while one was open for 4% of the time, Pallas kernels for 21%

profile of v5, /device:TPU:4, one launch (start us, length us, event | category | flops | bytes accessed | tf_op | source)
XLA Modules:
  0.0 385.7 jit_solution(5847383387570476789)
XLA Ops:
  20.9 12.9 %collective-permute-done.1 = bf16[128,2048]{1,0:T(8,128)(2,1)} collective-permute-done((bf16[128,2048]{1,0:T(8,128)(2,1)}, bf16[128,2048]{1,0:T(8,128)(2,1)}, u32[]{:S(2)}, u32[]{:S(2)}) %collective-permute-start.1) | collective-permute-done | bytes 524320 | tf_op jit(solution)/shard_map/ppermute | solution.py:502
  43.2 10.4 %collective-permute-done.3.refs_4_ = bf16[64,2048]{1,0:T(8,128)(2,1)S(1)} collective-permute-done((bf16[64,2048]{1,0:T(8,128)(2,1)S(1)}, bf16[64,2048]{1,0:T(8,128)(2,1)S(1)}, u32[]{:S(2)}, u32[]{:S(2)}) %collective-permute-start.3) | collective-permute-done | bytes 262176 | tf_op jit(solution)/shard_map/ppermute | solution.py:573
  54.3 10.1 %collective-permute-done.4.refs_5_ = bf16[64,2048]{1,0:T(8,128)(2,1)S(1)} collective-permute-done((bf16[64,2048]{1,0:T(8,128)(2,1)S(1)}, bf16[64,2048]{1,0:T(8,128)(2,1)S(1)}, u32[]{:S(2)}, u32[]{:S(2)}) %collective-permute-start.4) | collective-permute-done | bytes 262176 | tf_op jit(solution)/shard_map/ppermute | solution.py:573
  65.8 7.0 %all-to-all-done.refs_1_.refs_4_ = bf16[8,256,256]{2,1,0:T(8,128)(2,1)S(1)} async-done(((bf16[8,256,256]{2,1,0:T(8,128)(2,1)}), bf16[8,256,256]{2,1,0:T(8,128)(2,1)S(1)}, u32[]{:S(2)}, u32[]{:S(2)}) %all-to-all-start) | async-done | bytes 1048608 | tf_op jit(solution)/shard_map/all_to_all | solution.py:557
  82.6 5.8 %all-to-all-start.1 = ((bf16[8,256,256]{2,1,0:T(8,128)(2,1)}), bf16[8,256,256]{2,1,0:T(8,128)(2,1)}, u32[]{:S(2)}, u32[]{:S(2)}) async-start(bf16[8,256,256]{2,1,0:T(8,128)(2,1)} %copy-done.5), calls=%async_computation.1 | async-start | bytes 2097152 | tf_op jit(solution)/shard_map/all_to_all | solution.py:588
  88.5 16.2 %collective-permute-done.6.refs_2_.refs_3_.refs_4_ = bf16[256,2048]{1,0:T(8,128)(2,1)} collective-permute-done((bf16[256,2048]{1,0:T(8,128)(2,1)S(1)}, bf16[256,2048]{1,0:T(8,128)(2,1)}, u32[]{:S(2)}, u32[]{:S(2)}) %collective-permute-start.6) | collective-permute-done | bytes 1048608 | tf_op jit(solution)/shard_map/ppermute | solution.py:502
  109.8 5.7 %shard_map.100.refs_0_ = bf16[1024,512]{1,0:T(8,128)(2,1)S(1)} custom-call(s32[8]{0:T(128)S(1)} %concatenate.40.index_ref, bf16[1024,512]{1,0:T(8,128)(2,1)S(1)} %shard_map.99.refs_0_, bf16[256,2048]{1,0:T(8,128)(2,1)S(1)} %shard_map.97.refs_0_.refs_1_.refs_2_.refs_3_, bf16[256,2048]{1,0:T(8,128)(2,1)} %collective-permute-done.6.refs_2_.refs_3_.refs_4_, ...), custom_call_target="tpu_custom_call" | custom-call | tf_op jit(solution)/shard_map/pallas_call | solution.py:418
  120.1 20.5 %shard_map.102 = (bf16[2048,256]{1,0:T(8,128)(2,1)S(1)}, bf16[2,2048,256]{2,1,0:T(8,128)(2,1)}) custom-call(s32[1]{0:T(128)} %constant.368.clone.1.index_ref, bf16[1024,512]{1,0:T(8,128)(2,1)S(1)} %shard_map.100.refs_0_, bf16[2048,2048]{1,0:T(8,128)(2,1)} %constant.370.clone.refs_1_, bf16[2048,2048]{1,0:T(8,128)(2,1)} %constant.371.clone.refs_2_, ...), custom_call_target="tpu_custom_call" | custom-call | tf_op jit(solution)/shard_map/pallas_call | solution.py:121
  142.9 6.0 %shard_map.103.refs_0_ = bf16[1024,512]{1,0:T(8,128)(2,1)S(1)} custom-call(s32[8]{0:T(128)S(1)} %concatenate.39.index_ref, bf16[2,2048,256]{2,1,0:T(8,128)(2,1)} %get-tuple-element.13.refs_0_.refs_3_, bf16[1024,512]{1,0:T(8,128)(2,1)} %collective-permute-done.9.refs_1_.refs_8_.refs_6_.refs_7_, ...), custom_call_target="tpu_custom_call" | custom-call | tf_op jit(solution)/shard_map/pallas_call | solution.py:418
  148.9 6.6 %collective-permute-done.11.refs_2_ = bf16[4,256,256]{2,1,0:T(8,128)(2,1)S(1)} collective-permute-done((bf16[4,256,256]{2,1,0:T(8,128)(2,1)}, bf16[4,256,256]{2,1,0:T(8,128)(2,1)S(1)}, u32[]{:S(2)}, u32[]{:S(2)}) %collective-permute-start.11) | collective-permute-done | bytes 524320 | tf_op jit(solution)/shard_map/ppermute | solution.py:502
  161.0 21.9 %collective-permute-done.12.refs_2_.refs_3_.refs_6_.refs_4_ = bf16[1024,512]{1,0:T(8,128)(2,1)S(1)} collective-permute-done((bf16[1024,512]{1,0:T(8,128)(2,1)S(1)}, bf16[1024,512]{1,0:T(8,128)(2,1)S(1)}, u32[]{:S(2)}, u32[]{:S(2)}) %collective-permute-start.12) | collective-permute-done | bytes 1048608 | tf_op jit(solution)/shard_map/ppermute | solution.py:502
  183.0 19.4 %collective-permute-done.13.refs_9_ = bf16[1024,512]{1,0:T(8,128)(2,1)} collective-permute-done((bf16[1024,512]{1,0:T(8,128)(2,1)}, bf16[1024,512]{1,0:T(8,128)(2,1)}, u32[]{:S(2)}, u32[]{:S(2)}) %collective-permute-start.13) | collective-permute-done | bytes 1048608 | tf_op jit(solution)/shard_map/ppermute | solution.py:502
  203.4 6.7 %shard_map.105.refs_0_ = bf16[1024,512]{1,0:T(8,128)(2,1)} custom-call(s32[8]{0:T(128)S(1)} %concatenate.37.index_ref, bf16[512,512]{1,0:T(8,128)(2,1)} %get-tuple-element.15.refs_0_, bf16[512,512]{1,0:T(8,128)(2,1)S(1)} %copy-done.27, bf16[1024,512]{1,0:T(8,128)(2,1)S(1)} %collective-permute-done.12.refs_2_.refs_3_.refs_6_.refs_4_, ...), custom_call_target="tpu_custom_call" | custom-call | tf_op jit(solution)/shard_map/pallas_call | solution.py:418
  210.1 15.9 %collective-permute-start.15 = (bf16[1024,512]{1,0:T(8,128)(2,1)}, bf16[1024,512]{1,0:T(8,128)(2,1)}, u32[]{:S(2)}, u32[]{:S(2)}) collective-permute-start(bf16[1024,512]{1,0:T(8,128)(2,1)} %shard_map.105.refs_0_), channel_id=1, source_target_pairs={{0,8},{8,16},{16,24},{24,0},{1,9},{9,17},{17,25},{25,1},{2,10},{10... | collective-permute-start | bytes 3145736 | tf_op jit(solution)/shard_map/ppermute | solution.py:502
  226.1 9.8 %shard_map.106 = (bf16[2,256,1024]{2,1,0:T(8,128)(2,1)S(1)}, bf16[2,256,1024]{2,1,0:T(8,128)(2,1)}) custom-call(s32[4]{0:T(128)S(1)} %pad_add_fusion.1.index_ref, bf16[1024,512]{1,0:T(8,128)(2,1)} %shard_map.105.refs_0_, bf16[4,512,512]{2,1,0:T(8,128)(2,1)} %bitcast.112, bf16[1024,2048]{1,0:T(8,128)(2,1)} %refs_3_.1, ...), custom_call_target="tpu_custom_call" | custom-call | tf_op jit(solution)/shard_map/pallas_call | solution.py:482
  237.0 24.0 %collective-permute-done.15.refs_7_ = bf16[1024,512]{1,0:T(8,128)(2,1)} collective-permute-done((bf16[1024,512]{1,0:T(8,128)(2,1)}, bf16[1024,512]{1,0:T(8,128)(2,1)}, u32[]{:S(2)}, u32[]{:S(2)}) %collective-permute-start.15) | collective-permute-done | bytes 1048608 | tf_op jit(solution)/shard_map/ppermute | solution.py:502
  262.2 5.9 %shard_map.107 = bf16[2,1024,256]{2,1,0:T(8,128)(2,1)S(1)} custom-call(s32[8]{0:T(128)S(1)} %concatenate.41.index_ref, bf16[2,256,1024]{2,1,0:T(8,128)(2,1)S(1)} %copy-done.16, bf16[256,2048]{1,0:T(8,128)(2,1)S(1)} %shard_map.97.refs_0_.refs_1_.refs_2_.refs_3_, bf16[256,2048]{1,0:T(8,128)(2,1)} %collective-permute-done.6.refs_2_.refs_3_.refs_4_, ...), custom_call_target="tpu_custom_call" | custom-call | tf_op jit(solution)/shard_map/pallas_call | solution.py:418
  273.8 4.9 %collective-permute-done.16.refs_5_ = bf16[1024,256]{1,0:T(8,128)(2,1)} collective-permute-done((bf16[1024,256]{1,0:T(8,128)(2,1)}, bf16[1024,256]{1,0:T(8,128)(2,1)}, u32[]{:S(2)}, u32[]{:S(2)}) %collective-permute-start.16) | collective-permute-done | bytes 524320 | tf_op jit(solution)/shard_map/ppermute | solution.py:502
  279.7 17.5 %shard_map.108 = bf16[2048,256]{1,0:T(8,128)(2,1)} custom-call(s32[2,16]{1,0:T(2,128)S(1)} %pad_add_fusion.index_ref, bf16[2,2,128,1024]{3,2,1,0:T(8,128)(2,1)S(1)} %bitcast.103, bf16[2048,2048]{1,0:T(8,128)(2,1)} %constant.370.clone.refs_1_, bf16[2048,2048]{1,0:T(8,128)(2,1)} %constant.371.clone.refs_2_, bf16[2,2048,256]{2,1,0:T(8,128)(2,1)S(1)} %copy-done.12, ...), custom_call_target="tpu_custom_call" | custom-call | tf_op jit(solution)/shard_map/pallas_call | solution.py:181
  298.6 9.5 %shard_map.110 = (bf16[2,256,1024]{2,1,0:T(8,128)(2,1)S(1)}, bf16[2,256,1024]{2,1,0:T(8,128)(2,1)}) custom-call(s32[4]{0:T(128)S(1)} %pad_add_fusion.1.index_ref, bf16[8,256,256]{2,1,0:T(8,128)(2,1)} %bitcast.45.refs_0_, bf16[2,4,32,1024]{3,2,1,0:T(8,128)(2,1)S(1)} %bitcast.105, bf16[4,512,512]{2,1,0:T(8,128)(2,1)} %bitcast.111, bf16[1024,2048]{1,0:T(8,128)(2,1)} %refs_3_.1, ...), custom_call_target="tpu_custom_call" | custom-call | tf_op jit(solution)/shard_map/pallas_call | solution.py:482
  308.1 18.1 %all-to-all-start.2 = ((bf16[8,256,256]{2,1,0:T(8,128)(2,1)}), bf16[8,256,256]{2,1,0:T(8,128)(2,1)S(1)}, u32[]{:S(2)}, u32[]{:S(2)}) async-start(bf16[8,256,256]{2,1,0:T(8,128)(2,1)} %bitcast.45.refs_0_), calls=%async_computation.2 | async-start | bytes 2097152 | tf_op jit(solution)/shard_map/all_to_all | solution.py:647
  330.1 5.8 %collective-permute-start.18 = (bf16[2,32,1024]{2,1,0:T(8,128)(2,1)S(1)}, bf16[2,32,1024]{2,1,0:T(8,128)(2,1)S(1)}, u32[]{:S(2)}, u32[]{:S(2)}) collective-permute-start(bf16[2,32,1024]{2,1,0:T(8,128)(2,1)S(1)} %get-tuple-element.40), channel_id=1, source_target_pairs={{0,0},{8,1},{16,2},{24,3},{1,8},{9,9},{17,10},{25,11},{2,16},{10,1... | collective-permute-start | bytes 393224 | tf_op jit(solution)/shard_map/ppermute | solution.py:660
  338.6 6.8 %collective-permute-done.23 = bf16[2,128,1024]{2,1,0:T(8,128)(2,1)S(1)} collective-permute-done((bf16[2,128,1024]{2,1,0:T(8,128)(2,1)}, bf16[2,128,1024]{2,1,0:T(8,128)(2,1)S(1)}, u32[]{:S(2)}, u32[]{:S(2)}) %collective-permute-start.23) | collective-permute-done | bytes 524320 | tf_op jit(solution)/shard_map/ppermute | solution.py:502
  350.6 13.9 %collective-permute-done.18.refs_0_ = bf16[2,32,1024]{2,1,0:T(8,128)(2,1)S(1)} collective-permute-done((bf16[2,32,1024]{2,1,0:T(8,128)(2,1)S(1)}, bf16[2,32,1024]{2,1,0:T(8,128)(2,1)S(1)}, u32[]{:S(2)}, u32[]{:S(2)}) %collective-permute-start.18) | collective-permute-done | bytes 131104 | tf_op jit(solution)/shard_map/ppermute | solution.py:660
  (158 shorter events, 89.8 us)
Async XLA Ops:
  14.0 59.8 %collective-permute-start = (bf16[1024,1024]{1,0:T(8,128)(2,1)}, bf16[1024,1024]{1,0:T(8,128)(2,1)S(1)}, u32[]{:S(2)}, u32[]{:S(2)}) collective-permute-start(bf16[1024,1024]{1,0:T(8,128)(2,1)} %shard_map.95.refs_0_), channel_id=1, source_target_pairs={{0,4},{4,0},{1,5},{5,1},{2,6},{6,2},{3,7},{7,3},{8,12},{12,8},{9,1... | collective-permute-start | bytes 6291464 | tf_op jit(solution)/shard_map/ppermute | solution.py:502
  15.5 57.3 %all-to-all-start = ((bf16[8,256,256]{2,1,0:T(8,128)(2,1)}), bf16[8,256,256]{2,1,0:T(8,128)(2,1)S(1)}, u32[]{:S(2)}, u32[]{:S(2)}) async-start(bf16[8,256,256]{2,1,0:T(8,128)(2,1)} %copy-done.11), calls=%async_computation | async-start | bytes 2097152 | tf_op jit(solution)/shard_map/all_to_all | solution.py:557
  36.0 17.6 %collective-permute-start.3 = (bf16[64,2048]{1,0:T(8,128)(2,1)S(1)}, bf16[64,2048]{1,0:T(8,128)(2,1)S(1)}, u32[]{:S(2)}, u32[]{:S(2)}) collective-permute-start(bf16[64,2048]{1,0:T(8,128)(2,1)S(1)} %get-tuple-element.29), channel_id=1, source_target_pairs={{0,1},{1,9},{2,3},{3,11},{8,16},{9,24},{10,18},{11,26},{16,17},{17... | collective-permute-start | bytes 786440 | tf_op jit(solution)/shard_map/ppermute | solution.py:573
  39.2 25.2 %collective-permute-start.4 = (bf16[64,2048]{1,0:T(8,128)(2,1)S(1)}, bf16[64,2048]{1,0:T(8,128)(2,1)S(1)}, u32[]{:S(2)}, u32[]{:S(2)}) collective-permute-start(bf16[64,2048]{1,0:T(8,128)(2,1)S(1)} %get-tuple-element.30), channel_id=1, source_target_pairs={{0,16},{1,24},{2,18},{3,26},{8,17},{9,25},{10,19},{11,27},{16,0},{... | collective-permute-start | bytes 786440 | tf_op jit(solution)/shard_map/ppermute | solution.py:573
  41.5 23.5 %collective-permute-start.5 = (bf16[64,2048]{1,0:T(8,128)(2,1)S(1)}, bf16[64,2048]{1,0:T(8,128)(2,1)S(1)}, u32[]{:S(2)}, u32[]{:S(2)}) collective-permute-start(bf16[64,2048]{1,0:T(8,128)(2,1)S(1)} %get-tuple-element.27), channel_id=1, source_target_pairs={{0,17},{1,25},{2,19},{3,27},{8,0},{9,8},{10,2},{11,10},{16,1},{17,... | collective-permute-start | bytes 786440 | tf_op jit(solution)/shard_map/ppermute | solution.py:573
  80.5 24.2 %collective-permute-start.6 = (bf16[256,2048]{1,0:T(8,128)(2,1)S(1)}, bf16[256,2048]{1,0:T(8,128)(2,1)}, u32[]{:S(2)}, u32[]{:S(2)}) collective-permute-start(bf16[256,2048]{1,0:T(8,128)(2,1)S(1)} %shard_map.97.refs_0_.refs_1_.refs_2_.refs_3_), channel_id=1, source_target_pairs={{0,2},{2,0},{1,3},{3,1},{4,6},{6,4},{5,7},{7,5},{8,10},{10,8},{9,1... | collective-permute-start | bytes 3145736 | tf_op jit(solution)/shard_map/ppermute | solution.py:502
  82.6 36.3 %all-to-all-start.1 = ((bf16[8,256,256]{2,1,0:T(8,128)(2,1)}), bf16[8,256,256]{2,1,0:T(8,128)(2,1)}, u32[]{:S(2)}, u32[]{:S(2)}) async-start(bf16[8,256,256]{2,1,0:T(8,128)(2,1)} %copy-done.5), calls=%async_computation.1 | async-start | bytes 2097152 | tf_op jit(solution)/shard_map/all_to_all | solution.py:588
  88.4 137.8 %all-gather.5.cloned.1.call-start = ((), (), s32[]{:S(2)}) async-start(), calls=%async_computation.3 | async-start | bytes 2621440 | tf_op jit(solution)/shard_map/all_gather | solution.py:630
  88.4 21.4 %collective-permute-start.7 = (bf16[256,2048]{1,0:T(8,128)(2,1)S(1)}, bf16[256,2048]{1,0:T(8,128)(2,1)}, u32[]{:S(2)}, u32[]{:S(2)}) collective-permute-start(bf16[256,2048]{1,0:T(8,128)(2,1)S(1)} %shard_map.97.refs_0_.refs_1_.refs_2_.refs_3_), channel_id=1, source_target_pairs={{0,1},{1,0},{2,3},{3,2},{4,5},{5,4},{6,7},{7,6},{8,9},{9,8},{10,11... | collective-permute-start | bytes 3145736 | tf_op jit(solution)/shard_map/ppermute | solution.py:502
  107.0 35.2 %collective-permute-start.9 = (bf16[1024,512]{1,0:T(8,128)(2,1)}, bf16[1024,512]{1,0:T(8,128)(2,1)}, u32[]{:S(2)}, u32[]{:S(2)}) collective-permute-start(bf16[1024,512]{1,0:T(8,128)(2,1)} %shard_map.98.refs_0_), channel_id=1, source_target_pairs={{0,4},{4,0},{1,5},{5,1},{2,6},{6,2},{3,7},{7,3},{8,12},{12,8},{9,1... | collective-permute-start | bytes 3145736 | tf_op jit(solution)/shard_map/ppermute | solution.py:502
  115.6 27.3 %collective-permute-start.10 = (bf16[1024,512]{1,0:T(8,128)(2,1)S(1)}, bf16[1024,512]{1,0:T(8,128)(2,1)}, u32[]{:S(2)}, u32[]{:S(2)}) collective-permute-start(bf16[1024,512]{1,0:T(8,128)(2,1)S(1)} %shard_map.100.refs_0_), channel_id=1, source_target_pairs={{0,8},{8,16},{16,24},{24,0},{1,9},{9,17},{17,25},{25,1},{2,10},{10... | collective-permute-start | bytes 3145736 | tf_op jit(solution)/shard_map/ppermute | solution.py:502
  158.7 139.9 %all-gather.7.cloned.1.call-start = ((), (), s32[]{:S(2)}) async-start(), calls=%async_computation.4 | async-start | bytes 2621440 | tf_op jit(solution)/shard_map/all_gather | solution.py:630
  158.7 24.2 %collective-permute-start.12 = (bf16[1024,512]{1,0:T(8,128)(2,1)S(1)}, bf16[1024,512]{1,0:T(8,128)(2,1)S(1)}, u32[]{:S(2)}, u32[]{:S(2)}) collective-permute-start(bf16[1024,512]{1,0:T(8,128)(2,1)S(1)} %copy-done.14), channel_id=1, source_target_pairs={{0,4},{4,0},{1,5},{5,1},{2,6},{6,2},{3,7},{7,3},{8,12},{12,8},{9,1... | collective-permute-start | bytes 3145736 | tf_op jit(solution)/shard_map/ppermute | solution.py:502
  159.3 43.0 %collective-permute-start.13 = (bf16[1024,512]{1,0:T(8,128)(2,1)}, bf16[1024,512]{1,0:T(8,128)(2,1)}, u32[]{:S(2)}, u32[]{:S(2)}) collective-permute-start(bf16[1024,512]{1,0:T(8,128)(2,1)} %copy-done.17), channel_id=1, source_target_pairs={{0,8},{8,16},{16,24},{24,0},{1,9},{9,17},{17,25},{25,1},{2,10},{10... | collective-permute-start | bytes 3145736 | tf_op jit(solution)/shard_map/ppermute | solution.py:502
  210.1 50.9 %collective-permute-start.15 = (bf16[1024,512]{1,0:T(8,128)(2,1)}, bf16[1024,512]{1,0:T(8,128)(2,1)}, u32[]{:S(2)}, u32[]{:S(2)}) collective-permute-start(bf16[1024,512]{1,0:T(8,128)(2,1)} %shard_map.105.refs_0_), channel_id=1, source_target_pairs={{0,8},{8,16},{16,24},{24,0},{1,9},{9,17},{17,25},{25,1},{2,10},{10... | collective-permute-start | bytes 3145736 | tf_op jit(solution)/shard_map/ppermute | solution.py:502
  236.9 33.8 %collective-permute-start.14 = (bf16[2,256,1024]{2,1,0:T(8,128)(2,1)}, bf16[2,256,1024]{2,1,0:T(8,128)(2,1)}, u32[]{:S(2)}, u32[]{:S(2)}) collective-permute-start(bf16[2,256,1024]{2,1,0:T(8,128)(2,1)} %get-tuple-element.18), channel_id=1, source_target_pairs={{0,1},{1,0},{2,3},{3,2},{4,5},{5,4},{6,7},{7,6},{8,9},{9,8},{10,11... | collective-permute-start | bytes 3145736 | tf_op jit(solution)/shard_map/ppermute | solution.py:502
  273.2 24.0 %collective-permute-start.17 = (bf16[2,128,1024]{2,1,0:T(8,128)(2,1)}, bf16[2,128,1024]{2,1,0:T(8,128)(2,1)}, u32[]{:S(2)}, u32[]{:S(2)}) collective-permute-start(bf16[2,128,1024]{2,1,0:T(8,128)(2,1)} %slice_bitcast_fusion.2), channel_id=1, source_target_pairs={{0,2},{2,0},{1,3},{3,1},{4,6},{6,4},{5,7},{7,5},{8,10},{10,8},{9,1... | collective-permute-start | bytes 1572872 | tf_op jit(solution)/shard_map/ppermute | solution.py:502
  308.1 18.1 %collective-permute-start.22 = (bf16[2,256,1024]{2,1,0:T(8,128)(2,1)}, bf16[2,256,1024]{2,1,0:T(8,128)(2,1)}, u32[]{:S(2)}, u32[]{:S(2)}) collective-permute-start(bf16[2,256,1024]{2,1,0:T(8,128)(2,1)} %get-tuple-element.22), channel_id=1, source_target_pairs={{0,1},{1,0},{2,3},{3,2},{4,5},{5,4},{6,7},{7,6},{8,9},{9,8},{10,11... | collective-permute-start | bytes 3145736 | tf_op jit(solution)/shard_map/ppermute | solution.py:502
  308.1 57.9 %all-to-all-start.2 = ((bf16[8,256,256]{2,1,0:T(8,128)(2,1)}), bf16[8,256,256]{2,1,0:T(8,128)(2,1)S(1)}, u32[]{:S(2)}, u32[]{:S(2)}) async-start(bf16[8,256,256]{2,1,0:T(8,128)(2,1)} %bitcast.45.refs_0_), calls=%async_computation.2 | async-start | bytes 2097152 | tf_op jit(solution)/shard_map/all_to_all | solution.py:647
  330.1 34.3 %collective-permute-start.18 = (bf16[2,32,1024]{2,1,0:T(8,128)(2,1)S(1)}, bf16[2,32,1024]{2,1,0:T(8,128)(2,1)S(1)}, u32[]{:S(2)}, u32[]{:S(2)}) collective-permute-start(bf16[2,32,1024]{2,1,0:T(8,128)(2,1)S(1)} %get-tuple-element.40), channel_id=1, source_target_pairs={{0,0},{8,1},{16,2},{24,3},{1,8},{9,9},{17,10},{25,11},{2,16},{10,1... | collective-permute-start | bytes 393224 | tf_op jit(solution)/shard_map/ppermute | solution.py:660
  336.0 29.9 %collective-permute-start.19 = (bf16[2,32,1024]{2,1,0:T(8,128)(2,1)S(1)}, bf16[2,32,1024]{2,1,0:T(8,128)(2,1)S(1)}, u32[]{:S(2)}, u32[]{:S(2)}) collective-permute-start(bf16[2,32,1024]{2,1,0:T(8,128)(2,1)S(1)} %get-tuple-element.39), channel_id=1, source_target_pairs={{1,0},{9,1},{17,2},{25,3},{2,8},{10,9},{18,10},{26,11},{3,16},{11,... | collective-permute-start | bytes 393224 | tf_op jit(solution)/shard_map/ppermute | solution.py:660
  336.1 29.8 %collective-permute-start.20 = (bf16[2,32,1024]{2,1,0:T(8,128)(2,1)S(1)}, bf16[2,32,1024]{2,1,0:T(8,128)(2,1)S(1)}, u32[]{:S(2)}, u32[]{:S(2)}) collective-permute-start(bf16[2,32,1024]{2,1,0:T(8,128)(2,1)S(1)} %get-tuple-element.38), channel_id=1, source_target_pairs={{2,0},{10,1},{18,2},{26,3},{3,8},{11,9},{19,10},{27,11},{0,16},{8,... | collective-permute-start | bytes 393224 | tf_op jit(solution)/shard_map/ppermute | solution.py:660
  337.5 32.9 %collective-permute-start.21 = (bf16[2,32,1024]{2,1,0:T(8,128)(2,1)S(1)}, bf16[2,32,1024]{2,1,0:T(8,128)(2,1)S(1)}, u32[]{:S(2)}, u32[]{:S(2)}) collective-permute-start(bf16[2,32,1024]{2,1,0:T(8,128)(2,1)S(1)} %get-tuple-element.37), channel_id=1, source_target_pairs={{3,0},{11,1},{19,2},{27,3},{0,8},{8,9},{16,10},{24,11},{1,16},{9,1... | collective-permute-start | bytes 393224 | tf_op jit(solution)/shard_map/ppermute | solution.py:660
  347.5 25.4 %collective-permute-start.24 = (bf16[2,32,1024]{2,1,0:T(8,128)(2,1)}, bf16[2,32,1024]{2,1,0:T(8,128)(2,1)S(1)}, u32[]{:S(2)}, u32[]{:S(2)}) collective-permute-start(bf16[2,32,1024]{2,1,0:T(8,128)(2,1)} %get-tuple-element.36), channel_id=1, source_target_pairs={{0,0},{8,1},{16,2},{24,3},{1,8},{9,9},{17,10},{25,11},{2,16},{10,1... | collective-permute-start | bytes 393224 | tf_op jit(solution)/shard_map/ppermute | solution.py:660
  (44 other events, 307.9 us)
Sparse Core Ops, SparseCore 0:
  158.8 60.8 all-gather.4
  221.3 54.6 all-gather.6

commit v6 on v3

--- a/solution.py
+++ b/solution.py
@@ -246,7 +246,7 @@
 
 def arrange_kernel(dims, index_ref, *refs):
     outer, inner, far, near, halves, half_rows = dims
-    part_refs, out_refs = refs[:inner], refs[inner:]
+    part_refs, out_ref = refs[:inner], refs[-1]
     channels = part_refs[0].shape[-1]
     tp = far * near
     for s in range(inner):
@@ -257,7 +257,7 @@
                 for h in range(halves):
                     place = (ahead * outer + o) * half_rows
                     piece = part_refs[s][o, aligned(source * halves + h, half_rows)]
-                    out_refs[h][place : place + half_rows, lanes] = piece
+                    out_ref[h, place : place + half_rows, lanes] = piece
 
 
 def arrange(parts, inner_places, sources, dims, waits):
@@ -271,7 +271,7 @@
             slots = lax.dynamic_update_index_in_dim(slots, parts[s], inner_places[s], 0)
         slots = slots.reshape(inner, outer, tp, halves, half_rows, channels).transpose(2, 3, 1, 4, 0, 5)
         slots = jnp.stack([pick(slots, sources[a]) for a in range(tp)])
-        return [slots[:, h].reshape(shape) for h in range(halves)]
+        return jnp.stack([slots[:, h].reshape(shape) for h in range(halves)])
     index = jnp.concatenate([inner_places, sources]).astype(jnp.int32)
     size = math.prod(shape) * 2
     return pl.pallas_call(
@@ -279,8 +279,8 @@
         in_specs=[pl.BlockSpec(memory_space=pltpu.SMEM)]
         + [ANYWHERE] * len(waits)
         + [pl.BlockSpec(memory_space=pltpu.VMEM)] * inner,
-        out_specs=[pl.BlockSpec(memory_space=pltpu.VMEM)] * halves,
-        out_shape=[jax.ShapeDtypeStruct(shape, SHORT)] * halves,
+        out_specs=pl.BlockSpec(memory_space=pltpu.VMEM),
+        out_shape=jax.ShapeDtypeStruct((halves, *shape), SHORT),
         compiler_params=kernel_params(0),
         cost_estimate=NO_COST,
     )(index, *waits, *parts)
@@ -443,25 +443,26 @@
     @pl.when(pl.program_id(0) == 0)
     def _():
         for o in range(outer):
-            plain_ref[:, o * chunk : (o + 1) * chunk] = grad_ref[o]
+            plain_ref[:, o * chunk : (o + 1) * chunk] = grad_ref[o, 0]
 
     for i in range(inner):
         if i == 0:
             total = wide_dot_turned(plain_ref[...], own_ref[...])
         else:
             total = sum(
-                wide_dot_turned(grad_ref[index_ref[s]], received_refs[(i - 1) * outer + s][...]) for s in range(outer)
+                wide_dot_turned(grad_ref[index_ref[s], 0], received_refs[(i - 1) * outer + s][...]) for s in range(outer)
             )
         total = total.astype(SHORT)
         for n in range(near):
             out_refs[n][i] = total[n * size : (n + 1) * size]
 
 
-def shares(grad_values, in_weight, received, chunks, near, waits):
-    outer, rows, chunk = grad_values.shape
+def shares(grad_values, half, in_weight, received, chunks, near, waits):
+    outer, _, rows, chunk = grad_values.shape
     inner = len(received) + 1
     depth, width = in_weight.shape
     if chunk // inner % 128:
+        grad_values = grad_values[:, half]
         plain = grad_values.swapaxes(0, 1).reshape(rows, width)
         totals = [wide_dot_turned(plain, in_weight)] + [
             sum(
@@ -481,7 +482,7 @@
             num_scalar_prefetch=1,
             grid=(depth // block,),
             in_specs=[ANYWHERE] * len(waits)
-            + [pl.BlockSpec((outer, rows, chunk), lambda k, _: (0, 0, 0))]
+            + [pl.BlockSpec((outer, 1, rows, chunk), lambda k, _: (0, half, 0, 0))]
             + [pl.BlockSpec((block, width), lambda k, _: (k, 0))]
             + [pl.BlockSpec((block, chunk), lambda k, _, at=at: (k, at)) for _, at in flat],
             out_specs=[out_spec] * near,
@@ -617,24 +618,23 @@
             arranged = arrange(
                 grad_parts, jnp.stack(back_inner), jnp.stack(sources), (outer, inner, far, near, halves, half_rows), [running]
             )
-            gathered = [lax.all_gather(half, "outer", axis=0, tiled=False) for half in arranged]
-            waits = list(arranged)
+            gathered = lax.all_gather(arranged, "outer", axis=0, tiled=False)
+            waits = [arranged]
     value_parts = [running[0]] + [shifted(running[i], "inner", i) for i in range(1, inner)]
 
+    convolved = convolve(table, spectrum, value_parts, places, []).reshape(ctx_size, rows, channels)
+    exchanged = lax.all_to_all(convolved, ctx, split_axis=0, concat_axis=0, tiled=True)
+
     sent_back = []
-    waits = [running]
-    for at, half in enumerate(gathered):
-        by_near = shares(half, in_weight, received, jnp.stack(chunks), near, waits)
+    waits = [convolved]
+    for half in range(halves):
+        by_near = shares(gathered, half, in_weight, received, jnp.stack(chunks), near, waits)
+        waits = [by_near[0]]
         total = by_near[0].astype(WIDE) + sum(shifted(by_near[n], "near", n).astype(WIDE) for n in range(1, near))
         total = total.astype(SHORT).reshape(inner, far, outer * half_rows, depth)
-        if at == 0:
-            convolved = convolve(table, spectrum, value_parts, places, [total])
-            convolved = convolved.reshape(ctx_size, rows, channels)
-            exchanged = lax.all_to_all(convolved, ctx, split_axis=0, concat_axis=0, tiled=True)
         others = [shifted(total[:, f], "far", f) for f in range(1, far)]
         total = total[:, 0].astype(WIDE) + sum(other.astype(WIDE) for other in others)
         total = total.astype(SHORT).reshape(inner, outer, half_rows, depth)
-        waits = [convolved, total]
         if split == 1:
             total = total.swapaxes(0, 1)
         else:

time: 371 us -> 365 us (0.984)
  waiting for transfers between devices: 180 us -> 167 us
  starting transfers between devices: 49.8 us -> 55.3 us
    ppermute x8, waiting for transfers between devices: 20.7 us -> 4.55 us  [per_device(): back.append(lax.ppermute(pick(total, (at_tp - step) % tp), cell, pairs))]
    ppermute x8, starting transfers between devices: 12 us -> 18 us  [per_device(): back.append(lax.ppermute(pick(total, (at_tp - step) % tp), cell, pairs))]
    all_gather x2 -> x1, waiting for transfers between devices: 14.7 us -> 17.3 us  [per_device(): gathered = lax.all_gather(arranged, 'outer', axis=0, tiled=False)]
    unnamed x32 -> x38, local copies, waits for them, and re-layouts: 10.9 us -> 12.1 us
  transfers between devices with their start and end apart: 31 -> 30, of which waited for: 18 -> 17; matrix products, arithmetic and copies ran while one was open for 4% -> 3% of each run, Pallas kernels for 22% -> 21%
where the time goes in v6:
time: 365 us; the launch traced here: 364 us
  waiting for transfers between devices  167 us (46%)
  Pallas kernels  101 us (28%)
  starting transfers between devices  55.3 us (15%)
  local copies, waits for them, and re-layouts  19.1 us (5%)
  between operations  14.4 us (4%)
  other arithmetic  6.75 us (2%)
    ppermute x15, waiting for transfers between devices, shifted(): lax.ppermute(array, axis, [(at, (at + shift) % size) for at in range(size)])  132 us
    pallas_call x4, Pallas kernels, product(): pl.pallas_call(waiting(functools.partial(product_kernel, (inner, outer, l...  25.1 us
    ppermute x15, starting transfers between devices, shifted(): lax.ppermute(array, axis, [(at, (at + shift) % size) for at in range(size)])  20.8 us
    pallas_call x1, Pallas kernels, correlate(): pl.pallas_call(waiting(correlate_kernel, len(waits)), grid=(2, steps), in...  20.2 us
    ppermute x8, starting transfers between devices, per_device(): back.append(lax.ppermute(pick(total, (at_tp - step) % tp), cell, pairs))  18 us
    pallas_call x2, Pallas kernels, shares(): pl.pallas_call(waiting(functools.partial(shares_kernel, (outer, inner, ne...  17.9 us
    pallas_call x1, Pallas kernels, convolve(): pl.pallas_call(waiting(functools.partial(convolve_kernel, len(parts)), le...  17.6 us
    all_gather x1, waiting for transfers between devices, per_device(): gathered = lax.all_gather(arranged, 'outer', axis=0, tiled=False)  17.3 us
  transfers between devices with their start and end apart: 30, of which 17 were waited for; matrix products, arithmetic and copies ran while one was open for 3% of the time, Pallas kernels for 21%

profile of v6, /device:TPU:4, one launch (start us, length us, event | category | flops | bytes accessed | tf_op | source)
XLA Modules:
  0.0 363.6 jit_solution(5879795394240067088)
XLA Ops:
  14.8 13.2 %collective-permute-done.1 = bf16[128,2048]{1,0:T(8,128)(2,1)} collective-permute-done((bf16[128,2048]{1,0:T(8,128)(2,1)}, bf16[128,2048]{1,0:T(8,128)(2,1)}, u32[]{:S(2)}, u32[]{:S(2)}) %collective-permute-start.1) | collective-permute-done | bytes 524320 | tf_op jit(solution)/shard_map/ppermute | solution.py:499
  40.1 7.8 %collective-permute-done.3.refs_3_ = bf16[64,2048]{1,0:T(8,128)(2,1)S(1)} collective-permute-done((bf16[64,2048]{1,0:T(8,128)(2,1)S(1)}, bf16[64,2048]{1,0:T(8,128)(2,1)S(1)}, u32[]{:S(2)}, u32[]{:S(2)}) %collective-permute-start.3) | collective-permute-done | bytes 262176 | tf_op jit(solution)/shard_map/ppermute | solution.py:568
  47.8 6.1 %collective-permute-done.4.refs_4_ = bf16[64,2048]{1,0:T(8,128)(2,1)S(1)} collective-permute-done((bf16[64,2048]{1,0:T(8,128)(2,1)S(1)}, bf16[64,2048]{1,0:T(8,128)(2,1)S(1)}, u32[]{:S(2)}, u32[]{:S(2)}) %collective-permute-start.4) | collective-permute-done | bytes 262176 | tf_op jit(solution)/shard_map/ppermute | solution.py:568
  53.9 6.5 %collective-permute-done.refs_1_.refs_6_.refs_5_.refs_4_ = bf16[1024,1024]{1,0:T(8,128)(2,1)S(1)} collective-permute-done((bf16[1024,1024]{1,0:T(8,128)(2,1)}, bf16[1024,1024]{1,0:T(8,128)(2,1)S(1)}, u32[]{:S(2)}, u32[]{:S(2)}) %collective-permute-start) | collective-permute-done | bytes 2097184 | tf_op jit(solution)/shard_map/ppermute | solution.py:499
  63.2 5.9 %all-to-all-start = ((bf16[8,2,256,256]{3,2,1,0:T(8,128)(2,1)}), bf16[8,2,256,256]{3,2,1,0:T(8,128)(2,1)}, u32[]{:S(2)}, u32[]{:S(2)}) async-start(bf16[8,2,256,256]{3,2,1,0:T(8,128)(2,1)} %copy-done.4), calls=%async_computation | async-start | bytes 4194304 | tf_op jit(solution)/shard_map/all_to_all | solution.py:581
  69.7 23.3 %collective-permute-done.6.refs_2_.refs_1_ = bf16[256,2048]{1,0:T(8,128)(2,1)} collective-permute-done((bf16[256,2048]{1,0:T(8,128)(2,1)S(1)}, bf16[256,2048]{1,0:T(8,128)(2,1)}, u32[]{:S(2)}, u32[]{:S(2)}) %collective-permute-start.6) | collective-permute-done | bytes 1048608 | tf_op jit(solution)/shard_map/ppermute | solution.py:499
  96.5 6.4 %shard_map.98 = bf16[1024,512]{1,0:T(8,128)(2,1)} custom-call(s32[8]{0:T(128)S(1)} %concatenate.38.index_ref, bf16[1024,1024]{1,0:T(8,128)(2,1)} %shard_map.97.refs_0_, bf16[256,2048]{1,0:T(8,128)(2,1)S(1)} %shard_map.96.refs_0_.refs_1_, bf16[256,2048]{1,0:T(8,128)(2,1)} %collective-permute-done.6.refs_2_.refs_1_, ...), custom_call_target="tpu_custom_call" | custom-call | tf_op jit(solution)/shard_map/pallas_call | solution.py:414
  106.0 24.6 %collective-permute-done.9.refs_6_ = bf16[1024,512]{1,0:T(8,128)(2,1)} collective-permute-done((bf16[1024,512]{1,0:T(8,128)(2,1)}, bf16[1024,512]{1,0:T(8,128)(2,1)}, u32[]{:S(2)}, u32[]{:S(2)}) %collective-permute-start.9) | collective-permute-done | bytes 1048608 | tf_op jit(solution)/shard_map/ppermute | solution.py:499
  130.7 6.7 %shard_map.99.refs_0_ = bf16[1024,512]{1,0:T(8,128)(2,1)} custom-call(s32[8]{0:T(128)S(1)} %concatenate.37.index_ref, bf16[256,2048]{1,0:T(8,128)(2,1)S(1)} %shard_map.96.refs_0_.refs_1_, bf16[256,2048]{1,0:T(8,128)(2,1)} %collective-permute-done.6.refs_2_.refs_1_, bf16[256,2048]{1,0:T(8,128)(2,1)} %collective-permute-done.7.refs_3_.refs_2_, ...), custom_call_target="tpu_custom_call" | custom-call | tf_op jit(solution)/shard_map/pallas_call | solution.py:414
  137.4 7.2 %collective-permute-start.11 = (bf16[1024,512]{1,0:T(8,128)(2,1)}, bf16[1024,512]{1,0:T(8,128)(2,1)}, u32[]{:S(2)}, u32[]{:S(2)}) collective-permute-start(bf16[1024,512]{1,0:T(8,128)(2,1)} %shard_map.99.refs_0_), channel_id=1, source_target_pairs={{0,8},{8,16},{16,24},{24,0},{1,9},{9,17},{17,25},{25,1},{2,10},{10... | collective-permute-start | bytes 3145736 | tf_op jit(solution)/shard_map/ppermute | solution.py:499
  147.5 20.2 %shard_map.101 = (bf16[2048,256]{1,0:T(8,128)(2,1)S(1)}, bf16[2,2048,256]{2,1,0:T(8,128)(2,1)S(1)}) custom-call(s32[1]{0:T(128)} %constant.367.clone.1.index_ref, bf16[1024,512]{1,0:T(8,128)(2,1)} %shard_map.99.refs_0_, bf16[2048,2048]{1,0:T(8,128)(2,1)} %constant.370.clone.refs_1_.refs_0_, bf16[2048,2048]{1,0:T(8,128)(2,1)} %constant.371.clone.refs_2_.refs_1_, ...), custom_call_target="tpu_custom_call" | custom-call | tf_op jit(solution)/shard_map/pallas_call | solution.py:120
  172.9 6.0 %shard_map.102.refs_0_ = bf16[1024,512]{1,0:T(8,128)(2,1)S(1)} custom-call(s32[8]{0:T(128)S(1)} %concatenate.41.index_ref, bf16[2,2048,256]{2,1,0:T(8,128)(2,1)} %copy-done.5, bf16[256,2048]{1,0:T(8,128)(2,1)S(1)} %shard_map.96.refs_0_.refs_1_, bf16[256,2048]{1,0:T(8,128)(2,1)} %collective-permute-done.6.refs_2_.refs_1_, ...), custom_call_target="tpu_custom_call" | custom-call | tf_op jit(solution)/shard_map/pallas_call | solution.py:414
  178.9 5.0 %collective-permute-done.12.refs_2_ = bf16[4,256,256]{2,1,0:T(8,128)(2,1)} collective-permute-done((bf16[4,256,256]{2,1,0:T(8,128)(2,1)}, bf16[4,256,256]{2,1,0:T(8,128)(2,1)}, u32[]{:S(2)}, u32[]{:S(2)}) %collective-permute-start.12) | collective-permute-done | bytes 524320 | tf_op jit(solution)/shard_map/ppermute | solution.py:499
  189.9 38.8 %collective-permute-done.13.refs_7_ = bf16[1024,512]{1,0:T(8,128)(2,1)S(1)} collective-permute-done((bf16[1024,512]{1,0:T(8,128)(2,1)}, bf16[1024,512]{1,0:T(8,128)(2,1)S(1)}, u32[]{:S(2)}, u32[]{:S(2)}) %collective-permute-start.13) | collective-permute-done | bytes 1048608 | tf_op jit(solution)/shard_map/ppermute | solution.py:499
  229.7 6.0 %shard_map.104 = bf16[2,1024,256]{2,1,0:T(8,128)(2,1)S(1)} custom-call(s32[8]{0:T(128)S(1)} %concatenate.39.index_ref, bf16[2,512,512]{2,1,0:T(8,128)(2,1)} %shard_map.103.refs_0_, bf16[256,2048]{1,0:T(8,128)(2,1)S(1)} %shard_map.96.refs_0_.refs_1_, bf16[256,2048]{1,0:T(8,128)(2,1)} %collective-permute-done.6.refs_2_.refs_1_, ...), custom_call_target="tpu_custom_call" | custom-call | tf_op jit(solution)/shard_map/pallas_call | solution.py:414
  237.2 7.8 %collective-permute-done.14.refs_4_ = bf16[1024,256]{1,0:T(8,128)(2,1)S(1)} collective-permute-done((bf16[1024,256]{1,0:T(8,128)(2,1)S(1)}, bf16[1024,256]{1,0:T(8,128)(2,1)S(1)}, u32[]{:S(2)}, u32[]{:S(2)}) %collective-permute-start.14) | collective-permute-done | bytes 524320 | tf_op jit(solution)/shard_map/ppermute | solution.py:499
  246.6 17.6 %shard_map.105 = bf16[2048,256]{1,0:T(8,128)(2,1)} custom-call(s32[2,16]{1,0:T(2,128)S(1)} %pad_add_fusion.index_ref, bf16[2048,2048]{1,0:T(8,128)(2,1)} %constant.370.clone.refs_1_.refs_0_, bf16[2048,2048]{1,0:T(8,128)(2,1)} %constant.371.clone.refs_2_.refs_1_, bf16[2,2048,256]{2,1,0:T(8,128)(2,1)S(1)} %copy-done.6, ...), custom_call_target="tpu_custom_call" | custom-call | tf_op jit(solution)/shard_map/pallas_call | solution.py:179
  264.1 17.3 %all-gather.3.cloned.1.call-done = bf16[8,512,512]{2,1,0:T(8,128)(2,1)} async-done(((bf16[2,512,512]{2,1,0:T(8,128)(2,1)}), bf16[8,512,512]{2,1,0:T(8,128)(2,1)}) %all-gather.3.cloned.1.call-update) | async-done | bytes 4194320 | tf_op jit(solution)/shard_map/all_gather | solution.py:621
  281.4 8.9 %shard_map.107 = (bf16[2,256,1024]{2,1,0:T(8,128)(2,1)S(1)}, bf16[2,256,1024]{2,1,0:T(8,128)(2,1)}) custom-call(s32[4]{0:T(128)S(1)} %pad_add_fusion.3.index_ref, bf16[8,256,256]{2,1,0:T(8,128)(2,1)} %bitcast.43.refs_0_, bf16[4,2,512,512]{3,2,1,0:T(8,128)(2,1)} %bitcast.104, bf16[1024,2048]{1,0:T(8,128)(2,1)} %refs_2_.8, bf16[1024,1024]{1,0:T(8,128)(2,1)S(1)} %copy-done.3, ...), custom_call_target="tpu_custom_call" | custom-call | tf_op jit(solution)/shard_map/pallas_call | solution.py:479
  290.4 9.0 %shard_map.108 = (bf16[2,256,1024]{2,1,0:T(8,128)(2,1)S(1)}, bf16[2,256,1024]{2,1,0:T(8,128)(2,1)}) custom-call(s32[4]{0:T(128)S(1)} %pad_add_fusion.3.index_ref, bf16[2,256,1024]{2,1,0:T(8,128)(2,1)S(1)} %get-tuple-element.15.refs_0_, bf16[4,2,512,512]{3,2,1,0:T(8,128)(2,1)} %bitcast.105, bf16[1024,2048]{1,0:T(8,128)(2,1)} %refs_2_.8, ...), custom_call_target="tpu_custom_call" | custom-call | tf_op jit(solution)/shard_map/pallas_call | solution.py:479
  312.3 9.3 %collective-permute-done.22 = bf16[2,128,1024]{2,1,0:T(8,128)(2,1)S(1)} collective-permute-done((bf16[2,128,1024]{2,1,0:T(8,128)(2,1)S(1)}, bf16[2,128,1024]{2,1,0:T(8,128)(2,1)S(1)}, u32[]{:S(2)}, u32[]{:S(2)}) %collective-permute-start.22) | collective-permute-done | bytes 524320 | tf_op jit(solution)/shard_map/ppermute | solution.py:499
  321.9 4.8 %collective-permute-start.23 = (bf16[2,32,1024]{2,1,0:T(8,128)(2,1)S(1)}, bf16[2,32,1024]{2,1,0:T(8,128)(2,1)S(1)}, u32[]{:S(2)}, u32[]{:S(2)}) collective-permute-start(bf16[2,32,1024]{2,1,0:T(8,128)(2,1)S(1)} %get-tuple-element.32), channel_id=1, source_target_pairs={{0,0},{8,1},{16,2},{24,3},{1,8},{9,9},{17,10},{25,11},{2,16},{10,1... | collective-permute-start | bytes 393224 | tf_op jit(solution)/shard_map/ppermute | solution.py:646
  335.5 4.8 %collective-permute-start.17 = (bf16[2,32,1024]{2,1,0:T(8,128)(2,1)}, bf16[2,32,1024]{2,1,0:T(8,128)(2,1)S(1)}, u32[]{:S(2)}, u32[]{:S(2)}) collective-permute-start(bf16[2,32,1024]{2,1,0:T(8,128)(2,1)} %get-tuple-element.36), channel_id=1, source_target_pairs={{0,0},{8,1},{16,2},{24,3},{1,8},{9,9},{17,10},{25,11},{2,16},{10,1... | collective-permute-start | bytes 393224 | tf_op jit(solution)/shard_map/ppermute | solution.py:646
  346.3 5.5 %shard_map.106 = (bf16[256,2048]{1,0:T(8,128)(2,1)}, bf16[256,2048]{1,0:T(8,128)(2,1)}) custom-call(bf16[8,256,256]{2,1,0:T(8,128)(2,1)} %all-to-all-done.1.convolved_ref, bf16[256,2048]{1,0:T(8,128)(2,1)S(1)} %copy-done.8, bf16[256,2048]{1,0:T(8,128)(2,1)S(1)} %copy-done.10), custom_call_target="tpu_custom_call" | custom-call | tf_op jit(solution)/shard_map/pallas_call | solution.py:236
  (118 shorter events, 80.4 us)
Async XLA Ops:
  12.8 47.6 %collective-permute-start = (bf16[1024,1024]{1,0:T(8,128)(2,1)}, bf16[1024,1024]{1,0:T(8,128)(2,1)S(1)}, u32[]{:S(2)}, u32[]{:S(2)}) collective-permute-start(bf16[1024,1024]{1,0:T(8,128)(2,1)} %shard_map.94.refs_0_), channel_id=1, source_target_pairs={{0,4},{4,0},{1,5},{5,1},{2,6},{6,2},{3,7},{7,3},{8,12},{12,8},{9,1... | collective-permute-start | bytes 6291464 | tf_op jit(solution)/shard_map/ppermute | solution.py:499
  14.3 13.7 %collective-permute-start.1 = (bf16[128,2048]{1,0:T(8,128)(2,1)}, bf16[128,2048]{1,0:T(8,128)(2,1)}, u32[]{:S(2)}, u32[]{:S(2)}) collective-permute-start(bf16[128,2048]{1,0:T(8,128)(2,1)} %get-tuple-element.28.refs_0_), channel_id=1, source_target_pairs={{0,2},{2,0},{1,3},{3,1},{4,6},{6,4},{5,7},{7,5},{8,10},{10,8},{9,1... | collective-permute-start | bytes 1572872 | tf_op jit(solution)/shard_map/ppermute | solution.py:499
  30.3 17.5 %collective-permute-start.3 = (bf16[64,2048]{1,0:T(8,128)(2,1)S(1)}, bf16[64,2048]{1,0:T(8,128)(2,1)S(1)}, u32[]{:S(2)}, u32[]{:S(2)}) collective-permute-start(bf16[64,2048]{1,0:T(8,128)(2,1)S(1)} %get-tuple-element.25), channel_id=1, source_target_pairs={{0,1},{1,9},{2,3},{3,11},{8,16},{9,24},{10,18},{11,26},{16,17},{17... | collective-permute-start | bytes 786440 | tf_op jit(solution)/shard_map/ppermute | solution.py:568
  33.2 20.6 %collective-permute-start.4 = (bf16[64,2048]{1,0:T(8,128)(2,1)S(1)}, bf16[64,2048]{1,0:T(8,128)(2,1)S(1)}, u32[]{:S(2)}, u32[]{:S(2)}) collective-permute-start(bf16[64,2048]{1,0:T(8,128)(2,1)S(1)} %get-tuple-element.26), channel_id=1, source_target_pairs={{0,16},{1,24},{2,18},{3,26},{8,17},{9,25},{10,19},{11,27},{16,0},{... | collective-permute-start | bytes 786440 | tf_op jit(solution)/shard_map/ppermute | solution.py:568
  35.8 18.0 %collective-permute-start.5 = (bf16[64,2048]{1,0:T(8,128)(2,1)S(1)}, bf16[64,2048]{1,0:T(8,128)(2,1)S(1)}, u32[]{:S(2)}, u32[]{:S(2)}) collective-permute-start(bf16[64,2048]{1,0:T(8,128)(2,1)S(1)} %get-tuple-element.23), channel_id=1, source_target_pairs={{0,17},{1,25},{2,19},{3,27},{8,0},{9,8},{10,2},{11,10},{16,1},{17,... | collective-permute-start | bytes 786440 | tf_op jit(solution)/shard_map/ppermute | solution.py:568
  63.2 83.1 %all-to-all-start = ((bf16[8,2,256,256]{3,2,1,0:T(8,128)(2,1)}), bf16[8,2,256,256]{3,2,1,0:T(8,128)(2,1)}, u32[]{:S(2)}, u32[]{:S(2)}) async-start(bf16[8,2,256,256]{3,2,1,0:T(8,128)(2,1)} %copy-done.4), calls=%async_computation | async-start | bytes 4194304 | tf_op jit(solution)/shard_map/all_to_all | solution.py:581
  69.1 212.3 %all-gather.3.cloned.1.call-start = ((), (), s32[]{:S(2)}) async-start(), calls=%async_computation.2 | async-start | bytes 5242880 | tf_op jit(solution)/shard_map/all_gather | solution.py:621
  69.1 23.9 %collective-permute-start.6 = (bf16[256,2048]{1,0:T(8,128)(2,1)S(1)}, bf16[256,2048]{1,0:T(8,128)(2,1)}, u32[]{:S(2)}, u32[]{:S(2)}) collective-permute-start(bf16[256,2048]{1,0:T(8,128)(2,1)S(1)} %shard_map.96.refs_0_.refs_1_), channel_id=1, source_target_pairs={{0,2},{2,0},{1,3},{3,1},{4,6},{6,4},{5,7},{7,5},{8,10},{10,8},{9,1... | collective-permute-start | bytes 3145736 | tf_op jit(solution)/shard_map/ppermute | solution.py:499
  69.7 26.8 %collective-permute-start.7 = (bf16[256,2048]{1,0:T(8,128)(2,1)S(1)}, bf16[256,2048]{1,0:T(8,128)(2,1)}, u32[]{:S(2)}, u32[]{:S(2)}) collective-permute-start(bf16[256,2048]{1,0:T(8,128)(2,1)S(1)} %shard_map.96.refs_0_.refs_1_), channel_id=1, source_target_pairs={{0,1},{1,0},{2,3},{3,2},{4,5},{5,4},{6,7},{7,6},{8,9},{9,8},{10,11... | collective-permute-start | bytes 3145736 | tf_op jit(solution)/shard_map/ppermute | solution.py:499
  102.9 27.8 %collective-permute-start.9 = (bf16[1024,512]{1,0:T(8,128)(2,1)}, bf16[1024,512]{1,0:T(8,128)(2,1)}, u32[]{:S(2)}, u32[]{:S(2)}) collective-permute-start(bf16[1024,512]{1,0:T(8,128)(2,1)} %shard_map.98), channel_id=1, source_target_pairs={{0,8},{8,16},{16,24},{24,0},{1,9},{9,17},{17,25},{25,1},{2,10},{10... | collective-permute-start | bytes 3145736 | tf_op jit(solution)/shard_map/ppermute | solution.py:499
  104.5 67.1 %collective-permute-start.10 = (bf16[1024,1024]{1,0:T(8,128)(2,1)}, bf16[1024,1024]{1,0:T(8,128)(2,1)S(1)}, u32[]{:S(2)}, u32[]{:S(2)}) collective-permute-start(bf16[1024,1024]{1,0:T(8,128)(2,1)} %shard_map.97.refs_0_), channel_id=1, source_target_pairs={{0,4},{4,0},{1,5},{5,1},{2,6},{6,2},{3,7},{7,3},{8,12},{12,8},{9,1... | collective-permute-start | bytes 6291464 | tf_op jit(solution)/shard_map/ppermute | solution.py:499
  137.4 34.2 %collective-permute-start.11 = (bf16[1024,512]{1,0:T(8,128)(2,1)}, bf16[1024,512]{1,0:T(8,128)(2,1)}, u32[]{:S(2)}, u32[]{:S(2)}) collective-permute-start(bf16[1024,512]{1,0:T(8,128)(2,1)} %shard_map.99.refs_0_), channel_id=1, source_target_pairs={{0,8},{8,16},{16,24},{24,0},{1,9},{9,17},{17,25},{25,1},{2,10},{10... | collective-permute-start | bytes 3145736 | tf_op jit(solution)/shard_map/ppermute | solution.py:499
  170.1 13.9 %collective-permute-start.12 = (bf16[4,256,256]{2,1,0:T(8,128)(2,1)}, bf16[4,256,256]{2,1,0:T(8,128)(2,1)}, u32[]{:S(2)}, u32[]{:S(2)}) collective-permute-start(bf16[4,256,256]{2,1,0:T(8,128)(2,1)} %get-tuple-element.21), channel_id=1, source_target_pairs={{0,4},{4,0},{1,5},{5,1},{2,6},{6,2},{3,7},{7,3},{8,12},{12,8},{9,1... | collective-permute-start | bytes 1572872 | tf_op jit(solution)/shard_map/ppermute | solution.py:499
  187.1 41.6 %collective-permute-start.13 = (bf16[1024,512]{1,0:T(8,128)(2,1)}, bf16[1024,512]{1,0:T(8,128)(2,1)S(1)}, u32[]{:S(2)}, u32[]{:S(2)}) collective-permute-start(bf16[1024,512]{1,0:T(8,128)(2,1)} %copy-done.11), channel_id=1, source_target_pairs={{0,8},{8,16},{16,24},{24,0},{1,9},{9,17},{17,25},{25,1},{2,10},{10... | collective-permute-start | bytes 3145736 | tf_op jit(solution)/shard_map/ppermute | solution.py:499
  300.8 45.5 %all-to-all-start.1 = ((bf16[8,256,256]{2,1,0:T(8,128)(2,1)}), bf16[8,256,256]{2,1,0:T(8,128)(2,1)}, u32[]{:S(2)}, u32[]{:S(2)}) async-start(bf16[8,256,256]{2,1,0:T(8,128)(2,1)} %bitcast.43.refs_0_), calls=%async_computation.1 | async-start | bytes 2097152 | tf_op jit(solution)/shard_map/all_to_all | solution.py:626
  306.8 14.8 %collective-permute-start.22 = (bf16[2,128,1024]{2,1,0:T(8,128)(2,1)S(1)}, bf16[2,128,1024]{2,1,0:T(8,128)(2,1)S(1)}, u32[]{:S(2)}, u32[]{:S(2)}) collective-permute-start(bf16[2,128,1024]{2,1,0:T(8,128)(2,1)S(1)} %slice_bitcast_fusion), channel_id=1, source_target_pairs={{0,2},{2,0},{1,3},{3,1},{4,6},{6,4},{5,7},{7,5},{8,10},{10,8},{9,1... | collective-permute-start | bytes 1572872 | tf_op jit(solution)/shard_map/ppermute | solution.py:499
  310.8 22.8 %collective-permute-start.16 = (bf16[2,128,1024]{2,1,0:T(8,128)(2,1)}, bf16[2,128,1024]{2,1,0:T(8,128)(2,1)}, u32[]{:S(2)}, u32[]{:S(2)}) collective-permute-start(bf16[2,128,1024]{2,1,0:T(8,128)(2,1)} %slice_bitcast_fusion.2), channel_id=1, source_target_pairs={{0,2},{2,0},{1,3},{3,1},{4,6},{6,4},{5,7},{7,5},{8,10},{10,8},{9,1... | collective-permute-start | bytes 1572872 | tf_op jit(solution)/shard_map/ppermute | solution.py:499
  321.9 18.7 %collective-permute-start.23 = (bf16[2,32,1024]{2,1,0:T(8,128)(2,1)S(1)}, bf16[2,32,1024]{2,1,0:T(8,128)(2,1)S(1)}, u32[]{:S(2)}, u32[]{:S(2)}) collective-permute-start(bf16[2,32,1024]{2,1,0:T(8,128)(2,1)S(1)} %get-tuple-element.32), channel_id=1, source_target_pairs={{0,0},{8,1},{16,2},{24,3},{1,8},{9,9},{17,10},{25,11},{2,16},{10,1... | collective-permute-start | bytes 393224 | tf_op jit(solution)/shard_map/ppermute | solution.py:646
  326.7 14.9 %collective-permute-start.24 = (bf16[2,32,1024]{2,1,0:T(8,128)(2,1)S(1)}, bf16[2,32,1024]{2,1,0:T(8,128)(2,1)S(1)}, u32[]{:S(2)}, u32[]{:S(2)}) collective-permute-start(bf16[2,32,1024]{2,1,0:T(8,128)(2,1)S(1)} %get-tuple-element.31), channel_id=1, source_target_pairs={{1,0},{9,1},{17,2},{25,3},{2,8},{10,9},{18,10},{26,11},{3,16},{11,... | collective-permute-start | bytes 393224 | tf_op jit(solution)/shard_map/ppermute | solution.py:646
  326.8 16.2 %collective-permute-start.25 = (bf16[2,32,1024]{2,1,0:T(8,128)(2,1)S(1)}, bf16[2,32,1024]{2,1,0:T(8,128)(2,1)S(1)}, u32[]{:S(2)}, u32[]{:S(2)}) collective-permute-start(bf16[2,32,1024]{2,1,0:T(8,128)(2,1)S(1)} %get-tuple-element.30), channel_id=1, source_target_pairs={{2,0},{10,1},{18,2},{26,3},{3,8},{11,9},{19,10},{27,11},{0,16},{8,... | collective-permute-start | bytes 393224 | tf_op jit(solution)/shard_map/ppermute | solution.py:646
  328.3 23.5 %collective-permute-start.26 = (bf16[2,32,1024]{2,1,0:T(8,128)(2,1)S(1)}, bf16[2,32,1024]{2,1,0:T(8,128)(2,1)S(1)}, u32[]{:S(2)}, u32[]{:S(2)}) collective-permute-start(bf16[2,32,1024]{2,1,0:T(8,128)(2,1)S(1)} %get-tuple-element.29), channel_id=1, source_target_pairs={{3,0},{11,1},{19,2},{27,3},{0,8},{8,9},{16,10},{24,11},{1,16},{9,1... | collective-permute-start | bytes 393224 | tf_op jit(solution)/shard_map/ppermute | solution.py:646
  335.5 16.3 %collective-permute-start.17 = (bf16[2,32,1024]{2,1,0:T(8,128)(2,1)}, bf16[2,32,1024]{2,1,0:T(8,128)(2,1)S(1)}, u32[]{:S(2)}, u32[]{:S(2)}) collective-permute-start(bf16[2,32,1024]{2,1,0:T(8,128)(2,1)} %get-tuple-element.36), channel_id=1, source_target_pairs={{0,0},{8,1},{16,2},{24,3},{1,8},{9,9},{17,10},{25,11},{2,16},{10,1... | collective-permute-start | bytes 393224 | tf_op jit(solution)/shard_map/ppermute | solution.py:646
  340.6 12.7 %collective-permute-start.18 = (bf16[2,32,1024]{2,1,0:T(8,128)(2,1)}, bf16[2,32,1024]{2,1,0:T(8,128)(2,1)S(1)}, u32[]{:S(2)}, u32[]{:S(2)}) collective-permute-start(bf16[2,32,1024]{2,1,0:T(8,128)(2,1)} %get-tuple-element.35), channel_id=1, source_target_pairs={{1,0},{9,1},{17,2},{25,3},{2,8},{10,9},{18,10},{26,11},{3,16},{11,... | collective-permute-start | bytes 393224 | tf_op jit(solution)/shard_map/ppermute | solution.py:646
  341.6 12.9 %collective-permute-start.19 = (bf16[2,32,1024]{2,1,0:T(8,128)(2,1)S(1)}, bf16[2,32,1024]{2,1,0:T(8,128)(2,1)S(1)}, u32[]{:S(2)}, u32[]{:S(2)}) collective-permute-start(bf16[2,32,1024]{2,1,0:T(8,128)(2,1)S(1)} %get-tuple-element.34), channel_id=1, source_target_pairs={{2,0},{10,1},{18,2},{26,3},{3,8},{11,9},{19,10},{27,11},{0,16},{8,... | collective-permute-start | bytes 393224 | tf_op jit(solution)/shard_map/ppermute | solution.py:646
  (25 other events, 254.1 us)
Sparse Core Ops, SparseCore 0:
  187.2 94.1 all-gather.2

commit v7 on v6

--- a/solution.py
+++ b/solution.py
@@ -629,9 +629,9 @@
     waits = [convolved]
     for half in range(halves):
         by_near = shares(gathered, half, in_weight, received, jnp.stack(chunks), near, waits)
-        waits = [by_near[0]]
         total = by_near[0].astype(WIDE) + sum(shifted(by_near[n], "near", n).astype(WIDE) for n in range(1, near))
         total = total.astype(SHORT).reshape(inner, far, outer * half_rows, depth)
+        waits = [total]
         others = [shifted(total[:, f], "far", f) for f in range(1, far)]
         total = total[:, 0].astype(WIDE) + sum(other.astype(WIDE) for other in others)
         total = total.astype(SHORT).reshape(inner, outer, half_rows, depth)

time: 365 us -> 367 us (level)
  waiting for transfers between devices: 167 us -> 173 us
  local copies, waits for them, and re-layouts: 19.1 us -> 23.3 us
    ppermute x8, waiting for transfers between devices: 4.55 us -> 11.6 us  [per_device(): back.append(lax.ppermute(pick(total, (at_tp - step) % tp), cell, pairs))]
    ppermute x8, starting transfers between devices: 18 us -> 12.7 us  [per_device(): back.append(lax.ppermute(pick(total, (at_tp - step) % tp), cell, pairs))]
    unnamed x38 -> x46, local copies, waits for them, and re-layouts: 12.1 us -> 14 us
  transfers between devices with their start and end apart: 30 -> 30, of which waited for: 17 -> 19; matrix products, arithmetic and copies ran while one was open for 3% -> 4% of each run, Pallas kernels for 21% -> 20%
where the time goes in v7:
time: 367 us; the launch traced here: 366 us
  waiting for transfers between devices  173 us (47%)
  Pallas kernels  97.6 us (27%)
  starting transfers between devices  51.9 us (14%)
  local copies, waits for them, and re-layouts  23.3 us (6%)
  between operations  14.4 us (4%)
  other arithmetic  6.57 us (2%)
    ppermute x15, waiting for transfers between devices, shifted(): lax.ppermute(array, axis, [(at, (at + shift) % size) for at in range(size)])  133 us
    pallas_call x4, Pallas kernels, product(): pl.pallas_call(waiting(functools.partial(product_kernel, (inner, outer, l...  25.1 us
    ppermute x15, starting transfers between devices, shifted(): lax.ppermute(array, axis, [(at, (at + shift) % size) for at in range(size)])  20.4 us
    pallas_call x1, Pallas kernels, correlate(): pl.pallas_call(waiting(correlate_kernel, len(waits)), grid=(2, steps), in...  20.2 us
    pallas_call x2, Pallas kernels, shares(): pl.pallas_call(waiting(functools.partial(shares_kernel, (outer, inner, ne...  17.3 us
    pallas_call x1, Pallas kernels, convolve(): pl.pallas_call(waiting(functools.partial(convolve_kernel, len(parts)), le...  16.7 us
    all_gather x1, waiting for transfers between devices, per_device(): gathered = lax.all_gather(arranged, 'outer', axis=0, tiled=False)  14.5 us
    unnamed x46, local copies, waits for them, and re-layouts  14 us
  transfers between devices with their start and end apart: 30, of which 19 were waited for; matrix products, arithmetic and copies ran while one was open for 4% of the time, Pallas kernels for 20%

profile of v7, /device:TPU:4, one launch (start us, length us, event | category | flops | bytes accessed | tf_op | source)
XLA Modules:
  0.0 366.4 jit_solution(2019209269701228426)
XLA Ops:
  14.8 13.2 %collective-permute-done.1 = bf16[128,2048]{1,0:T(8,128)(2,1)} collective-permute-done((bf16[128,2048]{1,0:T(8,128)(2,1)}, bf16[128,2048]{1,0:T(8,128)(2,1)}, u32[]{:S(2)}, u32[]{:S(2)}) %collective-permute-start.1) | collective-permute-done | bytes 524320 | tf_op jit(solution)/shard_map/ppermute | solution.py:499
  40.1 7.8 %collective-permute-done.3.refs_3_ = bf16[64,2048]{1,0:T(8,128)(2,1)S(1)} collective-permute-done((bf16[64,2048]{1,0:T(8,128)(2,1)S(1)}, bf16[64,2048]{1,0:T(8,128)(2,1)S(1)}, u32[]{:S(2)}, u32[]{:S(2)}) %collective-permute-start.3) | collective-permute-done | bytes 262176 | tf_op jit(solution)/shard_map/ppermute | solution.py:568
  47.8 6.1 %collective-permute-done.4.refs_4_ = bf16[64,2048]{1,0:T(8,128)(2,1)S(1)} collective-permute-done((bf16[64,2048]{1,0:T(8,128)(2,1)S(1)}, bf16[64,2048]{1,0:T(8,128)(2,1)S(1)}, u32[]{:S(2)}, u32[]{:S(2)}) %collective-permute-start.4) | collective-permute-done | bytes 262176 | tf_op jit(solution)/shard_map/ppermute | solution.py:568
  53.9 6.5 %collective-permute-done.refs_1_.refs_6_.refs_5_.refs_4_ = bf16[1024,1024]{1,0:T(8,128)(2,1)S(1)} collective-permute-done((bf16[1024,1024]{1,0:T(8,128)(2,1)}, bf16[1024,1024]{1,0:T(8,128)(2,1)S(1)}, u32[]{:S(2)}, u32[]{:S(2)}) %collective-permute-start) | collective-permute-done | bytes 2097184 | tf_op jit(solution)/shard_map/ppermute | solution.py:499
  63.2 5.9 %all-to-all-start = ((bf16[8,2,256,256]{3,2,1,0:T(8,128)(2,1)}), bf16[8,2,256,256]{3,2,1,0:T(8,128)(2,1)}, u32[]{:S(2)}, u32[]{:S(2)}) async-start(bf16[8,2,256,256]{3,2,1,0:T(8,128)(2,1)} %copy-done.4), calls=%async_computation | async-start | bytes 4194304 | tf_op jit(solution)/shard_map/all_to_all | solution.py:581
  69.7 23.3 %collective-permute-done.6.refs_2_.refs_1_ = bf16[256,2048]{1,0:T(8,128)(2,1)} collective-permute-done((bf16[256,2048]{1,0:T(8,128)(2,1)S(1)}, bf16[256,2048]{1,0:T(8,128)(2,1)}, u32[]{:S(2)}, u32[]{:S(2)}) %collective-permute-start.6) | collective-permute-done | bytes 1048608 | tf_op jit(solution)/shard_map/ppermute | solution.py:499
  96.5 6.4 %shard_map.98 = bf16[1024,512]{1,0:T(8,128)(2,1)} custom-call(s32[8]{0:T(128)S(1)} %concatenate.38.index_ref, bf16[1024,1024]{1,0:T(8,128)(2,1)} %shard_map.97.refs_0_, bf16[256,2048]{1,0:T(8,128)(2,1)S(1)} %shard_map.96.refs_0_.refs_1_, bf16[256,2048]{1,0:T(8,128)(2,1)} %collective-permute-done.6.refs_2_.refs_1_, ...), custom_call_target="tpu_custom_call" | custom-call | tf_op jit(solution)/shard_map/pallas_call | solution.py:414
  106.1 24.6 %collective-permute-done.9.refs_6_ = bf16[1024,512]{1,0:T(8,128)(2,1)} collective-permute-done((bf16[1024,512]{1,0:T(8,128)(2,1)}, bf16[1024,512]{1,0:T(8,128)(2,1)}, u32[]{:S(2)}, u32[]{:S(2)}) %collective-permute-start.9) | collective-permute-done | bytes 1048608 | tf_op jit(solution)/shard_map/ppermute | solution.py:499
  130.7 6.8 %shard_map.99.refs_0_ = bf16[1024,512]{1,0:T(8,128)(2,1)} custom-call(s32[8]{0:T(128)S(1)} %concatenate.37.index_ref, bf16[256,2048]{1,0:T(8,128)(2,1)S(1)} %shard_map.96.refs_0_.refs_1_, bf16[256,2048]{1,0:T(8,128)(2,1)} %collective-permute-done.6.refs_2_.refs_1_, bf16[256,2048]{1,0:T(8,128)(2,1)} %collective-permute-done.7.refs_3_.refs_2_, ...), custom_call_target="tpu_custom_call" | custom-call | tf_op jit(solution)/shard_map/pallas_call | solution.py:414
  137.4 7.2 %collective-permute-start.11 = (bf16[1024,512]{1,0:T(8,128)(2,1)}, bf16[1024,512]{1,0:T(8,128)(2,1)}, u32[]{:S(2)}, u32[]{:S(2)}) collective-permute-start(bf16[1024,512]{1,0:T(8,128)(2,1)} %shard_map.99.refs_0_), channel_id=1, source_target_pairs={{0,8},{8,16},{16,24},{24,0},{1,9},{9,17},{17,25},{25,1},{2,10},{10... | collective-permute-start | bytes 3145736 | tf_op jit(solution)/shard_map/ppermute | solution.py:499
  147.5 20.2 %shard_map.101 = (bf16[2048,256]{1,0:T(8,128)(2,1)S(1)}, bf16[2,2048,256]{2,1,0:T(8,128)(2,1)S(1)}) custom-call(s32[1]{0:T(128)} %constant.367.clone.1.index_ref, bf16[1024,512]{1,0:T(8,128)(2,1)} %shard_map.99.refs_0_, bf16[2048,2048]{1,0:T(8,128)(2,1)} %constant.370.clone.refs_1_.refs_0_, bf16[2048,2048]{1,0:T(8,128)(2,1)} %constant.371.clone.refs_2_.refs_1_, ...), custom_call_target="tpu_custom_call" | custom-call | tf_op jit(solution)/shard_map/pallas_call | solution.py:120
  173.0 6.0 %shard_map.102.refs_0_ = bf16[1024,512]{1,0:T(8,128)(2,1)S(1)} custom-call(s32[8]{0:T(128)S(1)} %concatenate.41.index_ref, bf16[2,2048,256]{2,1,0:T(8,128)(2,1)} %copy-done.6, bf16[256,2048]{1,0:T(8,128)(2,1)S(1)} %shard_map.96.refs_0_.refs_1_, bf16[256,2048]{1,0:T(8,128)(2,1)} %collective-permute-done.6.refs_2_.refs_1_, ...), custom_call_target="tpu_custom_call" | custom-call | tf_op jit(solution)/shard_map/pallas_call | solution.py:414
  179.0 5.0 %collective-permute-done.12.refs_2_ = bf16[4,256,256]{2,1,0:T(8,128)(2,1)} collective-permute-done((bf16[4,256,256]{2,1,0:T(8,128)(2,1)}, bf16[4,256,256]{2,1,0:T(8,128)(2,1)}, u32[]{:S(2)}, u32[]{:S(2)}) %collective-permute-start.12) | collective-permute-done | bytes 524320 | tf_op jit(solution)/shard_map/ppermute | solution.py:499
  188.9 38.8 %collective-permute-done.13.refs_7_ = bf16[1024,512]{1,0:T(8,128)(2,1)S(1)} collective-permute-done((bf16[1024,512]{1,0:T(8,128)(2,1)}, bf16[1024,512]{1,0:T(8,128)(2,1)S(1)}, u32[]{:S(2)}, u32[]{:S(2)}) %collective-permute-start.13) | collective-permute-done | bytes 1048608 | tf_op jit(solution)/shard_map/ppermute | solution.py:499
  228.7 6.0 %shard_map.104 = bf16[2,1024,256]{2,1,0:T(8,128)(2,1)S(1)} custom-call(s32[8]{0:T(128)S(1)} %concatenate.39.index_ref, bf16[2,512,512]{2,1,0:T(8,128)(2,1)} %shard_map.103.refs_0_, bf16[256,2048]{1,0:T(8,128)(2,1)S(1)} %shard_map.96.refs_0_.refs_1_, bf16[256,2048]{1,0:T(8,128)(2,1)} %collective-permute-done.6.refs_2_.refs_1_, ...), custom_call_target="tpu_custom_call" | custom-call | tf_op jit(solution)/shard_map/pallas_call | solution.py:414
  237.0 7.8 %collective-permute-done.14.refs_4_ = bf16[1024,256]{1,0:T(8,128)(2,1)S(1)} collective-permute-done((bf16[1024,256]{1,0:T(8,128)(2,1)S(1)}, bf16[1024,256]{1,0:T(8,128)(2,1)S(1)}, u32[]{:S(2)}, u32[]{:S(2)}) %collective-permute-start.14) | collective-permute-done | bytes 524320 | tf_op jit(solution)/shard_map/ppermute | solution.py:499
  249.2 16.7 %shard_map.105 = bf16[2048,256]{1,0:T(8,128)(2,1)S(1)} custom-call(s32[2,16]{1,0:T(2,128)S(1)} %pad_add_fusion.index_ref, bf16[2048,2048]{1,0:T(8,128)(2,1)} %constant.370.clone.refs_1_.refs_0_, bf16[2048,2048]{1,0:T(8,128)(2,1)} %constant.371.clone.refs_2_.refs_1_, bf16[2,2048,256]{2,1,0:T(8,128)(2,1)S(1)} %copy-done.7, bf16[1024,256]{1,0:T(8,128)(2,1)S(1)} %copy-done.15, ...), custom_call_target="tpu_custom_call" | custom-call | tf_op jit(solution)/shard_map/pallas_call | solution.py:179
  265.9 14.5 %all-gather.3.cloned.1.call-done = bf16[8,512,512]{2,1,0:T(8,128)(2,1)} async-done(((bf16[2,512,512]{2,1,0:T(8,128)(2,1)}), bf16[8,512,512]{2,1,0:T(8,128)(2,1)}) %all-gather.3.cloned.1.call-update) | async-done | bytes 4194320 | tf_op jit(solution)/shard_map/all_gather | solution.py:621
  280.5 8.3 %shard_map.107 = (bf16[2,256,1024]{2,1,0:T(8,128)(2,1)S(1)}, bf16[2,256,1024]{2,1,0:T(8,128)(2,1)S(1)}) custom-call(s32[4]{0:T(128)S(1)} %pad_add_fusion.3.index_ref, bf16[8,256,256]{2,1,0:T(8,128)(2,1)S(1)} %bitcast.112, bf16[4,2,512,512]{3,2,1,0:T(8,128)(2,1)} %bitcast.115, bf16[1024,2048]{1,0:T(8,128)(2,1)} %refs_2_.8, bf16[1024,1024]{1,0:T(8,128)(2,1)S(1)} %copy-done.3, ...), custom_call_target="tpu_custom_call" | custom-call | tf_op jit(solution)/shard_map/pallas_call | solution.py:479
  291.9 9.0 %shard_map.108 = (bf16[2,256,1024]{2,1,0:T(8,128)(2,1)S(1)}, bf16[2,256,1024]{2,1,0:T(8,128)(2,1)}) custom-call(s32[4]{0:T(128)S(1)} %pad_add_fusion.3.index_ref, bf16[2,2,128,1024]{3,2,1,0:T(8,128)(2,1)S(1)} %bitcast.109, bf16[4,2,512,512]{3,2,1,0:T(8,128)(2,1)} %bitcast.116, bf16[1024,2048]{1,0:T(8,128)(2,1)} %refs_2_.8, bf16[1024,1024]{1,0:T(8,128)(2,1)S(1)} %copy-done.3, ...), custom_call_target="tpu_custom_call" | custom-call | tf_op jit(solution)/shard_map/pallas_call | solution.py:479
  302.0 6.6 %all-to-all-start.1 = ((bf16[8,256,256]{2,1,0:T(8,128)(2,1)}), bf16[8,256,256]{2,1,0:T(8,128)(2,1)S(1)}, u32[]{:S(2)}, u32[]{:S(2)}) async-start(bf16[8,256,256]{2,1,0:T(8,128)(2,1)} %bitcast.113), calls=%async_computation.1 | async-start | bytes 2097152 | tf_op jit(solution)/shard_map/all_to_all | solution.py:626
  314.9 9.7 %collective-permute-done.16 = bf16[2,128,1024]{2,1,0:T(8,128)(2,1)} collective-permute-done((bf16[2,128,1024]{2,1,0:T(8,128)(2,1)}, bf16[2,128,1024]{2,1,0:T(8,128)(2,1)}, u32[]{:S(2)}, u32[]{:S(2)}) %collective-permute-start.16) | collective-permute-done | bytes 524320 | tf_op jit(solution)/shard_map/ppermute | solution.py:499
  326.5 4.9 %collective-permute-start.17 = (bf16[2,32,1024]{2,1,0:T(8,128)(2,1)S(1)}, bf16[2,32,1024]{2,1,0:T(8,128)(2,1)S(1)}, u32[]{:S(2)}, u32[]{:S(2)}) collective-permute-start(bf16[2,32,1024]{2,1,0:T(8,128)(2,1)S(1)} %get-tuple-element.36), channel_id=1, source_target_pairs={{0,0},{8,1},{16,2},{24,3},{1,8},{9,9},{17,10},{25,11},{2,16},{10,1... | collective-permute-start | bytes 393224 | tf_op jit(solution)/shard_map/ppermute | solution.py:646
  351.3 4.3 %collective-permute-done.23.refs_4_ = bf16[2,32,1024]{2,1,0:T(8,128)(2,1)} collective-permute-done((bf16[2,32,1024]{2,1,0:T(8,128)(2,1)}, bf16[2,32,1024]{2,1,0:T(8,128)(2,1)}, u32[]{:S(2)}, u32[]{:S(2)}) %collective-permute-start.23) | collective-permute-done | bytes 131104 | tf_op jit(solution)/shard_map/ppermute | solution.py:646
  (126 shorter events, 86.6 us)
Async XLA Ops:
  12.8 47.6 %collective-permute-start = (bf16[1024,1024]{1,0:T(8,128)(2,1)}, bf16[1024,1024]{1,0:T(8,128)(2,1)S(1)}, u32[]{:S(2)}, u32[]{:S(2)}) collective-permute-start(bf16[1024,1024]{1,0:T(8,128)(2,1)} %shard_map.94.refs_0_), channel_id=1, source_target_pairs={{0,4},{4,0},{1,5},{5,1},{2,6},{6,2},{3,7},{7,3},{8,12},{12,8},{9,1... | collective-permute-start | bytes 6291464 | tf_op jit(solution)/shard_map/ppermute | solution.py:499
  14.3 13.7 %collective-permute-start.1 = (bf16[128,2048]{1,0:T(8,128)(2,1)}, bf16[128,2048]{1,0:T(8,128)(2,1)}, u32[]{:S(2)}, u32[]{:S(2)}) collective-permute-start(bf16[128,2048]{1,0:T(8,128)(2,1)} %get-tuple-element.28.refs_0_), channel_id=1, source_target_pairs={{0,2},{2,0},{1,3},{3,1},{4,6},{6,4},{5,7},{7,5},{8,10},{10,8},{9,1... | collective-permute-start | bytes 1572872 | tf_op jit(solution)/shard_map/ppermute | solution.py:499
  29.6 10.5 %collective-permute-start.2 = (bf16[64,2048]{1,0:T(8,128)(2,1)S(1)}, bf16[64,2048]{1,0:T(8,128)(2,1)S(1)}, u32[]{:S(2)}, u32[]{:S(2)}) collective-permute-start(bf16[64,2048]{1,0:T(8,128)(2,1)S(1)} %get-tuple-element.24), channel_id=1, source_target_pairs={{0,0},{1,8},{2,2},{3,10},{8,1},{9,9},{10,3},{11,11},{16,16},{17,24... | collective-permute-start | bytes 786440 | tf_op jit(solution)/shard_map/ppermute | solution.py:568
  30.3 17.5 %collective-permute-start.3 = (bf16[64,2048]{1,0:T(8,128)(2,1)S(1)}, bf16[64,2048]{1,0:T(8,128)(2,1)S(1)}, u32[]{:S(2)}, u32[]{:S(2)}) collective-permute-start(bf16[64,2048]{1,0:T(8,128)(2,1)S(1)} %get-tuple-element.25), channel_id=1, source_target_pairs={{0,1},{1,9},{2,3},{3,11},{8,16},{9,24},{10,18},{11,26},{16,17},{17... | collective-permute-start | bytes 786440 | tf_op jit(solution)/shard_map/ppermute | solution.py:568
  33.3 20.6 %collective-permute-start.4 = (bf16[64,2048]{1,0:T(8,128)(2,1)S(1)}, bf16[64,2048]{1,0:T(8,128)(2,1)S(1)}, u32[]{:S(2)}, u32[]{:S(2)}) collective-permute-start(bf16[64,2048]{1,0:T(8,128)(2,1)S(1)} %get-tuple-element.26), channel_id=1, source_target_pairs={{0,16},{1,24},{2,18},{3,26},{8,17},{9,25},{10,19},{11,27},{16,0},{... | collective-permute-start | bytes 786440 | tf_op jit(solution)/shard_map/ppermute | solution.py:568
  35.8 18.0 %collective-permute-start.5 = (bf16[64,2048]{1,0:T(8,128)(2,1)S(1)}, bf16[64,2048]{1,0:T(8,128)(2,1)S(1)}, u32[]{:S(2)}, u32[]{:S(2)}) collective-permute-start(bf16[64,2048]{1,0:T(8,128)(2,1)S(1)} %get-tuple-element.23), channel_id=1, source_target_pairs={{0,17},{1,25},{2,19},{3,27},{8,0},{9,8},{10,2},{11,10},{16,1},{17,... | collective-permute-start | bytes 786440 | tf_op jit(solution)/shard_map/ppermute | solution.py:568
  63.2 83.1 %all-to-all-start = ((bf16[8,2,256,256]{3,2,1,0:T(8,128)(2,1)}), bf16[8,2,256,256]{3,2,1,0:T(8,128)(2,1)}, u32[]{:S(2)}, u32[]{:S(2)}) async-start(bf16[8,2,256,256]{3,2,1,0:T(8,128)(2,1)} %copy-done.4), calls=%async_computation | async-start | bytes 4194304 | tf_op jit(solution)/shard_map/all_to_all | solution.py:581
  69.1 211.4 %all-gather.3.cloned.1.call-start = ((), (), s32[]{:S(2)}) async-start(), calls=%async_computation.2 | async-start | bytes 5242880 | tf_op jit(solution)/shard_map/all_gather | solution.py:621
  69.1 23.9 %collective-permute-start.6 = (bf16[256,2048]{1,0:T(8,128)(2,1)S(1)}, bf16[256,2048]{1,0:T(8,128)(2,1)}, u32[]{:S(2)}, u32[]{:S(2)}) collective-permute-start(bf16[256,2048]{1,0:T(8,128)(2,1)S(1)} %shard_map.96.refs_0_.refs_1_), channel_id=1, source_target_pairs={{0,2},{2,0},{1,3},{3,1},{4,6},{6,4},{5,7},{7,5},{8,10},{10,8},{9,1... | collective-permute-start | bytes 3145736 | tf_op jit(solution)/shard_map/ppermute | solution.py:499
  69.7 26.8 %collective-permute-start.7 = (bf16[256,2048]{1,0:T(8,128)(2,1)S(1)}, bf16[256,2048]{1,0:T(8,128)(2,1)}, u32[]{:S(2)}, u32[]{:S(2)}) collective-permute-start(bf16[256,2048]{1,0:T(8,128)(2,1)S(1)} %shard_map.96.refs_0_.refs_1_), channel_id=1, source_target_pairs={{0,1},{1,0},{2,3},{3,2},{4,5},{5,4},{6,7},{7,6},{8,9},{9,8},{10,11... | collective-permute-start | bytes 3145736 | tf_op jit(solution)/shard_map/ppermute | solution.py:499
  102.9 27.8 %collective-permute-start.9 = (bf16[1024,512]{1,0:T(8,128)(2,1)}, bf16[1024,512]{1,0:T(8,128)(2,1)}, u32[]{:S(2)}, u32[]{:S(2)}) collective-permute-start(bf16[1024,512]{1,0:T(8,128)(2,1)} %shard_map.98), channel_id=1, source_target_pairs={{0,8},{8,16},{16,24},{24,0},{1,9},{9,17},{17,25},{25,1},{2,10},{10... | collective-permute-start | bytes 3145736 | tf_op jit(solution)/shard_map/ppermute | solution.py:499
  104.5 67.1 %collective-permute-start.10 = (bf16[1024,1024]{1,0:T(8,128)(2,1)}, bf16[1024,1024]{1,0:T(8,128)(2,1)S(1)}, u32[]{:S(2)}, u32[]{:S(2)}) collective-permute-start(bf16[1024,1024]{1,0:T(8,128)(2,1)} %shard_map.97.refs_0_), channel_id=1, source_target_pairs={{0,4},{4,0},{1,5},{5,1},{2,6},{6,2},{3,7},{7,3},{8,12},{12,8},{9,1... | collective-permute-start | bytes 6291464 | tf_op jit(solution)/shard_map/ppermute | solution.py:499
  137.4 34.2 %collective-permute-start.11 = (bf16[1024,512]{1,0:T(8,128)(2,1)}, bf16[1024,512]{1,0:T(8,128)(2,1)}, u32[]{:S(2)}, u32[]{:S(2)}) collective-permute-start(bf16[1024,512]{1,0:T(8,128)(2,1)} %shard_map.99.refs_0_), channel_id=1, source_target_pairs={{0,8},{8,16},{16,24},{24,0},{1,9},{9,17},{17,25},{25,1},{2,10},{10... | collective-permute-start | bytes 3145736 | tf_op jit(solution)/shard_map/ppermute | solution.py:499
  170.1 13.9 %collective-permute-start.12 = (bf16[4,256,256]{2,1,0:T(8,128)(2,1)}, bf16[4,256,256]{2,1,0:T(8,128)(2,1)}, u32[]{:S(2)}, u32[]{:S(2)}) collective-permute-start(bf16[4,256,256]{2,1,0:T(8,128)(2,1)} %get-tuple-element.21), channel_id=1, source_target_pairs={{0,4},{4,0},{1,5},{5,1},{2,6},{6,2},{3,7},{7,3},{8,12},{12,8},{9,1... | collective-permute-start | bytes 1572872 | tf_op jit(solution)/shard_map/ppermute | solution.py:499
  186.1 41.6 %collective-permute-start.13 = (bf16[1024,512]{1,0:T(8,128)(2,1)}, bf16[1024,512]{1,0:T(8,128)(2,1)S(1)}, u32[]{:S(2)}, u32[]{:S(2)}) collective-permute-start(bf16[1024,512]{1,0:T(8,128)(2,1)} %copy-done.12), channel_id=1, source_target_pairs={{0,8},{8,16},{16,24},{24,0},{1,9},{9,17},{17,25},{25,1},{2,10},{10... | collective-permute-start | bytes 3145736 | tf_op jit(solution)/shard_map/ppermute | solution.py:499
  302.0 46.1 %all-to-all-start.1 = ((bf16[8,256,256]{2,1,0:T(8,128)(2,1)}), bf16[8,256,256]{2,1,0:T(8,128)(2,1)S(1)}, u32[]{:S(2)}, u32[]{:S(2)}) async-start(bf16[8,256,256]{2,1,0:T(8,128)(2,1)} %bitcast.113), calls=%async_computation.1 | async-start | bytes 2097152 | tf_op jit(solution)/shard_map/all_to_all | solution.py:626
  309.5 15.1 %collective-permute-start.16 = (bf16[2,128,1024]{2,1,0:T(8,128)(2,1)}, bf16[2,128,1024]{2,1,0:T(8,128)(2,1)}, u32[]{:S(2)}, u32[]{:S(2)}) collective-permute-start(bf16[2,128,1024]{2,1,0:T(8,128)(2,1)} %slice_bitcast_fusion.2), channel_id=1, source_target_pairs={{0,2},{2,0},{1,3},{3,1},{4,6},{6,4},{5,7},{7,5},{8,10},{10,8},{9,1... | collective-permute-start | bytes 1572872 | tf_op jit(solution)/shard_map/ppermute | solution.py:499
  313.5 22.7 %collective-permute-start.22 = (bf16[2,128,1024]{2,1,0:T(8,128)(2,1)}, bf16[2,128,1024]{2,1,0:T(8,128)(2,1)}, u32[]{:S(2)}, u32[]{:S(2)}) collective-permute-start(bf16[2,128,1024]{2,1,0:T(8,128)(2,1)} %slice_bitcast_fusion), channel_id=1, source_target_pairs={{0,2},{2,0},{1,3},{3,1},{4,6},{6,4},{5,7},{7,5},{8,10},{10,8},{9,1... | collective-permute-start | bytes 1572872 | tf_op jit(solution)/shard_map/ppermute | solution.py:499
  326.5 17.8 %collective-permute-start.17 = (bf16[2,32,1024]{2,1,0:T(8,128)(2,1)S(1)}, bf16[2,32,1024]{2,1,0:T(8,128)(2,1)S(1)}, u32[]{:S(2)}, u32[]{:S(2)}) collective-permute-start(bf16[2,32,1024]{2,1,0:T(8,128)(2,1)S(1)} %get-tuple-element.36), channel_id=1, source_target_pairs={{0,0},{8,1},{16,2},{24,3},{1,8},{9,9},{17,10},{25,11},{2,16},{10,1... | collective-permute-start | bytes 393224 | tf_op jit(solution)/shard_map/ppermute | solution.py:646
  331.5 16.5 %collective-permute-start.18 = (bf16[2,32,1024]{2,1,0:T(8,128)(2,1)S(1)}, bf16[2,32,1024]{2,1,0:T(8,128)(2,1)S(1)}, u32[]{:S(2)}, u32[]{:S(2)}) collective-permute-start(bf16[2,32,1024]{2,1,0:T(8,128)(2,1)S(1)} %get-tuple-element.35), channel_id=1, source_target_pairs={{1,0},{9,1},{17,2},{25,3},{2,8},{10,9},{18,10},{26,11},{3,16},{11,... | collective-permute-start | bytes 393224 | tf_op jit(solution)/shard_map/ppermute | solution.py:646
  331.5 16.5 %collective-permute-start.19 = (bf16[2,32,1024]{2,1,0:T(8,128)(2,1)S(1)}, bf16[2,32,1024]{2,1,0:T(8,128)(2,1)S(1)}, u32[]{:S(2)}, u32[]{:S(2)}) collective-permute-start(bf16[2,32,1024]{2,1,0:T(8,128)(2,1)S(1)} %get-tuple-element.34), channel_id=1, source_target_pairs={{2,0},{10,1},{18,2},{26,3},{3,8},{11,9},{19,10},{27,11},{0,16},{8,... | collective-permute-start | bytes 393224 | tf_op jit(solution)/shard_map/ppermute | solution.py:646
  333.0 18.3 %collective-permute-start.20 = (bf16[2,32,1024]{2,1,0:T(8,128)(2,1)}, bf16[2,32,1024]{2,1,0:T(8,128)(2,1)}, u32[]{:S(2)}, u32[]{:S(2)}) collective-permute-start(bf16[2,32,1024]{2,1,0:T(8,128)(2,1)} %get-tuple-element.33), channel_id=1, source_target_pairs={{3,0},{11,1},{19,2},{27,3},{0,8},{8,9},{16,10},{24,11},{1,16},{9,1... | collective-permute-start | bytes 393224 | tf_op jit(solution)/shard_map/ppermute | solution.py:646
  338.3 17.4 %collective-permute-start.23 = (bf16[2,32,1024]{2,1,0:T(8,128)(2,1)}, bf16[2,32,1024]{2,1,0:T(8,128)(2,1)}, u32[]{:S(2)}, u32[]{:S(2)}) collective-permute-start(bf16[2,32,1024]{2,1,0:T(8,128)(2,1)} %get-tuple-element.32), channel_id=1, source_target_pairs={{0,0},{8,1},{16,2},{24,3},{1,8},{9,9},{17,10},{25,11},{2,16},{10,1... | collective-permute-start | bytes 393224 | tf_op jit(solution)/shard_map/ppermute | solution.py:646
  344.3 12.2 %collective-permute-start.24 = (bf16[2,32,1024]{2,1,0:T(8,128)(2,1)}, bf16[2,32,1024]{2,1,0:T(8,128)(2,1)}, u32[]{:S(2)}, u32[]{:S(2)}) collective-permute-start(bf16[2,32,1024]{2,1,0:T(8,128)(2,1)} %get-tuple-element.31), channel_id=1, source_target_pairs={{1,0},{9,1},{17,2},{25,3},{2,8},{10,9},{18,10},{26,11},{3,16},{11,... | collective-permute-start | bytes 393224 | tf_op jit(solution)/shard_map/ppermute | solution.py:646
  (29 other events, 274.2 us)
Sparse Core Ops, SparseCore 0:
  186.3 94.1 all-gather.2
